TPU v7x, 512 devices: a whole 4x4x16 slice. The times are simulated.
512 devices in a mesh: brow: 16 (over z), bcol: 32 (over y, x, core).
Axes of the slice: x: 4, y: 4, z: 16, core: 2. Of those that a mesh axis runs over, the one named last changes fastest.
Arguments:
- ancestor_cov: bfloat16 [5632, 5632], P('brow', 'bcol'), may hold values from -1 to 4
- ancestor_pattern: int32 [22], replicated, may hold values 0 or 1
- parent_panel: bfloat16 [5632, 4096], P('brow'), may hold values from -0.5 to 0.5
- parent_inverse: bfloat16 [4096, 4096], P('brow', 'bcol'), may hold values from -1 to 4
- child_pattern: int32 [16], replicated, may hold values 0 or 1
- child_panel: bfloat16 [4096, 4096], P('brow', 'bcol'), may hold values from -0.3125 to 0.3125
- child_inverse: bfloat16 [4096, 4096], P('brow', 'bcol'), may hold values from -1 to 4
Outputs:
- ancestor_block: bfloat16 [5632, 4096], P('brow', 'bcol')
- parent_diag: bfloat16 [4096, 4096], P('brow', 'bcol')
- parent_child: bfloat16 [4096, 4096], P('brow', 'bcol')
- child_diag: bfloat16 [4096, 4096], P('brow', 'bcol')
All inputs are finite; a program needn't handle non-finite values.
Results may differ from a plain program's by a relative error of at most 0.006.
Values may be sent and summed in bfloat16 or wider, within the bound.
No kernel may reach another device: no remote copies, remote signals or barrier semaphores. Data moves between devices by JAX's collectives and lax.ppermute only.
A program may use at most 64 MiB of HBM per device.

v0:
```python
import jax
import jax.numpy as jnp
from jax import lax
from jax.sharding import PartitionSpec as P


def block_keep(pattern, first_row, count, total_rows):
    block_rows = total_rows // pattern.shape[0]
    row_ids = first_row + lax.iota(jnp.int32, count)
    block_ids = lax.iota(jnp.int32, pattern.shape[0])
    matches = row_ids[:, None] // block_rows == block_ids[None, :]
    return jnp.sum(jnp.where(matches, pattern[None, :], 0), axis=1)


def per_device(
    ancestor_cov,
    ancestor_pattern,
    parent_panel,
    parent_inverse,
    child_pattern,
    child_panel,
    child_inverse,
):
    row_index = lax.axis_index("brow")
    column_index = lax.axis_index("bcol")
    row_devices = lax.axis_size("brow")
    local_rows = parent_panel.shape[0]
    band_rows = parent_inverse.shape[0]
    band_columns = parent_inverse.shape[1]
    ancestor_keep = block_keep(
        ancestor_pattern, row_index * local_rows, local_rows, local_rows * row_devices
    )
    child_keep = block_keep(
        child_pattern, row_index * band_rows, band_rows, band_rows * row_devices
    )
    parent_masked = parent_panel * ancestor_keep[:, None].astype(jnp.bfloat16)
    child_masked = child_panel * child_keep[:, None].astype(jnp.bfloat16)
    panel_slab = lax.dynamic_slice_in_dim(
        parent_masked, column_index * band_columns, band_columns, 1
    )
    parent_columns, child_columns = (
        lax.all_gather(panel_slab, "brow", axis=0, tiled=True),
        lax.all_gather(child_masked, "brow", axis=0, tiled=True),
    )
    factor_rows = parent_columns
    ancestor_sum = jnp.dot(
        lax.all_gather(ancestor_cov, "bcol", axis=1, tiled=True),
        factor_rows,
        preferred_element_type=jnp.float32,
    )
    ancestor_block = (-ancestor_sum * ancestor_keep[:, None].astype(jnp.float32)).astype(
        jnp.bfloat16
    )
    parent_wide = lax.all_to_all(parent_masked, "brow", split_axis=1, concat_axis=0, tiled=True)
    image_band = lax.all_gather(ancestor_block, "brow", axis=0, tiled=True)
    parent_inner = jnp.einsum(
        "ka,kb->ab", parent_wide, image_band, preferred_element_type=jnp.float32
    )
    parent_diag = (parent_inverse.astype(jnp.float32) - parent_inner).astype(jnp.bfloat16)
    factor_rows = child_columns
    parent_sum = jnp.dot(
        lax.all_gather(parent_diag, "bcol", axis=1, tiled=True),
        factor_rows,
        preferred_element_type=jnp.float32,
    )
    parent_child = (-parent_sum * child_keep[:, None].astype(jnp.float32)).astype(jnp.bfloat16)
    child_band = lax.all_gather(child_masked, "bcol", axis=1, tiled=True)
    child_inner = lax.psum_scatter(
        jnp.einsum("ka,kb->ab", child_band, parent_child, preferred_element_type=jnp.float32),
        "brow",
        scatter_dimension=0,
        tiled=True,
    )
    child_diag = (child_inverse.astype(jnp.float32) - child_inner).astype(jnp.bfloat16)
    return (ancestor_block, parent_diag, parent_child, child_diag)


def solution(mesh):
    return jax.shard_map(
        per_device,
        mesh=mesh,
        in_specs=(
            P("brow", "bcol"),
            P(),
            P("brow", None),
            P("brow", "bcol"),
            P(),
            P("brow", "bcol"),
            P("brow", "bcol"),
        ),
        out_specs=(P("brow", "bcol"), P("brow", "bcol"), P("brow", "bcol"), P("brow", "bcol")),
        check_vma=False,
    )
```

profile of v0, /device:TPU:8, one launch (start us, length us, event | category | flops | bytes accessed | tf_op | source)
XLA Modules:
  0.0 577.8 jit_solution(14311863399539205714)
XLA Ops:
  7.2 0.0 all-gather.7.cloned.1.call-start
  7.2 0.7 select_reduce_fusion
  8.0 2.1 broadcast_multiply_fusion
  10.1 0.7 constant_dynamic-slice_fusion
  10.8 0.0 all-gather.9.cloned.1.call-start
  10.8 0.7 all-gather.9.cloned.1.call-update
  11.5 1.9 copy.16
  13.4 15.2 %all-to-all-start = ((bf16[352,16,256]{2,0,1:T(8,128)(2,1)}), bf16[352,16,256]{2,0,1:T(8,128)(2,1)S(1)}, u32[]{:S(2)}, u32[]{:S(2)}) async-start(bf16[352,16,256]{2,0,1:T(8,128)(2,1)} %bitcast.19), calls=%async_computation | async-start | bytes 5767168 | tf_op jit(solution)/shard_map/all_to_all | solution.py:54
  28.6 0.0 all-gather.11.cloned.1.call-start
  28.7 119.7 %all-gather.7.cloned.1.call-done = bf16[5632,128]{1,0:T(8,128)(2,1)} async-done(((bf16[352,128]{1,0:T(8,128)(2,1)}), bf16[5632,128]{1,0:T(8,128)(2,1)}) %all-gather.7.cloned.1.call-update) | async-done | bytes 1441808 | tf_op jit(solution)/shard_map/all_gather | solution.py:42
  148.3 73.0 %all-gather.9.cloned.1.call-done = bf16[352,5632]{0,1:T(8,128)(2,1)} async-done(((bf16[352,176]{0,1:T(8,128)(2,1)}), bf16[352,5632]{0,1:T(8,128)(2,1)}) %all-gather.9.cloned.1.call-update) | async-done | bytes 3964944 | tf_op jit(solution)/shard_map/all_gather | solution.py:47
  221.3 5.1 fusion.5
  226.4 0.0 all-gather.11.cloned.1.call-update
  226.4 0.0 all-gather.15.cloned.1.call-start
  226.5 0.1 select_reduce_fusion.1
  226.6 0.7 broadcast_multiply_fusion.1
  227.3 0.0 all-gather.15.cloned.1.call-update
  227.4 0.0 all-gather.13.cloned.1.call-start
  227.4 71.0 %all-gather.11.cloned.1.call-done = bf16[5632,128]{1,0:T(8,128)(2,1)} async-done(((bf16[352,128]{1,0:T(8,128)(2,1)}), bf16[5632,128]{1,0:T(8,128)(2,1)}) %all-gather.11.cloned.1.call-update) | async-done | bytes 1441808 | tf_op jit(solution)/shard_map/all_gather | solution.py:55
  298.4 2.9 fusion.3
  301.4 0.0 all-gather.13.cloned.1.call-update
  301.4 0.0 all-gather.17.cloned.1.call-start
  301.4 0.5 all-gather.17.cloned.1.call-update
  302.0 0.0 reduce-scatter.2.cloned.1.call-start
  302.0 66.9 %all-gather.15.cloned.1.call-done = bf16[4096,128]{1,0:T(8,128)(2,1)} async-done(((bf16[256,128]{1,0:T(8,128)(2,1)}), bf16[4096,128]{1,0:T(8,128)(2,1)}) %all-gather.15.cloned.1.call-update) | async-done | bytes 1048592 | tf_op jit(solution)/shard_map/all_gather | solution.py:43
  368.9 60.1 %all-gather.13.cloned.1.call-done = bf16[256,4096]{1,0:T(8,128)(2,1)} async-done(((bf16[256,128]{1,0:T(8,128)(2,1)}), bf16[256,4096]{1,0:T(8,128)(2,1)}) %all-gather.13.cloned.1.call-update) | async-done | bytes 2097168 | tf_op jit(solution)/shard_map/all_gather | solution.py:62
  429.0 2.6 fusion.4
  431.6 60.5 %all-gather.17.cloned.1.call-done = bf16[256,4096]{1,0:T(8,128)(2,1)} async-done(((bf16[256,128]{1,0:T(8,128)(2,1)}), bf16[256,4096]{1,0:T(8,128)(2,1)}) %all-gather.17.cloned.1.call-update) | async-done | bytes 2097168 | tf_op jit(solution)/shard_map/all_gather | solution.py:67
  492.2 3.7 fusion.11
  495.8 0.0 reduce-scatter.2.cloned.1.call-update
  495.8 73.5 %reduce-scatter.2.cloned.1.call-done = f32[256,128]{1,0:T(8,128)} async-done(((f32[4096,128]{1,0:T(8,128)}), f32[256,128]{1,0:T(8,128)}) %reduce-scatter.2.cloned.1.call-update) | async-done | bytes 131088 | tf_op jit(solution)/shard_map/reduce_scatter | solution.py:68
  569.4 1.5 subtract_convert_fusion
  (16 shorter events, 0.1 us)
Async XLA Ops:
  7.2 141.2 %all-gather.7.cloned.1.call-start = ((), (), s32[]{:S(2)}) async-start(), calls=%async_computation.2 | async-start | bytes 1531904 | tf_op jit(solution)/shard_map/all_gather | solution.py:42
  10.8 210.5 %all-gather.9.cloned.1.call-start = ((), (), s32[]{:S(2)}) async-start(), calls=%async_computation.3 | async-start | bytes 4460544 | tf_op jit(solution)/shard_map/all_gather | solution.py:47
  13.4 285.0 %all-to-all-start = ((bf16[352,16,256]{2,0,1:T(8,128)(2,1)}), bf16[352,16,256]{2,0,1:T(8,128)(2,1)S(1)}, u32[]{:S(2)}, u32[]{:S(2)}) async-start(bf16[352,16,256]{2,0,1:T(8,128)(2,1)} %bitcast.19), calls=%async_computation | async-start | bytes 5767168 | tf_op jit(solution)/shard_map/all_to_all | solution.py:54
  28.6 269.8 %all-gather.11.cloned.1.call-start = ((), (), s32[]{:S(2)}) async-start(), calls=%async_computation.4 | async-start | bytes 1531904 | tf_op jit(solution)/shard_map/all_gather | solution.py:55
  221.3 5.2 copy-start.4
  221.3 5.3 copy-start.2
  221.3 77.1 %copy-start.1 = (bf16[256,128]{1,0:T(8,128)(2,1)S(1)}, bf16[256,128]{1,0:T(8,128)(2,1)}, u32[]{:S(2)}) copy-start(bf16[256,128]{1,0:T(8,128)(2,1)} %param.10) | copy-start | bytes 196612
  226.4 142.5 %all-gather.15.cloned.1.call-start = ((), (), s32[]{:S(2)}) async-start(), calls=%async_computation.6 | async-start | bytes 1114112 | tf_op jit(solution)/shard_map/all_gather | solution.py:43
  227.4 201.7 %all-gather.13.cloned.1.call-start = ((), (), s32[]{:S(2)}) async-start(), calls=%async_computation.5 | async-start | bytes 2162688 | tf_op jit(solution)/shard_map/all_gather | solution.py:62
  301.4 190.8 %all-gather.17.cloned.1.call-start = ((), (), s32[]{:S(2)}) async-start(), calls=%async_computation.7 | async-start | bytes 2162688 | tf_op jit(solution)/shard_map/all_gather | solution.py:67
  302.0 267.4 %reduce-scatter.2.cloned.1.call-start = ((), (), s32[]{:S(2)}) async-start(), calls=%async_computation.8 | async-start | bytes 2228224 | tf_op jit(solution)/shard_map/reduce_scatter | solution.py:68
  431.6 64.2 %copy-start = (bf16[256,128]{1,0:T(8,128)(2,1)}, bf16[256,128]{1,0:T(8,128)(2,1)S(1)}, u32[]{:S(2)}) copy-start(bf16[256,128]{1,0:T(8,128)(2,1)S(1)} %fusion.4) | copy-start | bytes 196612
  495.8 73.6 %copy-start.3 = (bf16[256,128]{1,0:T(8,128)(2,1)S(1)}, bf16[256,128]{1,0:T(8,128)(2,1)}, u32[]{:S(2)}) copy-start(bf16[256,128]{1,0:T(8,128)(2,1)} %param.13) | copy-start | bytes 196612
Sparse Core Ops, SparseCore 0:
  10.9 137.3 all-gather.6
  151.5 69.7 all-gather.8
  226.5 71.8 all-gather.10
  300.9 67.9 all-gather.14
  372.4 56.5 all-gather.12
  432.5 59.5 all-gather.16
  496.0 73.3 reduce-scatter.1
where the time goes:
time: 578 us
  waiting for transfers between devices  526 us (91%)
  starting transfers between devices  15.5 us (3%)
  matrix products  14.2 us (2%)
  between operations  14.2 us (2%)
    all_gather x1, waiting for transfers between devices, per_device(): lax.all_gather(panel_slab, 'brow', axis=0, tiled=True)  120 us
    reduce_scatter x1, waiting for transfers between devices, per_device(): lax.psum_scatter(jnp.einsum('ka,kb->ab', child_band, parent_child, prefer...  73.5 us
    all_gather x1, waiting for transfers between devices, per_device(): lax.all_gather(ancestor_cov, 'bcol', axis=1, tiled=True)  73 us
    all_gather x1, waiting for transfers between devices, per_device(): image_band = lax.all_gather(ancestor_block, 'brow', axis=0, tiled=True)  71 us
    all_gather x1, waiting for transfers between devices, per_device(): lax.all_gather(child_masked, 'brow', axis=0, tiled=True)  66.9 us
    all_gather x1, waiting for transfers between devices, per_device(): child_band = lax.all_gather(child_masked, 'bcol', axis=1, tiled=True)  60.5 us
    all_gather x1, waiting for transfers between devices, per_device(): lax.all_gather(parent_diag, 'bcol', axis=1, tiled=True)  60.1 us
    all_to_all x1, starting transfers between devices, per_device(): lax.all_to_all(parent_masked, 'brow', split_axis=1, concat_axis=0, tiled=...  15.2 us
  transfers between devices with their start and end apart: 8, of which 7 were waited for; matrix products, arithmetic and copies ran while one was open for 2% of the time, Pallas kernels for 0%

commit v1 on v0

v1 whole, which is shorter than its diff:
```python
import jax
import jax.numpy as jnp
from jax import lax
from jax.experimental import pallas as pl
from jax.experimental.pallas import tpu as pltpu
from jax.sharding import Mesh, PartitionSpec as P

BF = jnp.bfloat16
F32 = jnp.float32
VMEM = pl.BlockSpec(memory_space=pltpu.VMEM)
SMEM = pl.BlockSpec(memory_space=pltpu.SMEM)
Z = ("zh", "zl")
PLANE = ("y", "x", "c")


def block_keep(pattern, first_row, count, total_rows):
    block_rows = total_rows // pattern.shape[0]
    row_ids = first_row + lax.iota(jnp.int32, count)
    block_ids = lax.iota(jnp.int32, pattern.shape[0])
    matches = row_ids[:, None] // block_rows == block_ids[None, :]
    return jnp.sum(jnp.where(matches, pattern[None, :], 0), axis=1)


def call(kernel, outs, args, flops):
    specs = [SMEM if a.dtype == jnp.int32 else VMEM for a in args]
    size = sum(a.size * a.dtype.itemsize for a in args)
    size += sum(o.size * o.dtype.itemsize for o in outs)
    return pl.pallas_call(
        kernel,
        out_shape=outs,
        in_specs=specs,
        out_specs=[VMEM] * len(outs),
        compiler_params=pltpu.CompilerParams(vmem_limit_bytes=40 * 1024 * 1024),
        cost_estimate=pl.CostEstimate(flops=flops, bytes_accessed=size, transcendentals=0),
    )(*args)


def image_kernel(classes, at_ref, panel_ref, own_ref, right_ref, left_ref, far_ref):
    at = at_ref[...]
    for n, out in enumerate((right_ref, left_ref, far_ref, own_ref)):
        for rh in range(4):
            start = pl.multiple_of((4 * rh + classes[n]) * 256, 256)
            block = jnp.dot(at, panel_ref[:, pl.ds(start, 256)], preferred_element_type=F32)
            out[rh] = block.astype(out.dtype)


def panel_kernel(left_ref, blocks_ref, out_ref):
    rows = left_ref.shape[0] // 4
    total = None
    for h in range(4):
        right = jnp.concatenate([blocks_ref[4 * h + n, :rows, :] for n in range(4)], axis=1)
        part = lax.dot_general(
            left_ref[h * rows : (h + 1) * rows, :],
            right,
            (((0,), (0,)), ((), ())),
            preferred_element_type=F32,
        )
        total = part if total is None else total + part
    for n in range(4):
        out_ref[n] = total[:, n * 128 : (n + 1) * 128].astype(out_ref.dtype)


def child_kernel(left_ref, blocks_ref, out_ref):
    total = None
    for h in range(4):
        right = jnp.concatenate([blocks_ref[4 * h + n, 352:608, :] for n in range(4)], axis=1)
        left = jnp.concatenate([left_ref[2 * h], left_ref[2 * h + 1]], axis=1)
        part = jnp.dot(left, right, preferred_element_type=F32)
        total = part if total is None else total + part
    for n in range(4):
        out_ref[n] = total[:, n * 128 : (n + 1) * 128].astype(out_ref.dtype)


def last_kernel(factor_ref, image_ref, out_ref):
    for y in range(4):
        total = None
        for x in range(4):
            n = (y * 4 + x) * 2
            left = jnp.concatenate([factor_ref[n], factor_ref[n + 1]], axis=1)
            part = lax.dot_general(
                left, image_ref[x], (((0,), (0,)), ((), ())), preferred_element_type=F32
            )
            total = part if total is None else total + part
        out_ref[y] = total.astype(out_ref.dtype)


def shift(value, by):
    return lax.ppermute(value, Z, [(i, (i + by) % 16) for i in range(16)])


def exchange(value, axis):
    return lax.all_to_all(value, axis, split_axis=0, concat_axis=0, tiled=True)


def after(value, *others):
    return lax.optimization_barrier((value, *others))[0]


def per_device(
    ancestor_cov,
    ancestor_pattern,
    parent_panel,
    parent_inverse,
    child_pattern,
    child_panel,
    child_inverse,
):
    z = lax.axis_index(Z)
    zl = lax.axis_index("zl")
    column = lax.axis_index(PLANE)
    ancestor_keep = block_keep(ancestor_pattern, z * 352, 352, 5632)
    child_keep = block_keep(child_pattern, z * 256, 256, 4096)
    slab = lax.dynamic_slice_in_dim(parent_panel, column * 128, 128, 1)
    slab = slab * ancestor_keep[:, None].astype(BF)
    child_masked = child_panel * child_keep[:, None].astype(BF)
    cov = (ancestor_cov * ancestor_keep[:, None].astype(BF)).T

    swapped = lax.ppermute(
        jnp.concatenate([slab, child_masked], axis=0),
        ("zl", "x"),
        [(a * 4 + b, b * 4 + a) for a in range(4) for b in range(4)],
    )
    blocks = lax.all_gather(swapped, Z, axis=0)

    classes = jnp.stack([(zl + 1) % 4, (zl + 3) % 4, (zl + 2) % 4, zl]).astype(jnp.int32)
    bundle = jax.ShapeDtypeStruct((4, 176, 256), BF)
    own, right, left, far = call(
        image_kernel,
        [jax.ShapeDtypeStruct((4, 176, 256), F32), bundle, bundle, bundle],
        [classes, cov, parent_panel],
        2 * 176 * 352 * 4096,
    )
    right, left = shift(right, 1), shift(left, -1)
    far = jnp.concatenate([shift(far[:2], 2), shift(far[2:], -2)], axis=0)
    image = own + right.astype(F32) + left.astype(F32) + far.astype(F32)
    image = exchange(image.astype(BF), "zh")
    image = jnp.sum(image.astype(F32), axis=0).astype(BF)

    cov_wide = lax.all_gather(cov, ("y", "c"), axis=0, tiled=True)
    image_wide = lax.all_gather(image, ("y", "c"), axis=0, tiled=True)
    factor = lax.all_gather(after(swapped[352:], image), PLANE, axis=0)

    (inner,) = call(
        panel_kernel,
        [jax.ShapeDtypeStruct((4, 256, 128), F32)],
        [image_wide, blocks],
        2 * 1408 * 256 * 512,
    )
    inner = jnp.sum(exchange(inner, "x"), axis=0)
    parent_diag = (parent_inverse.astype(F32) + inner).astype(BF)

    diag_wide = lax.all_gather(parent_diag, ("y", "c"), axis=0)
    (product,) = call(
        child_kernel,
        [jax.ShapeDtypeStruct((4, 256, 128), F32)],
        [diag_wide, blocks],
        2 * 1024 * 256 * 512,
    )
    product = jnp.sum(exchange(product, "x"), axis=0)
    parent_child = (-product * child_keep[:, None].astype(F32)).astype(BF)

    child_wide = lax.all_gather(parent_child, "zl", axis=0)

    (product,) = call(
        panel_kernel,
        [jax.ShapeDtypeStruct((4, 352, 128), F32)],
        [cov_wide, blocks],
        2 * 1408 * 352 * 512,
    )
    product = jnp.sum(exchange(after(product, child_wide), "x"), axis=0)
    ancestor_block = (-product * ancestor_keep[:, None].astype(F32)).astype(BF)

    (inner,) = call(
        last_kernel,
        [jax.ShapeDtypeStruct((4, 256, 128), BF)],
        [factor, child_wide],
        2 * 1024 * 1024 * 128,
    )
    inner = jnp.sum(exchange(inner, "zh").astype(F32), axis=0)
    child_diag = (child_inverse.astype(F32) - inner).astype(BF)
    return (ancestor_block, parent_diag, parent_child, child_diag)


def solution(mesh):
    fine = Mesh(mesh.devices.reshape(4, 4, 4, 4, 2), ("zh", "zl", "y", "x", "c"))
    blocked = P(Z, PLANE)
    return jax.shard_map(
        per_device,
        mesh=fine,
        in_specs=(blocked, P(), P(Z, None), blocked, P(), blocked, blocked),
        out_specs=(blocked, blocked, blocked, blocked),
        check_vma=False,
    )
```

time: 578 us -> 228 us (0.39)
  the two profiles are of different devices: /device:TPU:8 before, /device:TPU:32 now
where the time goes in v1:
time: 228 us; the launch traced here: 227 us
  waiting for transfers between devices  74.7 us (33%)
  blocking collectives  68.6 us (30%)
  starting transfers between devices  47.6 us (21%)
  between operations  14.3 us (6%)
  other arithmetic  7.81 us (3%)
  local copies, waits for them, and re-layouts  7.27 us (3%)
  Pallas kernels  6.67 us (3%)
    all_to_all x4, waiting for transfers between devices, exchange(): return lax.all_to_all(value, axis, split_axis=0, concat_axis=0, tiled=True)  48.6 us
    all_to_all x4, starting transfers between devices, exchange(): return lax.all_to_all(value, axis, split_axis=0, concat_axis=0, tiled=True)  26 us
    ppermute x4, starting transfers between devices, shift(): return lax.ppermute(value, Z, [(i, (i + by) % 16) for i in range(16)])  18.7 us
    all_gather x1, blocking collectives, per_device(): child_wide = lax.all_gather(parent_child, 'zl', axis=0)  14.3 us
    all_gather x1, blocking collectives, per_device(): image_wide = lax.all_gather(image, ('y', 'c'), axis=0, tiled=True)  13.8 us
    all_gather x1, blocking collectives, per_device(): cov_wide = lax.all_gather(cov, ('y', 'c'), axis=0, tiled=True)  13.8 us
    all_to_all x1, blocking collectives, exchange(): return lax.all_to_all(value, axis, split_axis=0, concat_axis=0, tiled=True)  13.4 us
    all_gather x1, blocking collectives, per_device(): diag_wide = lax.all_gather(parent_diag, ('y', 'c'), axis=0)  13.3 us
  transfers between devices with their start and end apart: 11, of which 7 were waited for; matrix products, arithmetic and copies ran while one was open for 2% of the time, Pallas kernels for 3%

profile of v1, /device:TPU:32, one launch (start us, length us, event | category | flops | bytes accessed | tf_op | source)
XLA Modules:
  0.0 227.0 jit_solution(10235138432429000896)
XLA Ops:
  8.8 0.9 broadcast_multiply_fusion
  9.7 1.0 dynamic-slice_multiply_fusion
  10.8 2.9 %collective-permute-start = (bf16[608,128]{1,0:T(8,128)(2,1)S(1)}, bf16[608,128]{1,0:T(8,128)(2,1)S(1)}, u32[]{:S(2)}, u32[]{:S(2)}) collective-permute-start(bf16[608,128]{1,0:T(8,128)(2,1)S(1)} %pad_maximum_fusion), channel_id=1, source_target_pairs={{0,0},{2,32},{4,64},{6,96},{32,2},{34,34},{36,66},{38,98},{64,4},{... | collective-permute-start | bytes 466952 | tf_op jit(solution)/shard_map/ppermute | solution.py:118
  13.7 9.9 %collective-permute-done = bf16[608,128]{1,0:T(8,128)(2,1)S(1)} collective-permute-done((bf16[608,128]{1,0:T(8,128)(2,1)S(1)}, bf16[608,128]{1,0:T(8,128)(2,1)S(1)}, u32[]{:S(2)}, u32[]{:S(2)}) %collective-permute-start) | collective-permute-done | bytes 155680 | tf_op jit(solution)/shard_map/ppermute | solution.py:118
  24.4 0.9 multiply_bitcast_fusion.at_ref
  25.4 1.8 copy-done.2
  27.2 1.5 shard_map.103
  28.6 4.8 %collective-permute-start.1 = (bf16[4,176,256]{2,1,0:T(8,128)(2,1)S(1)}, bf16[4,176,256]{2,1,0:T(8,128)(2,1)S(1)}, u32[]{:S(2)}, u32[]{:S(2)}) collective-permute-start(bf16[4,176,256]{2,1,0:T(8,128)(2,1)S(1)} %get-tuple-element.11), channel_id=1, source_target_pairs={{0,32},{32,64},{64,96},{96,128},{128,160},{160,192},{192,224},{224... | collective-permute-start | bytes 1081352 | tf_op jit(solution)/shard_map/ppermute | solution.py:88
  33.5 1.9 collective-permute-start.2
  35.4 3.4 %collective-permute-start.3 = (bf16[2,176,256]{2,1,0:T(8,128)(2,1)S(1)}, bf16[2,176,256]{2,1,0:T(8,128)(2,1)S(1)}, u32[]{:S(2)}, u32[]{:S(2)}) collective-permute-start(bf16[2,176,256]{2,1,0:T(8,128)(2,1)S(1)} %get-tuple-element.16), channel_id=1, source_target_pairs={{0,64},{32,96},{64,128},{96,160},{128,192},{160,224},{192,256},{22... | collective-permute-start | bytes 540680 | tf_op jit(solution)/shard_map/ppermute | solution.py:88
  38.8 8.6 %collective-permute-start.4 = (bf16[2,176,256]{2,1,0:T(8,128)(2,1)S(1)}, bf16[2,176,256]{2,1,0:T(8,128)(2,1)S(1)}, u32[]{:S(2)}, u32[]{:S(2)}) collective-permute-start(bf16[2,176,256]{2,1,0:T(8,128)(2,1)S(1)} %get-tuple-element.17), channel_id=1, source_target_pairs={{0,448},{32,480},{64,0},{96,32},{128,64},{160,96},{192,128},{224,1... | collective-permute-start | bytes 540680 | tf_op jit(solution)/shard_map/ppermute | solution.py:88
  47.4 6.6 %collective-permute-done.3 = bf16[2,176,256]{2,1,0:T(8,128)(2,1)S(1)} collective-permute-done((bf16[2,176,256]{2,1,0:T(8,128)(2,1)S(1)}, bf16[2,176,256]{2,1,0:T(8,128)(2,1)S(1)}, u32[]{:S(2)}, u32[]{:S(2)}) %collective-permute-start.3) | collective-permute-done | bytes 180256 | tf_op jit(solution)/shard_map/ppermute | solution.py:88
  54.0 2.8 %collective-permute-done.4 = bf16[2,176,256]{2,1,0:T(8,128)(2,1)S(1)} collective-permute-done((bf16[2,176,256]{2,1,0:T(8,128)(2,1)S(1)}, bf16[2,176,256]{2,1,0:T(8,128)(2,1)S(1)}, u32[]{:S(2)}, u32[]{:S(2)}) %collective-permute-start.4) | collective-permute-done | bytes 180256 | tf_op jit(solution)/shard_map/ppermute | solution.py:88
  57.7 10.4 %all-to-all-start = ((bf16[4,176,256]{2,1,0:T(8,128)(2,1)}), bf16[4,176,256]{2,1,0:T(8,128)(2,1)S(1)}, u32[]{:S(2)}, u32[]{:S(2)}) async-start(bf16[4,176,256]{2,1,0:T(8,128)(2,1)} %add_convert_fusion), calls=%async_computation | async-start | bytes 720896 | tf_op jit(solution)/shard_map/all_to_all | solution.py:92
  68.1 1.5 slice.12
  69.6 25.8 %all-to-all-done = bf16[4,176,256]{2,1,0:T(8,128)(2,1)S(1)} async-done(((bf16[4,176,256]{2,1,0:T(8,128)(2,1)}), bf16[4,176,256]{2,1,0:T(8,128)(2,1)S(1)}, u32[]{:S(2)}, u32[]{:S(2)}) %all-to-all-start) | async-done | bytes 360480 | tf_op jit(solution)/shard_map/all_to_all | solution.py:92
  95.5 13.8 %all_gather.31.left_ref = bf16[1408,256]{1,0:T(8,128)(2,1)S(1)} all-gather(bf16[176,256]{1,0:T(8,128)(2,1)S(1)} %reduce_sum.68), channel_id=1, replica_groups=mesh['zh'=4,'zl'=4,'y'=4,'x'=4,'c'=2] {'y','c'}, dimensions={0}, use_global_device_ids=true | all-gather | bytes 811008 | tf_op jit(solution)/shard_map/all_gather | solution.py:140
  109.3 6.8 %all-gather.6.cloned.1.call-done = bf16[9728,128]{1,0:T(8,128)(2,1)} async-done(((bf16[608,128]{1,0:T(8,128)(2,1)}), bf16[9728,128]{1,0:T(8,128)(2,1)}) %all-gather.6.cloned.1.call-update) | async-done | bytes 2490384 | tf_op jit(solution)/shard_map/all_gather | solution.py:123
  116.1 1.7 copy-done
  118.5 13.4 %all_to_all.25 = f32[4,256,128]{2,1,0:T(8,128)S(1)} all-to-all(f32[4,256,128]{2,1,0:T(8,128)S(1)} %shard_map.104), channel_id=1, replica_groups=mesh['zh'=4,'zl'=4,'y'=4,'x'=4,'c'=2] {'x'}, dimensions={0} | all-to-all | bytes 1048576 | tf_op jit(solution)/shard_map/all_to_all | solution.py:92
  132.0 13.3 %all-gather.1 = bf16[2048,128]{1,0:T(8,128)(2,1)S(1)} all-gather(bf16[256,128]{1,0:T(8,128)(2,1)S(1)} %add_convert_fusion.1), channel_id=3, replica_groups=mesh['zh'=4,'zl'=4,'y'=4,'x'=4,'c'=2] {'y','c'}, dimensions={0}, use_global_device_ids=true | all-gather | bytes 589824 | tf_op jit(solution)/shard_map/all_gather | solution.py:152
  145.3 1.2 shard_map.105
  146.5 3.5 %all-to-all-start.2 = ((f32[4,256,128]{2,1,0:T(8,128)}), f32[4,256,128]{2,1,0:T(8,128)S(1)}, u32[]{:S(2)}, u32[]{:S(2)}) async-start(f32[4,256,128]{2,1,0:T(8,128)} %shard_map.105), calls=%async_computation.2 | async-start | bytes 1048576 | tf_op jit(solution)/shard_map/all_to_all | solution.py:92
  150.0 13.8 %all_gather.28.left_ref = bf16[1408,352]{1,0:T(8,128)(2,1)S(1)} all-gather(bf16[176,352]{1,0:T(8,128)(2,1)S(1)} %multiply_bitcast_fusion.at_ref), channel_id=1, replica_groups=mesh['zh'=4,'zl'=4,'y'=4,'x'=4,'c'=2] {'y','c'}, dimensions={0}, use_global_device_ids=true | all-gather | bytes 1115136 | tf_op jit(solution)/shard_map/all_gather | solution.py:139
  163.8 1.8 shard_map.102
  165.7 14.3 %all_gather.34.image_ref = bf16[4,256,128]{2,1,0:T(8,128)(2,1)S(1)} all-gather(bf16[1,256,128]{2,1,0:T(8,128)(2,1)S(1)} %fusion), channel_id=1, replica_groups=mesh['zh'=4,'zl'=4,'y'=4,'x'=4,'c'=2] {'zl'}, dimensions={0}, use_global_device_ids=true | all-gather | bytes 327680 | tf_op jit(solution)/shard_map/all_gather | solution.py:162
  180.0 4.9 %all-to-all-start.3 = ((f32[4,352,128]{2,1,0:T(8,128)}), f32[4,352,128]{2,1,0:T(8,128)S(1)}, u32[]{:S(2)}, u32[]{:S(2)}) async-start(f32[4,352,128]{2,1,0:T(8,128)} %shard_map.102), calls=%async_computation.3 | async-start | bytes 1441792 | tf_op jit(solution)/shard_map/all_to_all | solution.py:92
  185.0 1.6 copy-done.3
  186.5 1.4 shard_map.106
  188.0 6.3 %all-to-all-done.3 = f32[4,352,128]{2,1,0:T(8,128)S(1)} async-done(((f32[4,352,128]{2,1,0:T(8,128)}), f32[4,352,128]{2,1,0:T(8,128)S(1)}, u32[]{:S(2)}, u32[]{:S(2)}) %all-to-all-start.3) | async-done | bytes 720928 | tf_op jit(solution)/shard_map/all_to_all | solution.py:92
  194.3 7.2 %all-to-all-start.4 = ((bf16[4,256,128]{2,1,0:T(8,128)(2,1)}), bf16[4,256,128]{2,1,0:T(8,128)(2,1)S(1)}, u32[]{:S(2)}, u32[]{:S(2)}) async-start(bf16[4,256,128]{2,1,0:T(8,128)(2,1)} %shard_map.106), calls=%async_computation.4 | async-start | bytes 524288 | tf_op jit(solution)/shard_map/all_to_all | solution.py:92
  202.9 16.5 %all-to-all-done.4 = bf16[4,256,128]{2,1,0:T(8,128)(2,1)S(1)} async-done(((bf16[4,256,128]{2,1,0:T(8,128)(2,1)}), bf16[4,256,128]{2,1,0:T(8,128)(2,1)S(1)}, u32[]{:S(2)}, u32[]{:S(2)}) %all-to-all-start.4) | async-done | bytes 262176 | tf_op jit(solution)/shard_map/all_to_all | solution.py:92
  (42 shorter events, 6.4 us)
Async XLA Ops:
  7.2 108.9 %all-gather.6.cloned.1.call-start = ((), (), s32[]{:S(2)}) async-start(), calls=%async_computation.5 | async-start | bytes 2646016 | tf_op jit(solution)/shard_map/all_gather | solution.py:123
  10.8 12.9 %collective-permute-start = (bf16[608,128]{1,0:T(8,128)(2,1)S(1)}, bf16[608,128]{1,0:T(8,128)(2,1)S(1)}, u32[]{:S(2)}, u32[]{:S(2)}) collective-permute-start(bf16[608,128]{1,0:T(8,128)(2,1)S(1)} %pad_maximum_fusion), channel_id=1, source_target_pairs={{0,0},{2,32},{4,64},{6,96},{32,2},{34,34},{36,66},{38,98},{64,4},{... | collective-permute-start | bytes 466952 | tf_op jit(solution)/shard_map/ppermute | solution.py:118
  23.6 0.7 copy-start.4
  25.4 1.8 copy-start.2
  28.6 28.2 %collective-permute-start.1 = (bf16[4,176,256]{2,1,0:T(8,128)(2,1)S(1)}, bf16[4,176,256]{2,1,0:T(8,128)(2,1)S(1)}, u32[]{:S(2)}, u32[]{:S(2)}) collective-permute-start(bf16[4,176,256]{2,1,0:T(8,128)(2,1)S(1)} %get-tuple-element.11), channel_id=1, source_target_pairs={{0,32},{32,64},{64,96},{96,128},{128,160},{160,192},{192,224},{224... | collective-permute-start | bytes 1081352 | tf_op jit(solution)/shard_map/ppermute | solution.py:88
  33.5 23.4 %collective-permute-start.2 = (bf16[4,176,256]{2,1,0:T(8,128)(2,1)S(1)}, bf16[4,176,256]{2,1,0:T(8,128)(2,1)S(1)}, u32[]{:S(2)}, u32[]{:S(2)}) collective-permute-start(bf16[4,176,256]{2,1,0:T(8,128)(2,1)S(1)} %get-tuple-element.12), channel_id=1, source_target_pairs={{0,480},{32,0},{64,32},{96,64},{128,96},{160,128},{192,160},{224,1... | collective-permute-start | bytes 1081352 | tf_op jit(solution)/shard_map/ppermute | solution.py:88
  35.4 18.6 %collective-permute-start.3 = (bf16[2,176,256]{2,1,0:T(8,128)(2,1)S(1)}, bf16[2,176,256]{2,1,0:T(8,128)(2,1)S(1)}, u32[]{:S(2)}, u32[]{:S(2)}) collective-permute-start(bf16[2,176,256]{2,1,0:T(8,128)(2,1)S(1)} %get-tuple-element.16), channel_id=1, source_target_pairs={{0,64},{32,96},{64,128},{96,160},{128,192},{160,224},{192,256},{22... | collective-permute-start | bytes 540680 | tf_op jit(solution)/shard_map/ppermute | solution.py:88
  38.8 18.0 %collective-permute-start.4 = (bf16[2,176,256]{2,1,0:T(8,128)(2,1)S(1)}, bf16[2,176,256]{2,1,0:T(8,128)(2,1)S(1)}, u32[]{:S(2)}, u32[]{:S(2)}) collective-permute-start(bf16[2,176,256]{2,1,0:T(8,128)(2,1)S(1)} %get-tuple-element.17), channel_id=1, source_target_pairs={{0,448},{32,480},{64,0},{96,32},{128,64},{160,96},{192,128},{224,1... | collective-permute-start | bytes 540680 | tf_op jit(solution)/shard_map/ppermute | solution.py:88
  57.7 37.7 %all-to-all-start = ((bf16[4,176,256]{2,1,0:T(8,128)(2,1)}), bf16[4,176,256]{2,1,0:T(8,128)(2,1)S(1)}, u32[]{:S(2)}, u32[]{:S(2)}) async-start(bf16[4,176,256]{2,1,0:T(8,128)(2,1)} %add_convert_fusion), calls=%async_computation | async-start | bytes 720896 | tf_op jit(solution)/shard_map/all_to_all | solution.py:92
  68.1 116.8 %all-gather.8.cloned.1.call-start = ((), (), s32[]{:S(2)}) async-start(), calls=%async_computation.6 | async-start | bytes 2162688 | tf_op jit(solution)/shard_map/all_gather | solution.py:141
  116.1 1.7 copy-start
  117.8 14.1 %copy-start.6 = (bf16[256,128]{1,0:T(8,128)(2,1)S(1)}, bf16[256,128]{1,0:T(8,128)(2,1)}, u32[]{:S(2)}) copy-start(bf16[256,128]{1,0:T(8,128)(2,1)} %param.10) | copy-start | bytes 196612
  117.8 27.5 %copy-start.1 = (bf16[9728,128]{1,0:T(8,128)(2,1)S(1)}, bf16[9728,128]{1,0:T(8,128)(2,1)}, u32[]{:S(2)}) copy-start(bf16[9728,128]{1,0:T(8,128)(2,1)} %all-gather.6.cloned.1.call-done) | copy-start | bytes 7471108
  131.9 14.6 %copy-start.5 = (bf16[256,128]{1,0:T(8,128)(2,1)}, bf16[256,128]{1,0:T(8,128)(2,1)S(1)}, u32[]{:S(2)}) copy-start(bf16[256,128]{1,0:T(8,128)(2,1)S(1)} %add_convert_fusion.1) | copy-start | bytes 196612
  146.5 19.1 %all-to-all-start.2 = ((f32[4,256,128]{2,1,0:T(8,128)}), f32[4,256,128]{2,1,0:T(8,128)S(1)}, u32[]{:S(2)}, u32[]{:S(2)}) async-start(f32[4,256,128]{2,1,0:T(8,128)} %shard_map.105), calls=%async_computation.2 | async-start | bytes 1048576 | tf_op jit(solution)/shard_map/all_to_all | solution.py:92
  180.0 39.5 %copy-start.7 = (bf16[256,128]{1,0:T(8,128)(2,1)S(1)}, bf16[256,128]{1,0:T(8,128)(2,1)}, u32[]{:S(2)}) copy-start(bf16[256,128]{1,0:T(8,128)(2,1)} %param.13) | copy-start | bytes 196612
  180.0 14.2 %all-to-all-start.3 = ((f32[4,352,128]{2,1,0:T(8,128)}), f32[4,352,128]{2,1,0:T(8,128)S(1)}, u32[]{:S(2)}, u32[]{:S(2)}) async-start(f32[4,352,128]{2,1,0:T(8,128)} %shard_map.102), calls=%async_computation.3 | async-start | bytes 1441792 | tf_op jit(solution)/shard_map/all_to_all | solution.py:92
  185.0 1.6 copy-start.3
  194.3 25.2 %all-to-all-start.4 = ((bf16[4,256,128]{2,1,0:T(8,128)(2,1)}), bf16[4,256,128]{2,1,0:T(8,128)(2,1)S(1)}, u32[]{:S(2)}, u32[]{:S(2)}) async-start(bf16[4,256,128]{2,1,0:T(8,128)(2,1)} %shard_map.106), calls=%async_computation.4 | async-start | bytes 524288 | tf_op jit(solution)/shard_map/all_to_all | solution.py:92
Sparse Core Ops, SparseCore 0:
  24.4 91.5 all-gather.5
  119.8 57.6 all-gather.7

commit v2 on v1

--- a/solution.py
+++ b/solution.py
@@ -60,32 +60,47 @@
         out_ref[n] = total[:, n * 128 : (n + 1) * 128].astype(out_ref.dtype)
 
 
-def child_kernel(left_ref, blocks_ref, out_ref):
-    total = None
-    for h in range(4):
-        right = jnp.concatenate([blocks_ref[4 * h + n, 352:608, :] for n in range(4)], axis=1)
-        left = jnp.concatenate([left_ref[2 * h], left_ref[2 * h + 1]], axis=1)
-        part = jnp.dot(left, right, preferred_element_type=F32)
-        total = part if total is None else total + part
-    for n in range(4):
-        out_ref[n] = total[:, n * 128 : (n + 1) * 128].astype(out_ref.dtype)
+def products_kernel(cov_ref, diag_ref, blocks_ref, out_ref):
+    for first, rows in ((0, 352), (352, 256)):
+        total = None
+        for h in range(4):
+            columns = [blocks_ref[4 * h + n, first : first + rows, :] for n in range(4)]
+            right = jnp.concatenate(columns, axis=1)
+            if first == 0:
+                part = lax.dot_general(
+                    cov_ref[h * 352 : (h + 1) * 352, :],
+                    right,
+                    (((0,), (0,)), ((), ())),
+                    preferred_element_type=F32,
+                )
+            else:
+                left = jnp.concatenate([diag_ref[2 * h], diag_ref[2 * h + 1]], axis=1)
+                part = jnp.dot(left, right, preferred_element_type=F32)
+            total = part if total is None else total + part
+        for n in range(4):
+            tile = total[:, n * 128 : (n + 1) * 128].astype(out_ref.dtype)
+            out_ref[n, first : first + rows, :] = tile
 
 
 def last_kernel(factor_ref, image_ref, out_ref):
-    for y in range(4):
+    for x in range(4):
         total = None
-        for x in range(4):
-            n = (y * 4 + x) * 2
-            left = jnp.concatenate([factor_ref[n], factor_ref[n + 1]], axis=1)
+        for y in range(4):
+            left = jnp.concatenate([factor_ref[y, x, 0], factor_ref[y, x, 1]], axis=1)
             part = lax.dot_general(
-                left, image_ref[x], (((0,), (0,)), ((), ())), preferred_element_type=F32
+                left, image_ref[y], (((0,), (0,)), ((), ())), preferred_element_type=F32
             )
             total = part if total is None else total + part
-        out_ref[y] = total.astype(out_ref.dtype)
+        out_ref[x] = total.astype(out_ref.dtype)
 
 
 def shift(value, by):
     return lax.ppermute(value, Z, [(i, (i + by) % 16) for i in range(16)])
+
+
+def swap(value, first, second):
+    pairs = [(a * 4 + b, b * 4 + a) for a in range(4) for b in range(4)]
+    return lax.ppermute(value, (first, second), pairs)
 
 
 def exchange(value, axis):
@@ -108,19 +123,16 @@
     z = lax.axis_index(Z)
     zl = lax.axis_index("zl")
     column = lax.axis_index(PLANE)
+
+    slab = lax.dynamic_slice_in_dim(parent_panel, column * 128, 128, 1)
+    swapped = swap(jnp.concatenate([slab, child_panel], axis=0), "zl", "x")
+
     ancestor_keep = block_keep(ancestor_pattern, z * 352, 352, 5632)
+    column_keep = block_keep(ancestor_pattern, column * 176, 176, 5632)
     child_keep = block_keep(child_pattern, z * 256, 256, 4096)
-    slab = lax.dynamic_slice_in_dim(parent_panel, column * 128, 128, 1)
-    slab = slab * ancestor_keep[:, None].astype(BF)
-    child_masked = child_panel * child_keep[:, None].astype(BF)
-    cov = (ancestor_cov * ancestor_keep[:, None].astype(BF)).T
-
-    swapped = lax.ppermute(
-        jnp.concatenate([slab, child_masked], axis=0),
-        ("zl", "x"),
-        [(a * 4 + b, b * 4 + a) for a in range(4) for b in range(4)],
-    )
-    blocks = lax.all_gather(swapped, Z, axis=0)
+    child_column_keep = block_keep(child_pattern, column * 128, 128, 4096)
+    cov = ancestor_cov * ancestor_keep[:, None].astype(BF) * column_keep[None, :].astype(BF)
+    cov = cov.T
 
     classes = jnp.stack([(zl + 1) % 4, (zl + 3) % 4, (zl + 2) % 4, zl]).astype(jnp.int32)
     bundle = jax.ShapeDtypeStruct((4, 176, 256), BF)
@@ -130,53 +142,50 @@
         [classes, cov, parent_panel],
         2 * 176 * 352 * 4096,
     )
+    blocks = lax.all_gather(after(swapped, own), Z, axis=0)
     right, left = shift(right, 1), shift(left, -1)
     far = jnp.concatenate([shift(far[:2], 2), shift(far[2:], -2)], axis=0)
+    factor = swap(after(child_panel, own), "zh", "y")
     image = own + right.astype(F32) + left.astype(F32) + far.astype(F32)
-    image = exchange(image.astype(BF), "zh")
+    image = image.astype(BF)
+
+    cov_wide = lax.all_gather(after(cov, image), ("y", "c"), axis=0, tiled=True)
+    factor = lax.all_gather(after(factor, image), "c", axis=0)
+    factor = lax.all_gather(factor, "x", axis=0)
+    image = after(exchange(image, "zh"), cov_wide, factor)
     image = jnp.sum(image.astype(F32), axis=0).astype(BF)
-
-    cov_wide = lax.all_gather(cov, ("y", "c"), axis=0, tiled=True)
+    factor = lax.all_gather(after(factor, image), "y", axis=0)
     image_wide = lax.all_gather(image, ("y", "c"), axis=0, tiled=True)
-    factor = lax.all_gather(after(swapped[352:], image), PLANE, axis=0)
 
     (inner,) = call(
         panel_kernel,
-        [jax.ShapeDtypeStruct((4, 256, 128), F32)],
+        [jax.ShapeDtypeStruct((4, 256, 128), BF)],
         [image_wide, blocks],
         2 * 1408 * 256 * 512,
     )
-    inner = jnp.sum(exchange(inner, "x"), axis=0)
+    inner = jnp.sum(exchange(inner, "x").astype(F32), axis=0)
     parent_diag = (parent_inverse.astype(F32) + inner).astype(BF)
 
-    diag_wide = lax.all_gather(parent_diag, ("y", "c"), axis=0)
+    diag_wide = parent_diag * child_column_keep[None, :].astype(BF)
+    diag_wide = lax.all_gather(diag_wide, ("y", "c"), axis=0)
     (product,) = call(
-        child_kernel,
-        [jax.ShapeDtypeStruct((4, 256, 128), F32)],
-        [diag_wide, blocks],
-        2 * 1024 * 256 * 512,
-    )
-    product = jnp.sum(exchange(product, "x"), axis=0)
-    parent_child = (-product * child_keep[:, None].astype(F32)).astype(BF)
-
-    child_wide = lax.all_gather(parent_child, "zl", axis=0)
-
-    (product,) = call(
-        panel_kernel,
-        [jax.ShapeDtypeStruct((4, 352, 128), F32)],
-        [cov_wide, blocks],
-        2 * 1408 * 352 * 512,
-    )
-    product = jnp.sum(exchange(after(product, child_wide), "x"), axis=0)
-    ancestor_block = (-product * ancestor_keep[:, None].astype(F32)).astype(BF)
-
+        products_kernel,
+        [jax.ShapeDtypeStruct((4, 608, 128), BF)],
+        [cov_wide, diag_wide, blocks],
+        2 * (1408 * 352 + 1024 * 256) * 512,
+    )
+    product = -jnp.sum(exchange(product, "x").astype(F32), axis=0)
+    ancestor_block = (product[:352] * ancestor_keep[:, None].astype(F32)).astype(BF)
+    parent_child = (product[352:] * child_keep[:, None].astype(F32)).astype(BF)
+
+    child_wide = lax.all_gather(parent_child, "zh", axis=0)
     (inner,) = call(
         last_kernel,
         [jax.ShapeDtypeStruct((4, 256, 128), BF)],
         [factor, child_wide],
         2 * 1024 * 1024 * 128,
     )
-    inner = jnp.sum(exchange(inner, "zh").astype(F32), axis=0)
+    inner = jnp.sum(exchange(inner, "zl").astype(F32), axis=0)
     child_diag = (child_inverse.astype(F32) - inner).astype(BF)
     return (ancestor_block, parent_diag, parent_child, child_diag)
 

time: 228 us -> 227 us (level)
  the two profiles are of different devices: /device:TPU:32 before, /device:TPU:8 now
where the time goes in v2:
time: 227 us; the launch traced here: 226 us
  blocking collectives  81.6 us (36%)
  waiting for transfers between devices  55.5 us (24%)
  starting transfers between devices  53.6 us (24%)
  between operations  14.4 us (6%)
  local copies, waits for them, and re-layouts  8.07 us (4%)
  other arithmetic  7 us (3%)
  Pallas kernels  6.37 us (3%)
    ppermute x4, starting transfers between devices, shift(): return lax.ppermute(value, Z, [(i, (i + by) % 16) for i in range(16)])  26.8 us
    all_to_all x4, waiting for transfers between devices, exchange(): return lax.all_to_all(value, axis, split_axis=0, concat_axis=0, tiled=True)  24.5 us
    all_gather x1, blocking collectives, per_device(): child_wide = lax.all_gather(parent_child, 'zh', axis=0)  22.4 us
    ppermute x2, waiting for transfers between devices, swap(): return lax.ppermute(value, (first, second), pairs)  20.9 us
    all_to_all x4, starting transfers between devices, exchange(): return lax.all_to_all(value, axis, split_axis=0, concat_axis=0, tiled=True)  18.4 us
    all_gather x1, blocking collectives, per_device(): factor = lax.all_gather(factor, 'x', axis=0)  16.7 us
    all_gather x1, blocking collectives, per_device(): cov_wide = lax.all_gather(after(cov, image), ('y', 'c'), axis=0, tiled=True)  14.1 us
    all_gather x1, blocking collectives, per_device(): image_wide = lax.all_gather(image, ('y', 'c'), axis=0, tiled=True)  13.4 us
  transfers between devices with their start and end apart: 12, of which 6 were waited for; matrix products, arithmetic and copies ran while one was open for 2% of the time, Pallas kernels for 2%

profile of v2, /device:TPU:8, one launch (start us, length us, event | category | flops | bytes accessed | tf_op | source)
XLA Modules:
  0.0 226.5 jit_solution(17357209555284681531)
XLA Ops:
  7.2 0.9 constant_dynamic-slice_fusion
  11.3 1.0 multiply_bitcast_fusion.at_ref
  12.3 1.8 copy-done.3
  14.2 1.5 shard_map.102
  16.3 10.0 %collective-permute-start = (bf16[4,176,256]{2,1,0:T(8,128)(2,1)S(1)}, bf16[4,176,256]{2,1,0:T(8,128)(2,1)S(1)}, u32[]{:S(2)}, u32[]{:S(2)}) collective-permute-start(bf16[4,176,256]{2,1,0:T(8,128)(2,1)S(1)} %get-tuple-element.15), channel_id=1, source_target_pairs={{0,32},{32,64},{64,96},{96,128},{128,160},{160,192},{192,224},{224... | collective-permute-start | bytes 1081352 | tf_op jit(solution)/shard_map/ppermute | solution.py:98
  26.4 8.6 %collective-permute-start.1 = (bf16[4,176,256]{2,1,0:T(8,128)(2,1)S(1)}, bf16[4,176,256]{2,1,0:T(8,128)(2,1)S(1)}, u32[]{:S(2)}, u32[]{:S(2)}) collective-permute-start(bf16[4,176,256]{2,1,0:T(8,128)(2,1)S(1)} %get-tuple-element.16), channel_id=1, source_target_pairs={{0,480},{32,0},{64,32},{96,64},{128,96},{160,128},{192,160},{224,1... | collective-permute-start | bytes 1081352 | tf_op jit(solution)/shard_map/ppermute | solution.py:98
  35.0 1.9 collective-permute-start.2
  37.0 6.2 %collective-permute-start.3 = (bf16[2,176,256]{2,1,0:T(8,128)(2,1)S(1)}, bf16[2,176,256]{2,1,0:T(8,128)(2,1)S(1)}, u32[]{:S(2)}, u32[]{:S(2)}) collective-permute-start(bf16[2,176,256]{2,1,0:T(8,128)(2,1)S(1)} %get-tuple-element.27), channel_id=1, source_target_pairs={{0,448},{32,480},{64,0},{96,32},{128,64},{160,96},{192,128},{224,1... | collective-permute-start | bytes 540680 | tf_op jit(solution)/shard_map/ppermute | solution.py:98
  43.2 5.6 %collective-permute-done.2 = bf16[2,176,256]{2,1,0:T(8,128)(2,1)S(1)} collective-permute-done((bf16[2,176,256]{2,1,0:T(8,128)(2,1)S(1)}, bf16[2,176,256]{2,1,0:T(8,128)(2,1)S(1)}, u32[]{:S(2)}, u32[]{:S(2)}) %collective-permute-start.2) | collective-permute-done | bytes 180256 | tf_op jit(solution)/shard_map/ppermute | solution.py:98
  48.8 4.5 %collective-permute-done.3 = bf16[2,176,256]{2,1,0:T(8,128)(2,1)S(1)} collective-permute-done((bf16[2,176,256]{2,1,0:T(8,128)(2,1)S(1)}, bf16[2,176,256]{2,1,0:T(8,128)(2,1)S(1)}, u32[]{:S(2)}, u32[]{:S(2)}) %collective-permute-start.3) | collective-permute-done | bytes 180256 | tf_op jit(solution)/shard_map/ppermute | solution.py:98
  53.2 0.9 add_convert_fusion
  54.2 8.2 %all-to-all-start = ((bf16[4,176,256]{2,1,0:T(8,128)(2,1)}), bf16[4,176,256]{2,1,0:T(8,128)(2,1)S(1)}, u32[]{:S(2)}, u32[]{:S(2)}) async-start(bf16[4,176,256]{2,1,0:T(8,128)(2,1)} %add_convert_fusion), calls=%async_computation | async-start | bytes 720896 | tf_op jit(solution)/shard_map/all_to_all | solution.py:107
  62.4 7.7 %collective-permute-start.4 = (bf16[256,128]{1,0:T(8,128)(2,1)S(1)}, bf16[256,128]{1,0:T(8,128)(2,1)S(1)}, u32[]{:S(2)}, u32[]{:S(2)}) collective-permute-start(bf16[256,128]{1,0:T(8,128)(2,1)S(1)} %copy-done.7), channel_id=1, source_target_pairs={{0,0},{8,128},{16,256},{24,384},{128,8},{136,136},{144,264},{152,3... | collective-permute-start | bytes 196616 | tf_op jit(solution)/shard_map/ppermute | solution.py:103
  70.0 20.9 %collective-permute-done.4 = bf16[256,128]{1,0:T(8,128)(2,1)S(1)} collective-permute-done((bf16[256,128]{1,0:T(8,128)(2,1)S(1)}, bf16[256,128]{1,0:T(8,128)(2,1)S(1)}, u32[]{:S(2)}, u32[]{:S(2)}) %collective-permute-start.4) | collective-permute-done | bytes 65568 | tf_op jit(solution)/shard_map/ppermute | solution.py:103
  90.9 1.9 all-gather
  92.8 16.7 %all-gather.1 = bf16[8,256,128]{2,1,0:T(8,128)(2,1)} all-gather(bf16[2,256,128]{2,1,0:T(8,128)(2,1)S(1)} %bitcast.18), channel_id=3, replica_groups=mesh['zh'=4,'zl'=4,'y'=4,'x'=4,'c'=2] {'x'}, dimensions={0}, use_global_device_ids=true | all-gather | bytes 655360 | tf_op jit(solution)/shard_map/all_gather | solution.py:154
  109.5 14.1 %all_gather.42.cov_ref = bf16[1408,352]{1,0:T(8,128)(2,1)} all-gather(bf16[176,352]{1,0:T(8,128)(2,1)S(1)} %multiply_bitcast_fusion.at_ref), channel_id=1, replica_groups=mesh['zh'=4,'zl'=4,'y'=4,'x'=4,'c'=2] {'y','c'}, dimensions={0}, use_global_device_ids=true | all-gather | bytes 1115136 | tf_op jit(solution)/shard_map/all_gather | solution.py:152
  123.8 13.4 %all_gather.47.left_ref = bf16[1408,256]{1,0:T(8,128)(2,1)S(1)} all-gather(bf16[176,256]{1,0:T(8,128)(2,1)S(1)} %reduce_sum.77), channel_id=1, replica_groups=mesh['zh'=4,'zl'=4,'y'=4,'x'=4,'c'=2] {'y','c'}, dimensions={0}, use_global_device_ids=true | all-gather | bytes 811008 | tf_op jit(solution)/shard_map/all_gather | solution.py:158
  137.2 1.8 copy-done
  139.0 1.4 shard_map.103
  140.4 3.4 %all-to-all-start.1 = ((bf16[4,256,128]{2,1,0:T(8,128)(2,1)}), bf16[4,256,128]{2,1,0:T(8,128)(2,1)S(1)}, u32[]{:S(2)}, u32[]{:S(2)}) async-start(bf16[4,256,128]{2,1,0:T(8,128)(2,1)} %shard_map.103), calls=%async_computation.1 | async-start | bytes 524288 | tf_op jit(solution)/shard_map/all_to_all | solution.py:107
  144.0 7.3 %all-to-all-done.1 = bf16[4,256,128]{2,1,0:T(8,128)(2,1)S(1)} async-done(((bf16[4,256,128]{2,1,0:T(8,128)(2,1)}), bf16[4,256,128]{2,1,0:T(8,128)(2,1)S(1)}, u32[]{:S(2)}, u32[]{:S(2)}) %all-to-all-start.1) | async-done | bytes 262176 | tf_op jit(solution)/shard_map/all_to_all | solution.py:107
  152.0 13.1 %all-gather.3 = bf16[2048,128]{1,0:T(8,128)(2,1)S(1)} all-gather(bf16[256,128]{1,0:T(8,128)(2,1)S(1)} %get-tuple-element.24), channel_id=5, replica_groups=mesh['zh'=4,'zl'=4,'y'=4,'x'=4,'c'=2] {'y','c'}, dimensions={0}, use_global_device_ids=true | all-gather | bytes 589824 | tf_op jit(solution)/shard_map/all_gather | solution.py:170
  165.1 1.2 copy-done.2
  166.3 2.0 shard_map.104
  168.3 3.5 %all-to-all-start.2 = ((bf16[4,608,128]{2,1,0:T(8,128)(2,1)}), bf16[4,608,128]{2,1,0:T(8,128)(2,1)S(1)}, u32[]{:S(2)}, u32[]{:S(2)}) async-start(bf16[4,608,128]{2,1,0:T(8,128)(2,1)} %shard_map.104), calls=%async_computation.2 | async-start | bytes 1245184 | tf_op jit(solution)/shard_map/all_to_all | solution.py:107
  171.9 11.2 %all-to-all-done.2 = bf16[4,608,128]{2,1,0:T(8,128)(2,1)S(1)} async-done(((bf16[4,608,128]{2,1,0:T(8,128)(2,1)}), bf16[4,608,128]{2,1,0:T(8,128)(2,1)S(1)}, u32[]{:S(2)}, u32[]{:S(2)}) %all-to-all-start.2) | async-done | bytes 622624 | tf_op jit(solution)/shard_map/all_to_all | solution.py:107
  183.3 22.4 %all-gather.5 = bf16[1024,128]{1,0:T(8,128)(2,1)S(1)} all-gather(bf16[256,128]{1,0:T(8,128)(2,1)S(1)} %fusion.1), channel_id=7, replica_groups=mesh['zh'=4,'zl'=4,'y'=4,'x'=4,'c'=2] {'zh'}, dimensions={0}, use_global_device_ids=true | all-gather | bytes 327680 | tf_op jit(solution)/shard_map/all_gather | solution.py:181
  205.7 1.6 copy-done.4
  207.3 1.5 shard_map.105
  208.8 3.4 %all-to-all-start.3 = ((bf16[4,256,128]{2,1,0:T(8,128)(2,1)}), bf16[4,256,128]{2,1,0:T(8,128)(2,1)S(1)}, u32[]{:S(2)}, u32[]{:S(2)}) async-start(bf16[4,256,128]{2,1,0:T(8,128)(2,1)} %shard_map.105), calls=%async_computation.3 | async-start | bytes 524288 | tf_op jit(solution)/shard_map/all_to_all | solution.py:107
  213.0 6.0 %all-to-all-done.3 = bf16[4,256,128]{2,1,0:T(8,128)(2,1)S(1)} async-done(((bf16[4,256,128]{2,1,0:T(8,128)(2,1)}), bf16[4,256,128]{2,1,0:T(8,128)(2,1)S(1)}, u32[]{:S(2)}, u32[]{:S(2)}) %all-to-all-start.3) | async-done | bytes 262176 | tf_op jit(solution)/shard_map/all_to_all | solution.py:107
  (53 shorter events, 6.5 us)
Async XLA Ops:
  7.2 130.0 %all-gather.9.cloned.1.call-start = ((), (), s32[]{:S(2)}) async-start(), calls=%async_computation.4 | async-start | bytes 2646016 | tf_op jit(solution)/shard_map/all_gather | solution.py:145
  9.0 6.7 %collective-permute-start.5 = (bf16[608,128]{1,0:T(8,128)(2,1)S(1)}, bf16[608,128]{1,0:T(8,128)(2,1)S(1)}, u32[]{:S(2)}, u32[]{:S(2)}) collective-permute-start(bf16[608,128]{1,0:T(8,128)(2,1)S(1)} %pad_maximum_fusion), channel_id=1, source_target_pairs={{0,0},{2,32},{4,64},{6,96},{32,2},{34,34},{36,66},{38,98},{64,4},{... | collective-permute-start | bytes 466952 | tf_op jit(solution)/shard_map/ppermute | solution.py:103
  12.3 1.8 copy-start.3
  15.6 46.7 %copy-start.7 = (bf16[256,128]{1,0:T(8,128)(2,1)S(1)}, bf16[256,128]{1,0:T(8,128)(2,1)}, u32[]{:S(2)}) copy-start(bf16[256,128]{1,0:T(8,128)(2,1)} %param.12) | copy-start | bytes 196612
  15.7 0.7 copy-start.6
  16.3 36.9 %collective-permute-start = (bf16[4,176,256]{2,1,0:T(8,128)(2,1)S(1)}, bf16[4,176,256]{2,1,0:T(8,128)(2,1)S(1)}, u32[]{:S(2)}, u32[]{:S(2)}) collective-permute-start(bf16[4,176,256]{2,1,0:T(8,128)(2,1)S(1)} %get-tuple-element.15), channel_id=1, source_target_pairs={{0,32},{32,64},{64,96},{96,128},{128,160},{160,192},{192,224},{224... | collective-permute-start | bytes 1081352 | tf_op jit(solution)/shard_map/ppermute | solution.py:98
  26.4 26.9 %collective-permute-start.1 = (bf16[4,176,256]{2,1,0:T(8,128)(2,1)S(1)}, bf16[4,176,256]{2,1,0:T(8,128)(2,1)S(1)}, u32[]{:S(2)}, u32[]{:S(2)}) collective-permute-start(bf16[4,176,256]{2,1,0:T(8,128)(2,1)S(1)} %get-tuple-element.16), channel_id=1, source_target_pairs={{0,480},{32,0},{64,32},{96,64},{128,96},{160,128},{192,160},{224,1... | collective-permute-start | bytes 1081352 | tf_op jit(solution)/shard_map/ppermute | solution.py:98
  35.0 13.7 %collective-permute-start.2 = (bf16[2,176,256]{2,1,0:T(8,128)(2,1)S(1)}, bf16[2,176,256]{2,1,0:T(8,128)(2,1)S(1)}, u32[]{:S(2)}, u32[]{:S(2)}) collective-permute-start(bf16[2,176,256]{2,1,0:T(8,128)(2,1)S(1)} %get-tuple-element.26), channel_id=1, source_target_pairs={{0,64},{32,96},{64,128},{96,160},{128,192},{160,224},{192,256},{22... | collective-permute-start | bytes 540680 | tf_op jit(solution)/shard_map/ppermute | solution.py:98
  37.0 16.3 %collective-permute-start.3 = (bf16[2,176,256]{2,1,0:T(8,128)(2,1)S(1)}, bf16[2,176,256]{2,1,0:T(8,128)(2,1)S(1)}, u32[]{:S(2)}, u32[]{:S(2)}) collective-permute-start(bf16[2,176,256]{2,1,0:T(8,128)(2,1)S(1)} %get-tuple-element.27), channel_id=1, source_target_pairs={{0,448},{32,480},{64,0},{96,32},{128,64},{160,96},{192,128},{224,1... | collective-permute-start | bytes 540680 | tf_op jit(solution)/shard_map/ppermute | solution.py:98
  54.2 69.5 %all-to-all-start = ((bf16[4,176,256]{2,1,0:T(8,128)(2,1)}), bf16[4,176,256]{2,1,0:T(8,128)(2,1)S(1)}, u32[]{:S(2)}, u32[]{:S(2)}) async-start(bf16[4,176,256]{2,1,0:T(8,128)(2,1)} %add_convert_fusion), calls=%async_computation | async-start | bytes 720896 | tf_op jit(solution)/shard_map/all_to_all | solution.py:107
  62.4 143.4 %all-gather.11.cloned.1.call-start = ((), (), s32[]{:S(2)}) async-start(), calls=%async_computation.5 | async-start | bytes 2621440 | tf_op jit(solution)/shard_map/all_gather | solution.py:157
  62.4 28.6 %collective-permute-start.4 = (bf16[256,128]{1,0:T(8,128)(2,1)S(1)}, bf16[256,128]{1,0:T(8,128)(2,1)S(1)}, u32[]{:S(2)}, u32[]{:S(2)}) collective-permute-start(bf16[256,128]{1,0:T(8,128)(2,1)S(1)} %copy-done.7), channel_id=1, source_target_pairs={{0,0},{8,128},{16,256},{24,384},{128,8},{136,136},{144,264},{152,3... | collective-permute-start | bytes 196616 | tf_op jit(solution)/shard_map/ppermute | solution.py:103
  123.7 20.1 %copy-start.10 = (s32[16]{0:T(128)S(1)}, s32[16]{0:T(128)}, u32[]{:S(2)}) copy-start(s32[16]{0:T(128)} %param.11) | copy-start | bytes 196
  123.7 27.6 %copy-start.8 = (bf16[256,128]{1,0:T(8,128)(2,1)S(1)}, bf16[256,128]{1,0:T(8,128)(2,1)}, u32[]{:S(2)}) copy-start(bf16[256,128]{1,0:T(8,128)(2,1)} %param.10) | copy-start | bytes 196612
  137.2 1.8 copy-start
  139.0 26.0 %copy-start.1 = (bf16[9728,128]{1,0:T(8,128)(2,1)S(1)}, bf16[9728,128]{1,0:T(8,128)(2,1)}, u32[]{:S(2)}) copy-start(bf16[9728,128]{1,0:T(8,128)(2,1)} %all-gather.9.cloned.1.call-done) | copy-start | bytes 7471108
  140.4 10.8 %all-to-all-start.1 = ((bf16[4,256,128]{2,1,0:T(8,128)(2,1)}), bf16[4,256,128]{2,1,0:T(8,128)(2,1)S(1)}, u32[]{:S(2)}, u32[]{:S(2)}) async-start(bf16[4,256,128]{2,1,0:T(8,128)(2,1)} %shard_map.103), calls=%async_computation.1 | async-start | bytes 524288 | tf_op jit(solution)/shard_map/all_to_all | solution.py:107
  165.1 1.2 copy-start.2
  168.3 14.8 %all-to-all-start.2 = ((bf16[4,608,128]{2,1,0:T(8,128)(2,1)}), bf16[4,608,128]{2,1,0:T(8,128)(2,1)S(1)}, u32[]{:S(2)}, u32[]{:S(2)}) async-start(bf16[4,608,128]{2,1,0:T(8,128)(2,1)} %shard_map.104), calls=%async_computation.2 | async-start | bytes 1245184 | tf_op jit(solution)/shard_map/all_to_all | solution.py:107
  183.2 35.8 %copy-start.9 = (bf16[256,128]{1,0:T(8,128)(2,1)S(1)}, bf16[256,128]{1,0:T(8,128)(2,1)}, u32[]{:S(2)}) copy-start(bf16[256,128]{1,0:T(8,128)(2,1)} %param.13) | copy-start | bytes 196612
  183.3 36.3 %copy-start.5 = (bf16[256,128]{1,0:T(8,128)(2,1)}, bf16[256,128]{1,0:T(8,128)(2,1)S(1)}, u32[]{:S(2)}) copy-start(bf16[256,128]{1,0:T(8,128)(2,1)S(1)} %fusion.1) | copy-start | bytes 196612
  205.7 1.6 copy-start.4
  208.8 10.2 %all-to-all-start.3 = ((bf16[4,256,128]{2,1,0:T(8,128)(2,1)}), bf16[4,256,128]{2,1,0:T(8,128)(2,1)S(1)}, u32[]{:S(2)}, u32[]{:S(2)}) async-start(bf16[4,256,128]{2,1,0:T(8,128)(2,1)} %shard_map.105), calls=%async_computation.3 | async-start | bytes 524288 | tf_op jit(solution)/shard_map/all_to_all | solution.py:107
Sparse Core Ops, SparseCore 0:
  16.5 104.9 all-gather.8
  123.9 34.6 all-gather.10

commit v3 on v2

--- a/solution.py
+++ b/solution.py
@@ -86,7 +86,8 @@
     for x in range(4):
         total = None
         for y in range(4):
-            left = jnp.concatenate([factor_ref[y, x, 0], factor_ref[y, x, 1]], axis=1)
+            n = (y * 4 + x) * 2
+            left = jnp.concatenate([factor_ref[n], factor_ref[n + 1]], axis=1)
             part = lax.dot_general(
                 left, image_ref[y], (((0,), (0,)), ((), ())), preferred_element_type=F32
             )
@@ -145,16 +146,14 @@
     blocks = lax.all_gather(after(swapped, own), Z, axis=0)
     right, left = shift(right, 1), shift(left, -1)
     far = jnp.concatenate([shift(far[:2], 2), shift(far[2:], -2)], axis=0)
-    factor = swap(after(child_panel, own), "zh", "y")
     image = own + right.astype(F32) + left.astype(F32) + far.astype(F32)
     image = image.astype(BF)
 
+    factor = swap(after(child_panel, image), "zh", "y")
     cov_wide = lax.all_gather(after(cov, image), ("y", "c"), axis=0, tiled=True)
-    factor = lax.all_gather(after(factor, image), "c", axis=0)
-    factor = lax.all_gather(factor, "x", axis=0)
-    image = after(exchange(image, "zh"), cov_wide, factor)
+    image = after(exchange(image, "zh"), cov_wide)
     image = jnp.sum(image.astype(F32), axis=0).astype(BF)
-    factor = lax.all_gather(after(factor, image), "y", axis=0)
+    factor = lax.all_gather(after(factor, image), PLANE, axis=0)
     image_wide = lax.all_gather(image, ("y", "c"), axis=0, tiled=True)
 
     (inner,) = call(

time: 227 us -> 209 us (0.921)
  the two profiles are of different devices: /device:TPU:8 before, /device:TPU:32 now
where the time goes in v3:
time: 209 us; the launch traced here: 208 us
  blocking collectives  77.4 us (37%)
  waiting for transfers between devices  51.7 us (25%)
  starting transfers between devices  42.5 us (20%)
  between operations  14.3 us (7%)
  local copies, waits for them, and re-layouts  8.6 us (4%)
  other arithmetic  6.99 us (3%)
  Pallas kernels  6.39 us (3%)
    all_gather x1, blocking collectives, per_device(): cov_wide = lax.all_gather(after(cov, image), ('y', 'c'), axis=0, tiled=True)  27 us
    all_to_all x4, waiting for transfers between devices, exchange(): return lax.all_to_all(value, axis, split_axis=0, concat_axis=0, tiled=True)  25.9 us
    all_to_all x4, starting transfers between devices, exchange(): return lax.all_to_all(value, axis, split_axis=0, concat_axis=0, tiled=True)  20.2 us
    all_gather x1, blocking collectives, per_device(): child_wide = lax.all_gather(parent_child, 'zh', axis=0)  19.3 us
    ppermute x4, starting transfers between devices, shift(): return lax.ppermute(value, Z, [(i, (i + by) % 16) for i in range(16)])  18.7 us
    all_gather x1, blocking collectives, per_device(): image_wide = lax.all_gather(image, ('y', 'c'), axis=0, tiled=True)  17 us
    all_gather x1, blocking collectives, per_device(): diag_wide = lax.all_gather(diag_wide, ('y', 'c'), axis=0)  14 us
    all_gather x1, waiting for transfers between devices, per_device(): blocks = lax.all_gather(after(swapped, own), Z, axis=0)  13.9 us
  transfers between devices with their start and end apart: 12, of which 8 were waited for; matrix products, arithmetic and copies ran while one was open for 3% of the time, Pallas kernels for 2%

profile of v3, /device:TPU:32, one launch (start us, length us, event | category | flops | bytes accessed | tf_op | source)
XLA Modules:
  0.0 207.8 jit_solution(5369623109125206854)
XLA Ops:
  7.2 0.9 constant_dynamic-slice_fusion
  8.1 0.8 pad_maximum_fusion
  9.0 2.9 %collective-permute-start.4 = (bf16[608,128]{1,0:T(8,128)(2,1)S(1)}, bf16[608,128]{1,0:T(8,128)(2,1)S(1)}, u32[]{:S(2)}, u32[]{:S(2)}) collective-permute-start(bf16[608,128]{1,0:T(8,128)(2,1)S(1)} %pad_maximum_fusion), channel_id=1, source_target_pairs={{0,0},{2,32},{4,64},{6,96},{32,2},{34,34},{36,66},{38,98},{64,4},{... | collective-permute-start | bytes 466952 | tf_op jit(solution)/shard_map/ppermute | solution.py:104
  13.5 1.0 multiply_bitcast_fusion.at_ref
  14.6 1.8 copy-done.3
  16.4 1.5 shard_map.102
  17.9 3.9 %collective-permute-done.4 = bf16[608,128]{1,0:T(8,128)(2,1)S(1)} collective-permute-done((bf16[608,128]{1,0:T(8,128)(2,1)S(1)}, bf16[608,128]{1,0:T(8,128)(2,1)S(1)}, u32[]{:S(2)}, u32[]{:S(2)}) %collective-permute-start.4) | collective-permute-done | bytes 155680 | tf_op jit(solution)/shard_map/ppermute | solution.py:104
  22.5 4.8 %collective-permute-start = (bf16[4,176,256]{2,1,0:T(8,128)(2,1)S(1)}, bf16[4,176,256]{2,1,0:T(8,128)(2,1)S(1)}, u32[]{:S(2)}, u32[]{:S(2)}) collective-permute-start(bf16[4,176,256]{2,1,0:T(8,128)(2,1)S(1)} %get-tuple-element.14), channel_id=1, source_target_pairs={{0,32},{32,64},{64,96},{96,128},{128,160},{160,192},{192,224},{224... | collective-permute-start | bytes 1081352 | tf_op jit(solution)/shard_map/ppermute | solution.py:99
  27.4 1.9 collective-permute-start.1
  29.3 3.4 %collective-permute-start.2 = (bf16[2,176,256]{2,1,0:T(8,128)(2,1)S(1)}, bf16[2,176,256]{2,1,0:T(8,128)(2,1)S(1)}, u32[]{:S(2)}, u32[]{:S(2)}) collective-permute-start(bf16[2,176,256]{2,1,0:T(8,128)(2,1)S(1)} %get-tuple-element.24), channel_id=1, source_target_pairs={{0,64},{32,96},{64,128},{96,160},{128,192},{160,224},{192,256},{22... | collective-permute-start | bytes 540680 | tf_op jit(solution)/shard_map/ppermute | solution.py:99
  32.7 8.6 %collective-permute-start.3 = (bf16[2,176,256]{2,1,0:T(8,128)(2,1)S(1)}, bf16[2,176,256]{2,1,0:T(8,128)(2,1)S(1)}, u32[]{:S(2)}, u32[]{:S(2)}) collective-permute-start(bf16[2,176,256]{2,1,0:T(8,128)(2,1)S(1)} %get-tuple-element.25), channel_id=1, source_target_pairs={{0,448},{32,480},{64,0},{96,32},{128,64},{160,96},{192,128},{224,1... | collective-permute-start | bytes 540680 | tf_op jit(solution)/shard_map/ppermute | solution.py:99
  41.3 7.2 %collective-permute-done.2 = bf16[2,176,256]{2,1,0:T(8,128)(2,1)S(1)} collective-permute-done((bf16[2,176,256]{2,1,0:T(8,128)(2,1)S(1)}, bf16[2,176,256]{2,1,0:T(8,128)(2,1)S(1)}, u32[]{:S(2)}, u32[]{:S(2)}) %collective-permute-start.2) | collective-permute-done | bytes 180256 | tf_op jit(solution)/shard_map/ppermute | solution.py:99
  49.2 0.9 add_convert_fusion
  50.1 7.4 %all-to-all-start = ((bf16[4,176,256]{2,1,0:T(8,128)(2,1)}), bf16[4,176,256]{2,1,0:T(8,128)(2,1)S(1)}, u32[]{:S(2)}, u32[]{:S(2)}) async-start(bf16[4,176,256]{2,1,0:T(8,128)(2,1)} %add_convert_fusion), calls=%async_computation | async-start | bytes 720896 | tf_op jit(solution)/shard_map/all_to_all | solution.py:108
  58.2 27.0 %all_gather.30.cov_ref = bf16[1408,352]{1,0:T(8,128)(2,1)} all-gather(bf16[176,352]{1,0:T(8,128)(2,1)S(1)} %multiply_bitcast_fusion.at_ref), channel_id=1, replica_groups=mesh['zh'=4,'zl'=4,'y'=4,'x'=4,'c'=2] {'y','c'}, dimensions={0}, use_global_device_ids=true | all-gather | bytes 1115136 | tf_op jit(solution)/shard_map/all_gather | solution.py:153
  85.2 2.7 %all-to-all-done = bf16[4,176,256]{2,1,0:T(8,128)(2,1)S(1)} async-done(((bf16[4,176,256]{2,1,0:T(8,128)(2,1)}), bf16[4,176,256]{2,1,0:T(8,128)(2,1)S(1)}, u32[]{:S(2)}, u32[]{:S(2)}) %all-to-all-start) | async-done | bytes 360480 | tf_op jit(solution)/shard_map/all_to_all | solution.py:108
  88.7 17.0 %all_gather.31.left_ref = bf16[1408,256]{1,0:T(8,128)(2,1)S(1)} all-gather(bf16[176,256]{1,0:T(8,128)(2,1)S(1)} %reduce_sum.77), channel_id=1, replica_groups=mesh['zh'=4,'zl'=4,'y'=4,'x'=4,'c'=2] {'y','c'}, dimensions={0}, use_global_device_ids=true | all-gather | bytes 811008 | tf_op jit(solution)/shard_map/all_gather | solution.py:157
  105.7 13.9 %all-gather.7.cloned.1.call-done = bf16[9728,128]{1,0:T(8,128)(2,1)} async-done(((bf16[608,128]{1,0:T(8,128)(2,1)}), bf16[9728,128]{1,0:T(8,128)(2,1)}) %all-gather.7.cloned.1.call-update) | async-done | bytes 2490384 | tf_op jit(solution)/shard_map/all_gather | solution.py:146
  119.6 1.7 copy-done
  121.3 1.4 shard_map.103
  122.8 5.6 %all-to-all-start.1 = ((bf16[4,256,128]{2,1,0:T(8,128)(2,1)}), bf16[4,256,128]{2,1,0:T(8,128)(2,1)S(1)}, u32[]{:S(2)}, u32[]{:S(2)}) async-start(bf16[4,256,128]{2,1,0:T(8,128)(2,1)} %shard_map.103), calls=%async_computation.1 | async-start | bytes 524288 | tf_op jit(solution)/shard_map/all_to_all | solution.py:108
  128.5 6.6 %all-to-all-done.1 = bf16[4,256,128]{2,1,0:T(8,128)(2,1)S(1)} async-done(((bf16[4,256,128]{2,1,0:T(8,128)(2,1)}), bf16[4,256,128]{2,1,0:T(8,128)(2,1)S(1)}, u32[]{:S(2)}, u32[]{:S(2)}) %all-to-all-start.1) | async-done | bytes 262176 | tf_op jit(solution)/shard_map/all_to_all | solution.py:108
  135.7 14.0 %all-gather.1 = bf16[2048,128]{1,0:T(8,128)(2,1)S(1)} all-gather(bf16[256,128]{1,0:T(8,128)(2,1)S(1)} %get-tuple-element.22), channel_id=3, replica_groups=mesh['zh'=4,'zl'=4,'y'=4,'x'=4,'c'=2] {'y','c'}, dimensions={0}, use_global_device_ids=true | all-gather | bytes 589824 | tf_op jit(solution)/shard_map/all_gather | solution.py:169
  149.7 1.2 copy-done.2
  151.0 2.0 shard_map.104
  153.0 3.5 %all-to-all-start.2 = ((bf16[4,608,128]{2,1,0:T(8,128)(2,1)}), bf16[4,608,128]{2,1,0:T(8,128)(2,1)S(1)}, u32[]{:S(2)}, u32[]{:S(2)}) async-start(bf16[4,608,128]{2,1,0:T(8,128)(2,1)} %shard_map.104), calls=%async_computation.2 | async-start | bytes 1245184 | tf_op jit(solution)/shard_map/all_to_all | solution.py:108
  156.6 11.2 %all-to-all-done.2 = bf16[4,608,128]{2,1,0:T(8,128)(2,1)S(1)} async-done(((bf16[4,608,128]{2,1,0:T(8,128)(2,1)}), bf16[4,608,128]{2,1,0:T(8,128)(2,1)S(1)}, u32[]{:S(2)}, u32[]{:S(2)}) %all-to-all-start.2) | async-done | bytes 622624 | tf_op jit(solution)/shard_map/all_to_all | solution.py:108
  168.0 19.3 %all-gather.3 = bf16[1024,128]{1,0:T(8,128)(2,1)S(1)} all-gather(bf16[256,128]{1,0:T(8,128)(2,1)S(1)} %fusion.1), channel_id=5, replica_groups=mesh['zh'=4,'zl'=4,'y'=4,'x'=4,'c'=2] {'zh'}, dimensions={0}, use_global_device_ids=true | all-gather | bytes 327680 | tf_op jit(solution)/shard_map/all_gather | solution.py:180
  187.4 1.6 copy-done.4
  189.0 1.5 shard_map.105
  190.4 3.7 %all-to-all-start.3 = ((bf16[4,256,128]{2,1,0:T(8,128)(2,1)}), bf16[4,256,128]{2,1,0:T(8,128)(2,1)S(1)}, u32[]{:S(2)}, u32[]{:S(2)}) async-start(bf16[4,256,128]{2,1,0:T(8,128)(2,1)} %shard_map.105), calls=%async_computation.3 | async-start | bytes 524288 | tf_op jit(solution)/shard_map/all_to_all | solution.py:108
  194.8 5.5 %all-to-all-done.3 = bf16[4,256,128]{2,1,0:T(8,128)(2,1)S(1)} async-done(((bf16[4,256,128]{2,1,0:T(8,128)(2,1)}), bf16[4,256,128]{2,1,0:T(8,128)(2,1)S(1)}, u32[]{:S(2)}, u32[]{:S(2)}) %all-to-all-start.3) | async-done | bytes 262176 | tf_op jit(solution)/shard_map/all_to_all | solution.py:108
  (53 shorter events, 7.0 us)
Async XLA Ops:
  7.2 112.5 %all-gather.7.cloned.1.call-start = ((), (), s32[]{:S(2)}) async-start(), calls=%async_computation.4 | async-start | bytes 2646016 | tf_op jit(solution)/shard_map/all_gather | solution.py:146
  9.0 12.9 %collective-permute-start.4 = (bf16[608,128]{1,0:T(8,128)(2,1)S(1)}, bf16[608,128]{1,0:T(8,128)(2,1)S(1)}, u32[]{:S(2)}, u32[]{:S(2)}) collective-permute-start(bf16[608,128]{1,0:T(8,128)(2,1)S(1)} %pad_maximum_fusion), channel_id=1, source_target_pairs={{0,0},{2,32},{4,64},{6,96},{32,2},{34,34},{36,66},{38,98},{64,4},{... | collective-permute-start | bytes 466952 | tf_op jit(solution)/shard_map/ppermute | solution.py:104
  14.6 1.8 copy-start.3
  17.9 39.6 %copy-start.7 = (bf16[256,128]{1,0:T(8,128)(2,1)S(1)}, bf16[256,128]{1,0:T(8,128)(2,1)}, u32[]{:S(2)}) copy-start(bf16[256,128]{1,0:T(8,128)(2,1)} %param.12) | copy-start | bytes 196612
  21.9 0.7 copy-start.6
  22.5 26.6 %collective-permute-start = (bf16[4,176,256]{2,1,0:T(8,128)(2,1)S(1)}, bf16[4,176,256]{2,1,0:T(8,128)(2,1)S(1)}, u32[]{:S(2)}, u32[]{:S(2)}) collective-permute-start(bf16[4,176,256]{2,1,0:T(8,128)(2,1)S(1)} %get-tuple-element.14), channel_id=1, source_target_pairs={{0,32},{32,64},{64,96},{96,128},{128,160},{160,192},{192,224},{224... | collective-permute-start | bytes 1081352 | tf_op jit(solution)/shard_map/ppermute | solution.py:99
  27.4 21.8 %collective-permute-start.1 = (bf16[4,176,256]{2,1,0:T(8,128)(2,1)S(1)}, bf16[4,176,256]{2,1,0:T(8,128)(2,1)S(1)}, u32[]{:S(2)}, u32[]{:S(2)}) collective-permute-start(bf16[4,176,256]{2,1,0:T(8,128)(2,1)S(1)} %get-tuple-element.15), channel_id=1, source_target_pairs={{0,480},{32,0},{64,32},{96,64},{128,96},{160,128},{192,160},{224,1... | collective-permute-start | bytes 1081352 | tf_op jit(solution)/shard_map/ppermute | solution.py:99
  29.3 19.2 %collective-permute-start.2 = (bf16[2,176,256]{2,1,0:T(8,128)(2,1)S(1)}, bf16[2,176,256]{2,1,0:T(8,128)(2,1)S(1)}, u32[]{:S(2)}, u32[]{:S(2)}) collective-permute-start(bf16[2,176,256]{2,1,0:T(8,128)(2,1)S(1)} %get-tuple-element.24), channel_id=1, source_target_pairs={{0,64},{32,96},{64,128},{96,160},{128,192},{160,224},{192,256},{22... | collective-permute-start | bytes 540680 | tf_op jit(solution)/shard_map/ppermute | solution.py:99
  32.7 16.5 %collective-permute-start.3 = (bf16[2,176,256]{2,1,0:T(8,128)(2,1)S(1)}, bf16[2,176,256]{2,1,0:T(8,128)(2,1)S(1)}, u32[]{:S(2)}, u32[]{:S(2)}) collective-permute-start(bf16[2,176,256]{2,1,0:T(8,128)(2,1)S(1)} %get-tuple-element.25), channel_id=1, source_target_pairs={{0,448},{32,480},{64,0},{96,32},{128,64},{160,96},{192,128},{224,1... | collective-permute-start | bytes 540680 | tf_op jit(solution)/shard_map/ppermute | solution.py:99
  50.1 37.9 %all-to-all-start = ((bf16[4,176,256]{2,1,0:T(8,128)(2,1)}), bf16[4,176,256]{2,1,0:T(8,128)(2,1)S(1)}, u32[]{:S(2)}, u32[]{:S(2)}) async-start(bf16[4,176,256]{2,1,0:T(8,128)(2,1)} %add_convert_fusion), calls=%async_computation | async-start | bytes 720896 | tf_op jit(solution)/shard_map/all_to_all | solution.py:108
  57.5 129.8 %all-gather.9.cloned.1.call-start = ((), (), s32[]{:S(2)}) async-start(), calls=%async_computation.5 | async-start | bytes 2162688 | tf_op jit(solution)/shard_map/all_gather | solution.py:156
  57.5 30.5 %collective-permute-start.5 = (bf16[256,128]{1,0:T(8,128)(2,1)S(1)}, bf16[256,128]{1,0:T(8,128)(2,1)S(1)}, u32[]{:S(2)}, u32[]{:S(2)}) collective-permute-start(bf16[256,128]{1,0:T(8,128)(2,1)S(1)} %copy-done.7), channel_id=1, source_target_pairs={{0,0},{8,128},{16,256},{24,384},{128,8},{136,136},{144,264},{152,3... | collective-permute-start | bytes 196616 | tf_op jit(solution)/shard_map/ppermute | solution.py:104
  88.0 40.3 %copy-start.11 = (s32[16]{0:T(128)S(1)}, s32[16]{0:T(128)}, u32[]{:S(2)}) copy-start(s32[16]{0:T(128)} %param.11) | copy-start | bytes 196
  88.1 0.6 copy-start.9
  88.7 46.4 %copy-start.8 = (bf16[256,128]{1,0:T(8,128)(2,1)S(1)}, bf16[256,128]{1,0:T(8,128)(2,1)}, u32[]{:S(2)}) copy-start(bf16[256,128]{1,0:T(8,128)(2,1)} %param.10) | copy-start | bytes 196612
  119.6 1.7 copy-start
  121.3 28.4 %copy-start.1 = (bf16[9728,128]{1,0:T(8,128)(2,1)S(1)}, bf16[9728,128]{1,0:T(8,128)(2,1)}, u32[]{:S(2)}) copy-start(bf16[9728,128]{1,0:T(8,128)(2,1)} %all-gather.7.cloned.1.call-done) | copy-start | bytes 7471108
  122.8 12.3 %all-to-all-start.1 = ((bf16[4,256,128]{2,1,0:T(8,128)(2,1)}), bf16[4,256,128]{2,1,0:T(8,128)(2,1)S(1)}, u32[]{:S(2)}, u32[]{:S(2)}) async-start(bf16[4,256,128]{2,1,0:T(8,128)(2,1)} %shard_map.103), calls=%async_computation.1 | async-start | bytes 524288 | tf_op jit(solution)/shard_map/all_to_all | solution.py:108
  149.7 1.2 copy-start.2
  153.0 14.8 %all-to-all-start.2 = ((bf16[4,608,128]{2,1,0:T(8,128)(2,1)}), bf16[4,608,128]{2,1,0:T(8,128)(2,1)S(1)}, u32[]{:S(2)}, u32[]{:S(2)}) async-start(bf16[4,608,128]{2,1,0:T(8,128)(2,1)} %shard_map.104), calls=%async_computation.2 | async-start | bytes 1245184 | tf_op jit(solution)/shard_map/all_to_all | solution.py:108
  167.9 32.4 %copy-start.10 = (bf16[256,128]{1,0:T(8,128)(2,1)S(1)}, bf16[256,128]{1,0:T(8,128)(2,1)}, u32[]{:S(2)}) copy-start(bf16[256,128]{1,0:T(8,128)(2,1)} %param.13) | copy-start | bytes 196612
  168.0 33.0 %copy-start.5 = (bf16[256,128]{1,0:T(8,128)(2,1)}, bf16[256,128]{1,0:T(8,128)(2,1)S(1)}, u32[]{:S(2)}) copy-start(bf16[256,128]{1,0:T(8,128)(2,1)S(1)} %fusion.1) | copy-start | bytes 196612
  187.4 1.6 copy-start.4
  190.4 9.9 %all-to-all-start.3 = ((bf16[4,256,128]{2,1,0:T(8,128)(2,1)}), bf16[4,256,128]{2,1,0:T(8,128)(2,1)S(1)}, u32[]{:S(2)}, u32[]{:S(2)}) async-start(bf16[4,256,128]{2,1,0:T(8,128)(2,1)} %shard_map.105), calls=%async_computation.3 | async-start | bytes 524288 | tf_op jit(solution)/shard_map/all_to_all | solution.py:108
Sparse Core Ops, SparseCore 0:
  22.7 96.9 all-gather.6
  123.3 57.2 all-gather.8

commit v4 on v3

--- a/solution.py
+++ b/solution.py
@@ -30,7 +30,7 @@
         out_shape=outs,
         in_specs=specs,
         out_specs=[VMEM] * len(outs),
-        compiler_params=pltpu.CompilerParams(vmem_limit_bytes=40 * 1024 * 1024),
+        compiler_params=pltpu.CompilerParams(vmem_limit_bytes=20 * 1024 * 1024),
         cost_estimate=pl.CostEstimate(flops=flops, bytes_accessed=size, transcendentals=0),
     )(*args)
 
@@ -44,14 +44,19 @@
             out[rh] = block.astype(out.dtype)
 
 
-def panel_kernel(left_ref, blocks_ref, out_ref):
+def block_of(x, h, n):
+    over = lax.rem(x - n + 6, 4) - 2 + n - x
+    return lax.rem(4 * h - over + 16, 16) + n
+
+
+def panel_kernel(x_ref, left_ref, blocks_ref, out_ref):
     rows = left_ref.shape[0] // 4
     total = None
     for h in range(4):
-        right = jnp.concatenate([blocks_ref[4 * h + n, :rows, :] for n in range(4)], axis=1)
+        blocks = [blocks_ref[block_of(x_ref[0], h, n), 0:352, :] for n in range(4)]
         part = lax.dot_general(
             left_ref[h * rows : (h + 1) * rows, :],
-            right,
+            jnp.concatenate(blocks, axis=1),
             (((0,), (0,)), ((), ())),
             preferred_element_type=F32,
         )
@@ -60,26 +65,17 @@
         out_ref[n] = total[:, n * 128 : (n + 1) * 128].astype(out_ref.dtype)
 
 
-def products_kernel(cov_ref, diag_ref, blocks_ref, out_ref):
-    for first, rows in ((0, 352), (352, 256)):
-        total = None
-        for h in range(4):
-            columns = [blocks_ref[4 * h + n, first : first + rows, :] for n in range(4)]
-            right = jnp.concatenate(columns, axis=1)
-            if first == 0:
-                part = lax.dot_general(
-                    cov_ref[h * 352 : (h + 1) * 352, :],
-                    right,
-                    (((0,), (0,)), ((), ())),
-                    preferred_element_type=F32,
-                )
-            else:
-                left = jnp.concatenate([diag_ref[2 * h], diag_ref[2 * h + 1]], axis=1)
-                part = jnp.dot(left, right, preferred_element_type=F32)
-            total = part if total is None else total + part
-        for n in range(4):
-            tile = total[:, n * 128 : (n + 1) * 128].astype(out_ref.dtype)
-            out_ref[n, first : first + rows, :] = tile
+def child_kernel(x_ref, left_ref, beside_ref, blocks_ref, out_ref):
+    total = None
+    for h in range(4):
+        blocks = [blocks_ref[block_of(x_ref[0], h, n), 352:608, :] for n in range(4)]
+        left = jnp.concatenate([left_ref[2 * h], left_ref[2 * h + 1]], axis=1)
+        part = jnp.dot(left, jnp.concatenate(blocks, axis=1), preferred_element_type=F32)
+        total = part if total is None else total + part
+    for n in range(4):
+        out_ref[n, 0:352, :] = beside_ref[n]
+        tile = total[:, n * 128 : (n + 1) * 128].astype(out_ref.dtype)
+        out_ref[n, 352:608, :] = tile
 
 
 def last_kernel(factor_ref, image_ref, out_ref):
@@ -102,6 +98,15 @@
 def swap(value, first, second):
     pairs = [(a * 4 + b, b * 4 + a) for a in range(4) for b in range(4)]
     return lax.ppermute(value, (first, second), pairs)
+
+
+def nearest(value):
+    pairs = []
+    for p in range(16):
+        for n in range(4):
+            plane = (p + (n - p + 1) % 4 - 1) % 16
+            pairs.append((p * 4 + n, plane * 4 + p % 4))
+    return lax.ppermute(value, ("zh", "zl", "x"), pairs)
 
 
 def exchange(value, axis):
@@ -124,9 +129,10 @@
     z = lax.axis_index(Z)
     zl = lax.axis_index("zl")
     column = lax.axis_index(PLANE)
+    place = lax.axis_index("x").astype(jnp.int32)[None]
 
     slab = lax.dynamic_slice_in_dim(parent_panel, column * 128, 128, 1)
-    swapped = swap(jnp.concatenate([slab, child_panel], axis=0), "zl", "x")
+    swapped = nearest(jnp.concatenate([slab, child_panel], axis=0))
 
     ancestor_keep = block_keep(ancestor_pattern, z * 352, 352, 5632)
     column_keep = block_keep(ancestor_pattern, column * 176, 176, 5632)
@@ -159,8 +165,14 @@
     (inner,) = call(
         panel_kernel,
         [jax.ShapeDtypeStruct((4, 256, 128), BF)],
-        [image_wide, blocks],
+        [place, image_wide, blocks],
         2 * 1408 * 256 * 512,
+    )
+    (beside,) = call(
+        panel_kernel,
+        [jax.ShapeDtypeStruct((4, 352, 128), BF)],
+        [place, cov_wide, after(blocks, inner)],
+        2 * 1408 * 352 * 512,
     )
     inner = jnp.sum(exchange(inner, "x").astype(F32), axis=0)
     parent_diag = (parent_inverse.astype(F32) + inner).astype(BF)
@@ -168,10 +180,10 @@
     diag_wide = parent_diag * child_column_keep[None, :].astype(BF)
     diag_wide = lax.all_gather(diag_wide, ("y", "c"), axis=0)
     (product,) = call(
-        products_kernel,
+        child_kernel,
         [jax.ShapeDtypeStruct((4, 608, 128), BF)],
-        [cov_wide, diag_wide, blocks],
-        2 * (1408 * 352 + 1024 * 256) * 512,
+        [place, diag_wide, beside, blocks],
+        2 * 1024 * 256 * 512,
     )
     product = -jnp.sum(exchange(product, "x").astype(F32), axis=0)
     ancestor_block = (product[:352] * ancestor_keep[:, None].astype(F32)).astype(BF)

time: 209 us -> 208 us (level)
  waiting for transfers between devices: 51.7 us -> 46.2 us
  starting transfers between devices: 42.5 us -> 45.3 us
    ppermute x2 -> x1, waiting for transfers between devices: 3.94 us -> 0.01 us  [swap(): return lax.ppermute(value, (first, second), pairs)]
    ppermute x4, starting transfers between devices: 18.7 us -> 22.6 us  [shift(): return lax.ppermute(value, Z, [(i, (i + by) % 16) for i in range(16)])]
    ppermute x0 -> x1, starting transfers between devices: none -> 2.94 us  [nearest(): return lax.ppermute(value, ('zh', 'zl', 'x'), pairs)]
    ppermute x2 -> x1, starting transfers between devices: 3.6 us -> 0.66 us  [swap(): return lax.ppermute(value, (first, second), pairs)]
    all_to_all x4, waiting for transfers between devices: 25.9 us -> 23.5 us  [exchange(): return lax.all_to_all(value, axis, split_axis=0, concat_axis=0, tiled=True)]
    pallas_call x4 -> x5, Pallas kernels: 6.39 us -> 6.58 us  [call(): pl.pallas_call(kernel, out_shape=outs, in_specs=specs, out_specs=[VMEM] *...]
  transfers between devices with their start and end apart: 12 -> 12, of which waited for: 8 -> 7; matrix products, arithmetic and copies ran while one was open for 3% -> 3% of each run, Pallas kernels for 2% -> 2%
where the time goes in v4:
time: 208 us; the launch traced here: 207 us
  blocking collectives  78.6 us (38%)
  waiting for transfers between devices  46.2 us (22%)
  starting transfers between devices  45.3 us (22%)
  between operations  14.4 us (7%)
  local copies, waits for them, and re-layouts  8.59 us (4%)
  other arithmetic  6.99 us (3%)
  Pallas kernels  6.58 us (3%)
    all_gather x1, blocking collectives, per_device(): cov_wide = lax.all_gather(after(cov, image), ('y', 'c'), axis=0, tiled=True)  27.1 us
    all_to_all x4, waiting for transfers between devices, exchange(): return lax.all_to_all(value, axis, split_axis=0, concat_axis=0, tiled=True)  23.5 us
    ppermute x4, starting transfers between devices, shift(): return lax.ppermute(value, Z, [(i, (i + by) % 16) for i in range(16)])  22.6 us
    all_gather x1, blocking collectives, per_device(): child_wide = lax.all_gather(parent_child, 'zh', axis=0)  19.7 us
    all_to_all x4, starting transfers between devices, exchange(): return lax.all_to_all(value, axis, split_axis=0, concat_axis=0, tiled=True)  19.1 us
    all_gather x1, blocking collectives, per_device(): image_wide = lax.all_gather(image, ('y', 'c'), axis=0, tiled=True)  17.6 us
    all_gather x1, blocking collectives, per_device(): diag_wide = lax.all_gather(diag_wide, ('y', 'c'), axis=0)  14.2 us
    all_gather x1, waiting for transfers between devices, per_device(): blocks = lax.all_gather(after(swapped, own), Z, axis=0)  12.9 us
  transfers between devices with their start and end apart: 12, of which 7 were waited for; matrix products, arithmetic and copies ran while one was open for 3% of the time, Pallas kernels for 2%

profile of v4, /device:TPU:32, one launch (start us, length us, event | category | flops | bytes accessed | tf_op | source)
XLA Modules:
  0.0 206.6 jit_solution(1983318692858133809)
XLA Ops:
  7.2 0.9 constant_dynamic-slice_fusion
  9.0 2.9 %collective-permute-start.4 = (bf16[608,128]{1,0:T(8,128)(2,1)S(1)}, bf16[608,128]{1,0:T(8,128)(2,1)S(1)}, u32[]{:S(2)}, u32[]{:S(2)}) collective-permute-start(bf16[608,128]{1,0:T(8,128)(2,1)S(1)} %pad_maximum_fusion), channel_id=1, source_target_pairs={{0,0},{2,32},{4,64},{6,480},{32,2},{34,34},{36,66},{38,98},{64,132... | collective-permute-start | bytes 466952 | tf_op jit(solution)/shard_map/ppermute | solution.py:109
  13.5 1.0 multiply_bitcast_fusion.at_ref
  14.6 1.8 copy-done.3
  16.4 1.5 shard_map.102
  18.6 9.7 %collective-permute-start = (bf16[4,176,256]{2,1,0:T(8,128)(2,1)S(1)}, bf16[4,176,256]{2,1,0:T(8,128)(2,1)S(1)}, u32[]{:S(2)}, u32[]{:S(2)}) collective-permute-start(bf16[4,176,256]{2,1,0:T(8,128)(2,1)S(1)} %get-tuple-element.15), channel_id=1, source_target_pairs={{0,32},{32,64},{64,96},{96,128},{128,160},{160,192},{192,224},{224... | collective-permute-start | bytes 1081352 | tf_op jit(solution)/shard_map/ppermute | solution.py:95
  28.4 1.9 collective-permute-start.1
  30.3 4.2 %collective-permute-start.2 = (bf16[2,176,256]{2,1,0:T(8,128)(2,1)S(1)}, bf16[2,176,256]{2,1,0:T(8,128)(2,1)S(1)}, u32[]{:S(2)}, u32[]{:S(2)}) collective-permute-start(bf16[2,176,256]{2,1,0:T(8,128)(2,1)S(1)} %get-tuple-element.26), channel_id=1, source_target_pairs={{0,64},{32,96},{64,128},{96,160},{128,192},{160,224},{192,256},{22... | collective-permute-start | bytes 540680 | tf_op jit(solution)/shard_map/ppermute | solution.py:95
  34.6 6.7 %collective-permute-start.3 = (bf16[2,176,256]{2,1,0:T(8,128)(2,1)S(1)}, bf16[2,176,256]{2,1,0:T(8,128)(2,1)S(1)}, u32[]{:S(2)}, u32[]{:S(2)}) collective-permute-start(bf16[2,176,256]{2,1,0:T(8,128)(2,1)S(1)} %get-tuple-element.27), channel_id=1, source_target_pairs={{0,448},{32,480},{64,0},{96,32},{128,64},{160,96},{192,128},{224,1... | collective-permute-start | bytes 540680 | tf_op jit(solution)/shard_map/ppermute | solution.py:95
  41.3 4.2 %collective-permute-done.2 = bf16[2,176,256]{2,1,0:T(8,128)(2,1)S(1)} collective-permute-done((bf16[2,176,256]{2,1,0:T(8,128)(2,1)S(1)}, bf16[2,176,256]{2,1,0:T(8,128)(2,1)S(1)}, u32[]{:S(2)}, u32[]{:S(2)}) %collective-permute-start.2) | collective-permute-done | bytes 180256 | tf_op jit(solution)/shard_map/ppermute | solution.py:95
  45.5 5.5 %collective-permute-done.3 = bf16[2,176,256]{2,1,0:T(8,128)(2,1)S(1)} collective-permute-done((bf16[2,176,256]{2,1,0:T(8,128)(2,1)S(1)}, bf16[2,176,256]{2,1,0:T(8,128)(2,1)S(1)}, u32[]{:S(2)}, u32[]{:S(2)}) %collective-permute-start.3) | collective-permute-done | bytes 180256 | tf_op jit(solution)/shard_map/ppermute | solution.py:95
  51.1 0.9 add_convert_fusion
  52.0 5.8 %all-to-all-start = ((bf16[4,176,256]{2,1,0:T(8,128)(2,1)}), bf16[4,176,256]{2,1,0:T(8,128)(2,1)S(1)}, u32[]{:S(2)}, u32[]{:S(2)}) async-start(bf16[4,176,256]{2,1,0:T(8,128)(2,1)} %add_convert_fusion), calls=%async_computation | async-start | bytes 720896 | tf_op jit(solution)/shard_map/all_to_all | solution.py:113
  58.5 27.1 %all_gather.30.left_ref = bf16[1408,352]{1,0:T(8,128)(2,1)} all-gather(bf16[176,352]{1,0:T(8,128)(2,1)S(1)} %multiply_bitcast_fusion.at_ref), channel_id=1, replica_groups=mesh['zh'=4,'zl'=4,'y'=4,'x'=4,'c'=2] {'y','c'}, dimensions={0}, use_global_device_ids=true | all-gather | bytes 1115136 | tf_op jit(solution)/shard_map/all_gather | solution.py:159
  85.5 2.5 %all-to-all-done = bf16[4,176,256]{2,1,0:T(8,128)(2,1)S(1)} async-done(((bf16[4,176,256]{2,1,0:T(8,128)(2,1)}), bf16[4,176,256]{2,1,0:T(8,128)(2,1)S(1)}, u32[]{:S(2)}, u32[]{:S(2)}) %all-to-all-start) | async-done | bytes 360480 | tf_op jit(solution)/shard_map/all_to_all | solution.py:113
  88.7 17.6 %all_gather.31.left_ref = bf16[1408,256]{1,0:T(8,128)(2,1)S(1)} all-gather(bf16[176,256]{1,0:T(8,128)(2,1)S(1)} %reduce_sum.77), channel_id=1, replica_groups=mesh['zh'=4,'zl'=4,'y'=4,'x'=4,'c'=2] {'y','c'}, dimensions={0}, use_global_device_ids=true | all-gather | bytes 811008 | tf_op jit(solution)/shard_map/all_gather | solution.py:163
  106.3 12.9 %all-gather.7.cloned.1.call-done = bf16[9728,128]{1,0:T(8,128)(2,1)} async-done(((bf16[608,128]{1,0:T(8,128)(2,1)}), bf16[9728,128]{1,0:T(8,128)(2,1)}) %all-gather.7.cloned.1.call-update) | async-done | bytes 2490384 | tf_op jit(solution)/shard_map/all_gather | solution.py:152
  119.2 1.7 copy-done
  120.9 1.4 shard_map.103
  122.4 4.7 %all-to-all-start.1 = ((bf16[4,256,128]{2,1,0:T(8,128)(2,1)}), bf16[4,256,128]{2,1,0:T(8,128)(2,1)S(1)}, u32[]{:S(2)}, u32[]{:S(2)}) async-start(bf16[4,256,128]{2,1,0:T(8,128)(2,1)} %shard_map.103), calls=%async_computation.1 | async-start | bytes 524288 | tf_op jit(solution)/shard_map/all_to_all | solution.py:113
  127.2 1.2 copy-done.2
  128.4 0.9 shard_map.104.beside_ref
  129.4 4.4 %all-to-all-done.1 = bf16[4,256,128]{2,1,0:T(8,128)(2,1)S(1)} async-done(((bf16[4,256,128]{2,1,0:T(8,128)(2,1)}), bf16[4,256,128]{2,1,0:T(8,128)(2,1)S(1)}, u32[]{:S(2)}, u32[]{:S(2)}) %all-to-all-start.1) | async-done | bytes 262176 | tf_op jit(solution)/shard_map/all_to_all | solution.py:113
  134.5 14.2 %all-gather.1 = bf16[2048,128]{1,0:T(8,128)(2,1)S(1)} all-gather(bf16[256,128]{1,0:T(8,128)(2,1)S(1)} %get-tuple-element.24), channel_id=3, replica_groups=mesh['zh'=4,'zl'=4,'y'=4,'x'=4,'c'=2] {'y','c'}, dimensions={0}, use_global_device_ids=true | all-gather | bytes 589824 | tf_op jit(solution)/shard_map/all_gather | solution.py:181
  148.7 1.3 shard_map.105
  150.0 3.5 %all-to-all-start.2 = ((bf16[4,608,128]{2,1,0:T(8,128)(2,1)}), bf16[4,608,128]{2,1,0:T(8,128)(2,1)S(1)}, u32[]{:S(2)}, u32[]{:S(2)}) async-start(bf16[4,608,128]{2,1,0:T(8,128)(2,1)} %shard_map.105), calls=%async_computation.2 | async-start | bytes 1245184 | tf_op jit(solution)/shard_map/all_to_all | solution.py:113
  153.6 11.2 %all-to-all-done.2 = bf16[4,608,128]{2,1,0:T(8,128)(2,1)S(1)} async-done(((bf16[4,608,128]{2,1,0:T(8,128)(2,1)}), bf16[4,608,128]{2,1,0:T(8,128)(2,1)S(1)}, u32[]{:S(2)}, u32[]{:S(2)}) %all-to-all-start.2) | async-done | bytes 622624 | tf_op jit(solution)/shard_map/all_to_all | solution.py:113
  165.0 19.7 %all-gather.3 = bf16[1024,128]{1,0:T(8,128)(2,1)S(1)} all-gather(bf16[256,128]{1,0:T(8,128)(2,1)S(1)} %fusion.1), channel_id=5, replica_groups=mesh['zh'=4,'zl'=4,'y'=4,'x'=4,'c'=2] {'zh'}, dimensions={0}, use_global_device_ids=true | all-gather | bytes 327680 | tf_op jit(solution)/shard_map/all_gather | solution.py:192
  184.7 1.6 copy-done.4
  186.3 1.5 shard_map.106
  187.7 5.1 %all-to-all-start.3 = ((bf16[4,256,128]{2,1,0:T(8,128)(2,1)}), bf16[4,256,128]{2,1,0:T(8,128)(2,1)S(1)}, u32[]{:S(2)}, u32[]{:S(2)}) async-start(bf16[4,256,128]{2,1,0:T(8,128)(2,1)} %shard_map.106), calls=%async_computation.3 | async-start | bytes 524288 | tf_op jit(solution)/shard_map/all_to_all | solution.py:113
  193.6 5.5 %all-to-all-done.3 = bf16[4,256,128]{2,1,0:T(8,128)(2,1)S(1)} async-done(((bf16[4,256,128]{2,1,0:T(8,128)(2,1)}), bf16[4,256,128]{2,1,0:T(8,128)(2,1)S(1)}, u32[]{:S(2)}, u32[]{:S(2)}) %all-to-all-start.3) | async-done | bytes 262176 | tf_op jit(solution)/shard_map/all_to_all | solution.py:113
  (54 shorter events, 7.1 us)
Async XLA Ops:
  7.2 112.1 %all-gather.7.cloned.1.call-start = ((), (), s32[]{:S(2)}) async-start(), calls=%async_computation.4 | async-start | bytes 2646016 | tf_op jit(solution)/shard_map/all_gather | solution.py:152
  9.0 8.9 %collective-permute-start.4 = (bf16[608,128]{1,0:T(8,128)(2,1)S(1)}, bf16[608,128]{1,0:T(8,128)(2,1)S(1)}, u32[]{:S(2)}, u32[]{:S(2)}) collective-permute-start(bf16[608,128]{1,0:T(8,128)(2,1)S(1)} %pad_maximum_fusion), channel_id=1, source_target_pairs={{0,0},{2,32},{4,64},{6,480},{32,2},{34,34},{36,66},{38,98},{64,132... | collective-permute-start | bytes 466952 | tf_op jit(solution)/shard_map/ppermute | solution.py:109
  14.6 1.8 copy-start.3
  17.9 39.9 %copy-start.7 = (bf16[256,128]{1,0:T(8,128)(2,1)S(1)}, bf16[256,128]{1,0:T(8,128)(2,1)}, u32[]{:S(2)}) copy-start(bf16[256,128]{1,0:T(8,128)(2,1)} %param.12) | copy-start | bytes 196612
  17.9 0.7 copy-start.6
  18.6 32.4 %collective-permute-start = (bf16[4,176,256]{2,1,0:T(8,128)(2,1)S(1)}, bf16[4,176,256]{2,1,0:T(8,128)(2,1)S(1)}, u32[]{:S(2)}, u32[]{:S(2)}) collective-permute-start(bf16[4,176,256]{2,1,0:T(8,128)(2,1)S(1)} %get-tuple-element.15), channel_id=1, source_target_pairs={{0,32},{32,64},{64,96},{96,128},{128,160},{160,192},{192,224},{224... | collective-permute-start | bytes 1081352 | tf_op jit(solution)/shard_map/ppermute | solution.py:95
  28.4 22.7 %collective-permute-start.1 = (bf16[4,176,256]{2,1,0:T(8,128)(2,1)S(1)}, bf16[4,176,256]{2,1,0:T(8,128)(2,1)S(1)}, u32[]{:S(2)}, u32[]{:S(2)}) collective-permute-start(bf16[4,176,256]{2,1,0:T(8,128)(2,1)S(1)} %get-tuple-element.16), channel_id=1, source_target_pairs={{0,480},{32,0},{64,32},{96,64},{128,96},{160,128},{192,160},{224,1... | collective-permute-start | bytes 1081352 | tf_op jit(solution)/shard_map/ppermute | solution.py:95
  30.3 15.2 %collective-permute-start.2 = (bf16[2,176,256]{2,1,0:T(8,128)(2,1)S(1)}, bf16[2,176,256]{2,1,0:T(8,128)(2,1)S(1)}, u32[]{:S(2)}, u32[]{:S(2)}) collective-permute-start(bf16[2,176,256]{2,1,0:T(8,128)(2,1)S(1)} %get-tuple-element.26), channel_id=1, source_target_pairs={{0,64},{32,96},{64,128},{96,160},{128,192},{160,224},{192,256},{22... | collective-permute-start | bytes 540680 | tf_op jit(solution)/shard_map/ppermute | solution.py:95
  34.6 16.5 %collective-permute-start.3 = (bf16[2,176,256]{2,1,0:T(8,128)(2,1)S(1)}, bf16[2,176,256]{2,1,0:T(8,128)(2,1)S(1)}, u32[]{:S(2)}, u32[]{:S(2)}) collective-permute-start(bf16[2,176,256]{2,1,0:T(8,128)(2,1)S(1)} %get-tuple-element.27), channel_id=1, source_target_pairs={{0,448},{32,480},{64,0},{96,32},{128,64},{160,96},{192,128},{224,1... | collective-permute-start | bytes 540680 | tf_op jit(solution)/shard_map/ppermute | solution.py:95
  52.0 36.0 %all-to-all-start = ((bf16[4,176,256]{2,1,0:T(8,128)(2,1)}), bf16[4,176,256]{2,1,0:T(8,128)(2,1)S(1)}, u32[]{:S(2)}, u32[]{:S(2)}) async-start(bf16[4,176,256]{2,1,0:T(8,128)(2,1)} %add_convert_fusion), calls=%async_computation | async-start | bytes 720896 | tf_op jit(solution)/shard_map/all_to_all | solution.py:113
  57.8 126.9 %all-gather.9.cloned.1.call-start = ((), (), s32[]{:S(2)}) async-start(), calls=%async_computation.5 | async-start | bytes 2162688 | tf_op jit(solution)/shard_map/all_gather | solution.py:162
  57.8 30.3 %collective-permute-start.5 = (bf16[256,128]{1,0:T(8,128)(2,1)S(1)}, bf16[256,128]{1,0:T(8,128)(2,1)S(1)}, u32[]{:S(2)}, u32[]{:S(2)}) collective-permute-start(bf16[256,128]{1,0:T(8,128)(2,1)S(1)} %copy-done.7), channel_id=1, source_target_pairs={{0,0},{8,128},{16,256},{24,384},{128,8},{136,136},{144,264},{152,3... | collective-permute-start | bytes 196616 | tf_op jit(solution)/shard_map/ppermute | solution.py:100
  88.1 39.1 %copy-start.11 = (s32[16]{0:T(128)S(1)}, s32[16]{0:T(128)}, u32[]{:S(2)}) copy-start(s32[16]{0:T(128)} %param.11) | copy-start | bytes 196
  88.1 0.6 copy-start.9
  119.2 1.7 copy-start
  120.9 6.3 %copy-start.1 = (bf16[9728,128]{1,0:T(8,128)(2,1)S(1)}, bf16[9728,128]{1,0:T(8,128)(2,1)}, u32[]{:S(2)}) copy-start(bf16[9728,128]{1,0:T(8,128)(2,1)} %all-gather.7.cloned.1.call-done) | copy-start | bytes 7471108
  122.4 11.4 %copy-start.8 = (bf16[256,128]{1,0:T(8,128)(2,1)S(1)}, bf16[256,128]{1,0:T(8,128)(2,1)}, u32[]{:S(2)}) copy-start(bf16[256,128]{1,0:T(8,128)(2,1)} %param.10) | copy-start | bytes 196612
  122.4 11.4 %all-to-all-start.1 = ((bf16[4,256,128]{2,1,0:T(8,128)(2,1)}), bf16[4,256,128]{2,1,0:T(8,128)(2,1)S(1)}, u32[]{:S(2)}, u32[]{:S(2)}) async-start(bf16[4,256,128]{2,1,0:T(8,128)(2,1)} %shard_map.103), calls=%async_computation.1 | async-start | bytes 524288 | tf_op jit(solution)/shard_map/all_to_all | solution.py:113
  127.2 1.2 copy-start.2
  150.0 14.8 %all-to-all-start.2 = ((bf16[4,608,128]{2,1,0:T(8,128)(2,1)}), bf16[4,608,128]{2,1,0:T(8,128)(2,1)S(1)}, u32[]{:S(2)}, u32[]{:S(2)}) async-start(bf16[4,608,128]{2,1,0:T(8,128)(2,1)} %shard_map.105), calls=%async_computation.2 | async-start | bytes 1245184 | tf_op jit(solution)/shard_map/all_to_all | solution.py:113
  164.9 34.2 %copy-start.10 = (bf16[256,128]{1,0:T(8,128)(2,1)S(1)}, bf16[256,128]{1,0:T(8,128)(2,1)}, u32[]{:S(2)}) copy-start(bf16[256,128]{1,0:T(8,128)(2,1)} %param.13) | copy-start | bytes 196612
  165.0 34.7 %copy-start.5 = (bf16[256,128]{1,0:T(8,128)(2,1)}, bf16[256,128]{1,0:T(8,128)(2,1)S(1)}, u32[]{:S(2)}) copy-start(bf16[256,128]{1,0:T(8,128)(2,1)S(1)} %fusion.1) | copy-start | bytes 196612
  184.7 1.6 copy-start.4
  187.7 11.3 %all-to-all-start.3 = ((bf16[4,256,128]{2,1,0:T(8,128)(2,1)}), bf16[4,256,128]{2,1,0:T(8,128)(2,1)S(1)}, u32[]{:S(2)}, u32[]{:S(2)}) async-start(bf16[4,256,128]{2,1,0:T(8,128)(2,1)} %shard_map.106), calls=%async_computation.3 | async-start | bytes 524288 | tf_op jit(solution)/shard_map/all_to_all | solution.py:113
Sparse Core Ops, SparseCore 0:
  18.7 100.4 all-gather.6
  122.9 57.1 all-gather.8

commit v5 on v4

--- a/solution.py
+++ b/solution.py
@@ -155,12 +155,12 @@
     image = own + right.astype(F32) + left.astype(F32) + far.astype(F32)
     image = image.astype(BF)
 
-    factor = swap(after(child_panel, image), "zh", "y")
     cov_wide = lax.all_gather(after(cov, image), ("y", "c"), axis=0, tiled=True)
     image = after(exchange(image, "zh"), cov_wide)
     image = jnp.sum(image.astype(F32), axis=0).astype(BF)
-    factor = lax.all_gather(after(factor, image), PLANE, axis=0)
+    factor = swap(after(child_panel, image), "zh", "y")
     image_wide = lax.all_gather(image, ("y", "c"), axis=0, tiled=True)
+    factor = lax.all_gather(after(factor, image_wide), PLANE, axis=0)
 
     (inner,) = call(
         panel_kernel,

time: 208 us -> 204 us (0.981)
  blocking collectives: 78.6 us -> 65 us
  waiting for transfers between devices: 46.2 us -> 55.8 us
    all_gather x1, blocking collectives: 27.1 us -> 15 us  [per_device(): cov_wide = lax.all_gather(after(cov, image), ('y', 'c'), axis=0, tiled=True)]
    all_to_all x4, waiting for transfers between devices: 23.5 us -> 34.9 us  [exchange(): return lax.all_to_all(value, axis, split_axis=0, concat_axis=0, tiled=True)]
    all_gather x1, blocking collectives: 17.6 us -> 15.3 us  [per_device(): image_wide = lax.all_gather(image, ('y', 'c'), axis=0, tiled=True)]
  transfers between devices with their start and end apart: 12 -> 12, of which waited for: 7 -> 7; matrix products, arithmetic and copies ran while one was open for 3% -> 3% of each run, Pallas kernels for 2% -> 3%
where the time goes in v5:
time: 204 us; the launch traced here: 203 us
  blocking collectives  65 us (32%)
  waiting for transfers between devices  55.8 us (27%)
  starting transfers between devices  45.6 us (22%)
  between operations  14.3 us (7%)
  local copies, waits for them, and re-layouts  8.59 us (4%)
  other arithmetic  6.99 us (3%)
  Pallas kernels  6.59 us (3%)
    all_to_all x4, waiting for transfers between devices, exchange(): return lax.all_to_all(value, axis, split_axis=0, concat_axis=0, tiled=True)  34.9 us
    ppermute x4, starting transfers between devices, shift(): return lax.ppermute(value, Z, [(i, (i + by) % 16) for i in range(16)])  22.6 us
    all_to_all x4, starting transfers between devices, exchange(): return lax.all_to_all(value, axis, split_axis=0, concat_axis=0, tiled=True)  19.3 us
    all_gather x1, blocking collectives, per_device(): child_wide = lax.all_gather(parent_child, 'zh', axis=0)  18.8 us
    all_gather x1, blocking collectives, per_device(): diag_wide = lax.all_gather(diag_wide, ('y', 'c'), axis=0)  15.9 us
    all_gather x1, blocking collectives, per_device(): image_wide = lax.all_gather(image, ('y', 'c'), axis=0, tiled=True)  15.3 us
    all_gather x1, blocking collectives, per_device(): cov_wide = lax.all_gather(after(cov, image), ('y', 'c'), axis=0, tiled=True)  15 us
    all_gather x1, waiting for transfers between devices, per_device(): blocks = lax.all_gather(after(swapped, own), Z, axis=0)  11.1 us
  transfers between devices with their start and end apart: 12, of which 7 were waited for; matrix products, arithmetic and copies ran while one was open for 3% of the time, Pallas kernels for 3%

profile of v5, /device:TPU:32, one launch (start us, length us, event | category | flops | bytes accessed | tf_op | source)
XLA Modules:
  0.0 202.8 jit_solution(17052183230570075257)
XLA Ops:
  7.2 0.9 constant_dynamic-slice_fusion
  9.0 2.9 %collective-permute-start.4 = (bf16[608,128]{1,0:T(8,128)(2,1)S(1)}, bf16[608,128]{1,0:T(8,128)(2,1)S(1)}, u32[]{:S(2)}, u32[]{:S(2)}) collective-permute-start(bf16[608,128]{1,0:T(8,128)(2,1)S(1)} %pad_maximum_fusion), channel_id=1, source_target_pairs={{0,0},{2,32},{4,64},{6,480},{32,2},{34,34},{36,66},{38,98},{64,132... | collective-permute-start | bytes 466952 | tf_op jit(solution)/shard_map/ppermute | solution.py:109
  13.5 1.0 multiply_bitcast_fusion.at_ref
  14.6 1.8 copy-done.3
  16.4 1.5 shard_map.102
  18.6 9.7 %collective-permute-start = (bf16[4,176,256]{2,1,0:T(8,128)(2,1)S(1)}, bf16[4,176,256]{2,1,0:T(8,128)(2,1)S(1)}, u32[]{:S(2)}, u32[]{:S(2)}) collective-permute-start(bf16[4,176,256]{2,1,0:T(8,128)(2,1)S(1)} %get-tuple-element.15), channel_id=1, source_target_pairs={{0,32},{32,64},{64,96},{96,128},{128,160},{160,192},{192,224},{224... | collective-permute-start | bytes 1081352 | tf_op jit(solution)/shard_map/ppermute | solution.py:95
  28.3 1.9 collective-permute-start.1
  30.3 4.3 %collective-permute-start.2 = (bf16[2,176,256]{2,1,0:T(8,128)(2,1)S(1)}, bf16[2,176,256]{2,1,0:T(8,128)(2,1)S(1)}, u32[]{:S(2)}, u32[]{:S(2)}) collective-permute-start(bf16[2,176,256]{2,1,0:T(8,128)(2,1)S(1)} %get-tuple-element.26), channel_id=1, source_target_pairs={{0,64},{32,96},{64,128},{96,160},{128,192},{160,224},{192,256},{22... | collective-permute-start | bytes 540680 | tf_op jit(solution)/shard_map/ppermute | solution.py:95
  34.6 6.7 %collective-permute-start.3 = (bf16[2,176,256]{2,1,0:T(8,128)(2,1)S(1)}, bf16[2,176,256]{2,1,0:T(8,128)(2,1)S(1)}, u32[]{:S(2)}, u32[]{:S(2)}) collective-permute-start(bf16[2,176,256]{2,1,0:T(8,128)(2,1)S(1)} %get-tuple-element.27), channel_id=1, source_target_pairs={{0,448},{32,480},{64,0},{96,32},{128,64},{160,96},{192,128},{224,1... | collective-permute-start | bytes 540680 | tf_op jit(solution)/shard_map/ppermute | solution.py:95
  41.3 4.2 %collective-permute-done.2 = bf16[2,176,256]{2,1,0:T(8,128)(2,1)S(1)} collective-permute-done((bf16[2,176,256]{2,1,0:T(8,128)(2,1)S(1)}, bf16[2,176,256]{2,1,0:T(8,128)(2,1)S(1)}, u32[]{:S(2)}, u32[]{:S(2)}) %collective-permute-start.2) | collective-permute-done | bytes 180256 | tf_op jit(solution)/shard_map/ppermute | solution.py:95
  45.5 5.5 %collective-permute-done.3 = bf16[2,176,256]{2,1,0:T(8,128)(2,1)S(1)} collective-permute-done((bf16[2,176,256]{2,1,0:T(8,128)(2,1)S(1)}, bf16[2,176,256]{2,1,0:T(8,128)(2,1)S(1)}, u32[]{:S(2)}, u32[]{:S(2)}) %collective-permute-start.3) | collective-permute-done | bytes 180256 | tf_op jit(solution)/shard_map/ppermute | solution.py:95
  51.0 0.9 add_convert_fusion
  52.0 5.9 %all-to-all-start = ((bf16[4,176,256]{2,1,0:T(8,128)(2,1)}), bf16[4,176,256]{2,1,0:T(8,128)(2,1)S(1)}, u32[]{:S(2)}, u32[]{:S(2)}) async-start(bf16[4,176,256]{2,1,0:T(8,128)(2,1)} %add_convert_fusion), calls=%async_computation | async-start | bytes 720896 | tf_op jit(solution)/shard_map/all_to_all | solution.py:113
  57.8 15.0 %all_gather.30.left_ref = bf16[1408,352]{1,0:T(8,128)(2,1)} all-gather(bf16[176,352]{1,0:T(8,128)(2,1)S(1)} %multiply_bitcast_fusion.at_ref), channel_id=1, replica_groups=mesh['zh'=4,'zl'=4,'y'=4,'x'=4,'c'=2] {'y','c'}, dimensions={0}, use_global_device_ids=true | all-gather | bytes 1115136 | tf_op jit(solution)/shard_map/all_gather | solution.py:158
  72.9 13.9 %all-to-all-done = bf16[4,176,256]{2,1,0:T(8,128)(2,1)S(1)} async-done(((bf16[4,176,256]{2,1,0:T(8,128)(2,1)}), bf16[4,176,256]{2,1,0:T(8,128)(2,1)S(1)}, u32[]{:S(2)}, u32[]{:S(2)}) %all-to-all-start) | async-done | bytes 360480 | tf_op jit(solution)/shard_map/all_to_all | solution.py:113
  87.6 15.3 %all_gather.31.left_ref = bf16[1408,256]{1,0:T(8,128)(2,1)S(1)} all-gather(bf16[176,256]{1,0:T(8,128)(2,1)S(1)} %reduce_sum.77), channel_id=1, replica_groups=mesh['zh'=4,'zl'=4,'y'=4,'x'=4,'c'=2] {'y','c'}, dimensions={0}, use_global_device_ids=true | all-gather | bytes 811008 | tf_op jit(solution)/shard_map/all_gather | solution.py:162
  103.5 11.1 %all-gather.7.cloned.1.call-done = bf16[9728,128]{1,0:T(8,128)(2,1)} async-done(((bf16[608,128]{1,0:T(8,128)(2,1)}), bf16[9728,128]{1,0:T(8,128)(2,1)}) %all-gather.7.cloned.1.call-update) | async-done | bytes 2490384 | tf_op jit(solution)/shard_map/all_gather | solution.py:152
  114.6 1.7 copy-done
  116.3 1.4 shard_map.103
  117.7 4.8 %all-to-all-start.1 = ((bf16[4,256,128]{2,1,0:T(8,128)(2,1)}), bf16[4,256,128]{2,1,0:T(8,128)(2,1)S(1)}, u32[]{:S(2)}, u32[]{:S(2)}) async-start(bf16[4,256,128]{2,1,0:T(8,128)(2,1)} %shard_map.103), calls=%async_computation.1 | async-start | bytes 524288 | tf_op jit(solution)/shard_map/all_to_all | solution.py:113
  122.6 1.2 copy-done.2
  123.8 0.9 shard_map.104.beside_ref
  124.8 4.4 %all-to-all-done.1 = bf16[4,256,128]{2,1,0:T(8,128)(2,1)S(1)} async-done(((bf16[4,256,128]{2,1,0:T(8,128)(2,1)}), bf16[4,256,128]{2,1,0:T(8,128)(2,1)S(1)}, u32[]{:S(2)}, u32[]{:S(2)}) %all-to-all-start.1) | async-done | bytes 262176 | tf_op jit(solution)/shard_map/all_to_all | solution.py:113
  129.9 15.9 %all-gather.1 = bf16[2048,128]{1,0:T(8,128)(2,1)S(1)} all-gather(bf16[256,128]{1,0:T(8,128)(2,1)S(1)} %get-tuple-element.24), channel_id=3, replica_groups=mesh['zh'=4,'zl'=4,'y'=4,'x'=4,'c'=2] {'y','c'}, dimensions={0}, use_global_device_ids=true | all-gather | bytes 589824 | tf_op jit(solution)/shard_map/all_gather | solution.py:181
  145.7 1.3 shard_map.105
  147.0 3.5 %all-to-all-start.2 = ((bf16[4,608,128]{2,1,0:T(8,128)(2,1)}), bf16[4,608,128]{2,1,0:T(8,128)(2,1)S(1)}, u32[]{:S(2)}, u32[]{:S(2)}) async-start(bf16[4,608,128]{2,1,0:T(8,128)(2,1)} %shard_map.105), calls=%async_computation.2 | async-start | bytes 1245184 | tf_op jit(solution)/shard_map/all_to_all | solution.py:113
  150.6 11.2 %all-to-all-done.2 = bf16[4,608,128]{2,1,0:T(8,128)(2,1)S(1)} async-done(((bf16[4,608,128]{2,1,0:T(8,128)(2,1)}), bf16[4,608,128]{2,1,0:T(8,128)(2,1)S(1)}, u32[]{:S(2)}, u32[]{:S(2)}) %all-to-all-start.2) | async-done | bytes 622624 | tf_op jit(solution)/shard_map/all_to_all | solution.py:113
  162.1 18.8 %all-gather.3 = bf16[1024,128]{1,0:T(8,128)(2,1)S(1)} all-gather(bf16[256,128]{1,0:T(8,128)(2,1)S(1)} %fusion.1), channel_id=5, replica_groups=mesh['zh'=4,'zl'=4,'y'=4,'x'=4,'c'=2] {'zh'}, dimensions={0}, use_global_device_ids=true | all-gather | bytes 327680 | tf_op jit(solution)/shard_map/all_gather | solution.py:192
  180.8 1.6 copy-done.4
  182.4 1.5 shard_map.106
  183.9 5.2 %all-to-all-start.3 = ((bf16[4,256,128]{2,1,0:T(8,128)(2,1)}), bf16[4,256,128]{2,1,0:T(8,128)(2,1)S(1)}, u32[]{:S(2)}, u32[]{:S(2)}) async-start(bf16[4,256,128]{2,1,0:T(8,128)(2,1)} %shard_map.106), calls=%async_computation.3 | async-start | bytes 524288 | tf_op jit(solution)/shard_map/all_to_all | solution.py:113
  189.8 5.5 %all-to-all-done.3 = bf16[4,256,128]{2,1,0:T(8,128)(2,1)S(1)} async-done(((bf16[4,256,128]{2,1,0:T(8,128)(2,1)}), bf16[4,256,128]{2,1,0:T(8,128)(2,1)S(1)}, u32[]{:S(2)}, u32[]{:S(2)}) %all-to-all-start.3) | async-done | bytes 262176 | tf_op jit(solution)/shard_map/all_to_all | solution.py:113
  (54 shorter events, 7.2 us)
Async XLA Ops:
  7.2 107.4 %all-gather.7.cloned.1.call-start = ((), (), s32[]{:S(2)}) async-start(), calls=%async_computation.4 | async-start | bytes 2646016 | tf_op jit(solution)/shard_map/all_gather | solution.py:152
  9.0 8.9 %collective-permute-start.4 = (bf16[608,128]{1,0:T(8,128)(2,1)S(1)}, bf16[608,128]{1,0:T(8,128)(2,1)S(1)}, u32[]{:S(2)}, u32[]{:S(2)}) collective-permute-start(bf16[608,128]{1,0:T(8,128)(2,1)S(1)} %pad_maximum_fusion), channel_id=1, source_target_pairs={{0,0},{2,32},{4,64},{6,480},{32,2},{34,34},{36,66},{38,98},{64,132... | collective-permute-start | bytes 466952 | tf_op jit(solution)/shard_map/ppermute | solution.py:109
  14.6 1.8 copy-start.3
  17.9 0.7 copy-start.6
  18.6 32.4 %collective-permute-start = (bf16[4,176,256]{2,1,0:T(8,128)(2,1)S(1)}, bf16[4,176,256]{2,1,0:T(8,128)(2,1)S(1)}, u32[]{:S(2)}, u32[]{:S(2)}) collective-permute-start(bf16[4,176,256]{2,1,0:T(8,128)(2,1)S(1)} %get-tuple-element.15), channel_id=1, source_target_pairs={{0,32},{32,64},{64,96},{96,128},{128,160},{160,192},{192,224},{224... | collective-permute-start | bytes 1081352 | tf_op jit(solution)/shard_map/ppermute | solution.py:95
  28.3 22.7 %collective-permute-start.1 = (bf16[4,176,256]{2,1,0:T(8,128)(2,1)S(1)}, bf16[4,176,256]{2,1,0:T(8,128)(2,1)S(1)}, u32[]{:S(2)}, u32[]{:S(2)}) collective-permute-start(bf16[4,176,256]{2,1,0:T(8,128)(2,1)S(1)} %get-tuple-element.16), channel_id=1, source_target_pairs={{0,480},{32,0},{64,32},{96,64},{128,96},{160,128},{192,160},{224,1... | collective-permute-start | bytes 1081352 | tf_op jit(solution)/shard_map/ppermute | solution.py:95
  30.3 56.6 %copy-start.7 = (bf16[256,128]{1,0:T(8,128)(2,1)S(1)}, bf16[256,128]{1,0:T(8,128)(2,1)}, u32[]{:S(2)}) copy-start(bf16[256,128]{1,0:T(8,128)(2,1)} %param.12) | copy-start | bytes 196612
  30.3 15.2 %collective-permute-start.2 = (bf16[2,176,256]{2,1,0:T(8,128)(2,1)S(1)}, bf16[2,176,256]{2,1,0:T(8,128)(2,1)S(1)}, u32[]{:S(2)}, u32[]{:S(2)}) collective-permute-start(bf16[2,176,256]{2,1,0:T(8,128)(2,1)S(1)} %get-tuple-element.26), channel_id=1, source_target_pairs={{0,64},{32,96},{64,128},{96,160},{128,192},{160,224},{192,256},{22... | collective-permute-start | bytes 540680 | tf_op jit(solution)/shard_map/ppermute | solution.py:95
  34.6 16.4 %collective-permute-start.3 = (bf16[2,176,256]{2,1,0:T(8,128)(2,1)S(1)}, bf16[2,176,256]{2,1,0:T(8,128)(2,1)S(1)}, u32[]{:S(2)}, u32[]{:S(2)}) collective-permute-start(bf16[2,176,256]{2,1,0:T(8,128)(2,1)S(1)} %get-tuple-element.27), channel_id=1, source_target_pairs={{0,448},{32,480},{64,0},{96,32},{128,64},{160,96},{192,128},{224,1... | collective-permute-start | bytes 540680 | tf_op jit(solution)/shard_map/ppermute | solution.py:95
  52.0 34.8 %all-to-all-start = ((bf16[4,176,256]{2,1,0:T(8,128)(2,1)}), bf16[4,176,256]{2,1,0:T(8,128)(2,1)S(1)}, u32[]{:S(2)}, u32[]{:S(2)}) async-start(bf16[4,176,256]{2,1,0:T(8,128)(2,1)} %add_convert_fusion), calls=%async_computation | async-start | bytes 720896 | tf_op jit(solution)/shard_map/all_to_all | solution.py:113
  57.8 123.0 %all-gather.9.cloned.1.call-start = ((), (), s32[]{:S(2)}) async-start(), calls=%async_computation.5 | async-start | bytes 2162688 | tf_op jit(solution)/shard_map/all_gather | solution.py:163
  86.9 35.6 %copy-start.11 = (s32[16]{0:T(128)S(1)}, s32[16]{0:T(128)}, u32[]{:S(2)}) copy-start(s32[16]{0:T(128)} %param.11) | copy-start | bytes 196
  86.9 16.0 %collective-permute-start.5 = (bf16[256,128]{1,0:T(8,128)(2,1)S(1)}, bf16[256,128]{1,0:T(8,128)(2,1)S(1)}, u32[]{:S(2)}, u32[]{:S(2)}) collective-permute-start(bf16[256,128]{1,0:T(8,128)(2,1)S(1)} %copy-done.7), channel_id=1, source_target_pairs={{0,0},{8,128},{16,256},{24,384},{128,8},{136,136},{144,264},{152,3... | collective-permute-start | bytes 196616 | tf_op jit(solution)/shard_map/ppermute | solution.py:100
  102.9 0.6 copy-start.9
  114.6 1.7 copy-start
  116.3 6.3 %copy-start.1 = (bf16[9728,128]{1,0:T(8,128)(2,1)S(1)}, bf16[9728,128]{1,0:T(8,128)(2,1)}, u32[]{:S(2)}) copy-start(bf16[9728,128]{1,0:T(8,128)(2,1)} %all-gather.7.cloned.1.call-done) | copy-start | bytes 7471108
  117.7 11.5 %copy-start.8 = (bf16[256,128]{1,0:T(8,128)(2,1)S(1)}, bf16[256,128]{1,0:T(8,128)(2,1)}, u32[]{:S(2)}) copy-start(bf16[256,128]{1,0:T(8,128)(2,1)} %param.10) | copy-start | bytes 196612
  117.7 11.4 %all-to-all-start.1 = ((bf16[4,256,128]{2,1,0:T(8,128)(2,1)}), bf16[4,256,128]{2,1,0:T(8,128)(2,1)S(1)}, u32[]{:S(2)}, u32[]{:S(2)}) async-start(bf16[4,256,128]{2,1,0:T(8,128)(2,1)} %shard_map.103), calls=%async_computation.1 | async-start | bytes 524288 | tf_op jit(solution)/shard_map/all_to_all | solution.py:113
  122.6 1.2 copy-start.2
  147.0 14.8 %all-to-all-start.2 = ((bf16[4,608,128]{2,1,0:T(8,128)(2,1)}), bf16[4,608,128]{2,1,0:T(8,128)(2,1)S(1)}, u32[]{:S(2)}, u32[]{:S(2)}) async-start(bf16[4,608,128]{2,1,0:T(8,128)(2,1)} %shard_map.105), calls=%async_computation.2 | async-start | bytes 1245184 | tf_op jit(solution)/shard_map/all_to_all | solution.py:113
  161.9 33.5 %copy-start.10 = (bf16[256,128]{1,0:T(8,128)(2,1)S(1)}, bf16[256,128]{1,0:T(8,128)(2,1)}, u32[]{:S(2)}) copy-start(bf16[256,128]{1,0:T(8,128)(2,1)} %param.13) | copy-start | bytes 196612
  162.0 34.0 %copy-start.5 = (bf16[256,128]{1,0:T(8,128)(2,1)}, bf16[256,128]{1,0:T(8,128)(2,1)S(1)}, u32[]{:S(2)}) copy-start(bf16[256,128]{1,0:T(8,128)(2,1)S(1)} %fusion.1) | copy-start | bytes 196612
  180.8 1.6 copy-start.4
  183.9 11.4 %all-to-all-start.3 = ((bf16[4,256,128]{2,1,0:T(8,128)(2,1)}), bf16[4,256,128]{2,1,0:T(8,128)(2,1)S(1)}, u32[]{:S(2)}, u32[]{:S(2)}) async-start(bf16[4,256,128]{2,1,0:T(8,128)(2,1)} %shard_map.106), calls=%async_computation.3 | async-start | bytes 524288 | tf_op jit(solution)/shard_map/all_to_all | solution.py:113
Sparse Core Ops, SparseCore 0:
  18.7 95.7 all-gather.6
  118.3 59.7 all-gather.8

commit v6 on v5

--- a/solution.py
+++ b/solution.py
@@ -65,7 +65,23 @@
         out_ref[n] = total[:, n * 128 : (n + 1) * 128].astype(out_ref.dtype)
 
 
-def child_kernel(x_ref, left_ref, beside_ref, blocks_ref, out_ref):
+def beside_kernel(x_ref, left_ref, blocks_ref, *outs):
+    bands = [lax.rem(x_ref[0] + d, 4) for d in range(4)]
+    total = None
+    for h in range(4):
+        blocks = [blocks_ref[block_of(x_ref[0], h, n), 0:352, :] for n in bands]
+        part = lax.dot_general(
+            left_ref[h * 352 : (h + 1) * 352, :],
+            jnp.concatenate(blocks, axis=1),
+            (((0,), (0,)), ((), ())),
+            preferred_element_type=F32,
+        )
+        total = part if total is None else total + part
+    for n, out in enumerate(outs):
+        out[...] = total[:, n * 128 : (n + 1) * 128].astype(out.dtype)
+
+
+def child_kernel(x_ref, left_ref, blocks_ref, out_ref):
     total = None
     for h in range(4):
         blocks = [blocks_ref[block_of(x_ref[0], h, n), 352:608, :] for n in range(4)]
@@ -73,9 +89,7 @@
         part = jnp.dot(left, jnp.concatenate(blocks, axis=1), preferred_element_type=F32)
         total = part if total is None else total + part
     for n in range(4):
-        out_ref[n, 0:352, :] = beside_ref[n]
-        tile = total[:, n * 128 : (n + 1) * 128].astype(out_ref.dtype)
-        out_ref[n, 352:608, :] = tile
+        out_ref[n] = total[:, n * 128 : (n + 1) * 128].astype(out_ref.dtype)
 
 
 def last_kernel(factor_ref, image_ref, out_ref):
@@ -93,6 +107,10 @@
 
 def shift(value, by):
     return lax.ppermute(value, Z, [(i, (i + by) % 16) for i in range(16)])
+
+
+def along_x(value, by):
+    return lax.ppermute(value, "x", [(i, (i + by) % 4) for i in range(4)])
 
 
 def swap(value, first, second):
@@ -168,35 +186,38 @@
         [place, image_wide, blocks],
         2 * 1408 * 256 * 512,
     )
-    (beside,) = call(
-        panel_kernel,
-        [jax.ShapeDtypeStruct((4, 352, 128), BF)],
+    part = jax.ShapeDtypeStruct((352, 128), BF)
+    besides = call(
+        beside_kernel,
+        [jax.ShapeDtypeStruct((352, 128), F32), part, part, part],
         [place, cov_wide, after(blocks, inner)],
         2 * 1408 * 352 * 512,
     )
-    inner = jnp.sum(exchange(inner, "x").astype(F32), axis=0)
+    inner = jnp.sum(after(exchange(inner, "x"), besides[0]).astype(F32), axis=0)
     parent_diag = (parent_inverse.astype(F32) + inner).astype(BF)
 
     diag_wide = parent_diag * child_column_keep[None, :].astype(BF)
     diag_wide = lax.all_gather(diag_wide, ("y", "c"), axis=0)
     (product,) = call(
         child_kernel,
-        [jax.ShapeDtypeStruct((4, 608, 128), BF)],
-        [place, diag_wide, beside, blocks],
+        [jax.ShapeDtypeStruct((4, 256, 128), BF)],
+        [place, diag_wide, blocks],
         2 * 1024 * 256 * 512,
     )
-    product = -jnp.sum(exchange(product, "x").astype(F32), axis=0)
-    ancestor_block = (product[:352] * ancestor_keep[:, None].astype(F32)).astype(BF)
-    parent_child = (product[352:] * child_keep[:, None].astype(F32)).astype(BF)
+    moved = [along_x(after(besides[d], product), d) for d in range(1, 4)]
+    product = jnp.sum(exchange(product, "x").astype(F32), axis=0)
+    parent_child = (-product * child_keep[:, None].astype(F32)).astype(BF)
 
     child_wide = lax.all_gather(parent_child, "zh", axis=0)
     (inner,) = call(
         last_kernel,
         [jax.ShapeDtypeStruct((4, 256, 128), BF)],
-        [factor, child_wide],
+        [factor, after(child_wide, *moved)],
         2 * 1024 * 1024 * 128,
     )
     inner = jnp.sum(exchange(inner, "zl").astype(F32), axis=0)
+    product = besides[0] + sum(block.astype(F32) for block in moved)
+    ancestor_block = (-product * ancestor_keep[:, None].astype(F32)).astype(BF)
     child_diag = (child_inverse.astype(F32) - inner).astype(BF)
     return (ancestor_block, parent_diag, parent_child, child_diag)
 

time: 204 us -> 206 us (level)
  starting transfers between devices: 45.6 us -> 58.6 us
  waiting for transfers between devices: 55.8 us -> 43.8 us
    all_to_all x4, waiting for transfers between devices: 34.9 us -> 23 us  [exchange(): return lax.all_to_all(value, axis, split_axis=0, concat_axis=0, tiled=True)]
    ppermute x0 -> x3, starting transfers between devices: none -> 11.8 us  [along_x(): return lax.ppermute(value, 'x', [(i, (i + by) % 4) for i in range(4)])]
    unnamed x24 -> x22, local copies, waits for them, and re-layouts: 7.66 us -> 7.65 us
  transfers between devices with their start and end apart: 12 -> 15, of which waited for: 7 -> 6; matrix products, arithmetic and copies ran while one was open for 3% -> 3% of each run, Pallas kernels for 3% -> 2%
where the time goes in v6:
time: 206 us; the launch traced here: 205 us
  blocking collectives  65.1 us (32%)
  starting transfers between devices  58.6 us (28%)
  waiting for transfers between devices  43.8 us (21%)
  between operations  14.4 us (7%)
  local copies, waits for them, and re-layouts  8.58 us (4%)
  other arithmetic  7.66 us (4%)
  Pallas kernels  6.46 us (3%)
    all_to_all x4, waiting for transfers between devices, exchange(): return lax.all_to_all(value, axis, split_axis=0, concat_axis=0, tiled=True)  23 us
    ppermute x4, starting transfers between devices, shift(): return lax.ppermute(value, Z, [(i, (i + by) % 16) for i in range(16)])  22.6 us
    all_to_all x4, starting transfers between devices, exchange(): return lax.all_to_all(value, axis, split_axis=0, concat_axis=0, tiled=True)  20.5 us
    all_gather x1, blocking collectives, per_device(): child_wide = lax.all_gather(parent_child, 'zh', axis=0)  18.9 us
    all_gather x1, blocking collectives, per_device(): diag_wide = lax.all_gather(diag_wide, ('y', 'c'), axis=0)  15.9 us
    all_gather x1, blocking collectives, per_device(): image_wide = lax.all_gather(image, ('y', 'c'), axis=0, tiled=True)  15.3 us
    all_gather x1, blocking collectives, per_device(): cov_wide = lax.all_gather(after(cov, image), ('y', 'c'), axis=0, tiled=True)  15 us
    ppermute x3, starting transfers between devices, along_x(): return lax.ppermute(value, 'x', [(i, (i + by) % 4) for i in range(4)])  11.8 us
  transfers between devices with their start and end apart: 15, of which 6 were waited for; matrix products, arithmetic and copies ran while one was open for 3% of the time, Pallas kernels for 2%

profile of v6, /device:TPU:32, one launch (start us, length us, event | category | flops | bytes accessed | tf_op | source)
XLA Modules:
  0.0 204.6 jit_solution(5694513354486935569)
XLA Ops:
  9.0 2.9 %collective-permute-start.4 = (bf16[608,128]{1,0:T(8,128)(2,1)S(1)}, bf16[608,128]{1,0:T(8,128)(2,1)S(1)}, u32[]{:S(2)}, u32[]{:S(2)}) collective-permute-start(bf16[608,128]{1,0:T(8,128)(2,1)S(1)} %pad_maximum_fusion), channel_id=1, source_target_pairs={{0,0},{2,32},{4,64},{6,480},{32,2},{34,34},{36,66},{38,98},{64,132... | collective-permute-start | bytes 466952 | tf_op jit(solution)/shard_map/ppermute | solution.py:127
  13.5 1.0 multiply_bitcast_fusion.at_ref
  14.6 1.8 copy-done.3
  16.4 1.5 shard_map.102
  18.6 9.7 %collective-permute-start = (bf16[4,176,256]{2,1,0:T(8,128)(2,1)S(1)}, bf16[4,176,256]{2,1,0:T(8,128)(2,1)S(1)}, u32[]{:S(2)}, u32[]{:S(2)}) collective-permute-start(bf16[4,176,256]{2,1,0:T(8,128)(2,1)S(1)} %get-tuple-element.24), channel_id=1, source_target_pairs={{0,32},{32,64},{64,96},{96,128},{128,160},{160,192},{192,224},{224... | collective-permute-start | bytes 1081352 | tf_op jit(solution)/shard_map/ppermute | solution.py:109
  28.4 1.9 collective-permute-start.1
  30.3 4.3 %collective-permute-start.2 = (bf16[2,176,256]{2,1,0:T(8,128)(2,1)S(1)}, bf16[2,176,256]{2,1,0:T(8,128)(2,1)S(1)}, u32[]{:S(2)}, u32[]{:S(2)}) collective-permute-start(bf16[2,176,256]{2,1,0:T(8,128)(2,1)S(1)} %get-tuple-element.44), channel_id=1, source_target_pairs={{0,64},{32,96},{64,128},{96,160},{128,192},{160,224},{192,256},{22... | collective-permute-start | bytes 540680 | tf_op jit(solution)/shard_map/ppermute | solution.py:109
  34.6 6.7 %collective-permute-start.3 = (bf16[2,176,256]{2,1,0:T(8,128)(2,1)S(1)}, bf16[2,176,256]{2,1,0:T(8,128)(2,1)S(1)}, u32[]{:S(2)}, u32[]{:S(2)}) collective-permute-start(bf16[2,176,256]{2,1,0:T(8,128)(2,1)S(1)} %get-tuple-element.45), channel_id=1, source_target_pairs={{0,448},{32,480},{64,0},{96,32},{128,64},{160,96},{192,128},{224,1... | collective-permute-start | bytes 540680 | tf_op jit(solution)/shard_map/ppermute | solution.py:109
  41.3 4.2 %collective-permute-done.2 = bf16[2,176,256]{2,1,0:T(8,128)(2,1)S(1)} collective-permute-done((bf16[2,176,256]{2,1,0:T(8,128)(2,1)S(1)}, bf16[2,176,256]{2,1,0:T(8,128)(2,1)S(1)}, u32[]{:S(2)}, u32[]{:S(2)}) %collective-permute-start.2) | collective-permute-done | bytes 180256 | tf_op jit(solution)/shard_map/ppermute | solution.py:109
  45.5 5.5 %collective-permute-done.3 = bf16[2,176,256]{2,1,0:T(8,128)(2,1)S(1)} collective-permute-done((bf16[2,176,256]{2,1,0:T(8,128)(2,1)S(1)}, bf16[2,176,256]{2,1,0:T(8,128)(2,1)S(1)}, u32[]{:S(2)}, u32[]{:S(2)}) %collective-permute-start.3) | collective-permute-done | bytes 180256 | tf_op jit(solution)/shard_map/ppermute | solution.py:109
  52.0 5.9 %all-to-all-start = ((bf16[4,176,256]{2,1,0:T(8,128)(2,1)}), bf16[4,176,256]{2,1,0:T(8,128)(2,1)S(1)}, u32[]{:S(2)}, u32[]{:S(2)}) async-start(bf16[4,176,256]{2,1,0:T(8,128)(2,1)} %add_convert_fusion), calls=%async_computation | async-start | bytes 720896 | tf_op jit(solution)/shard_map/all_to_all | solution.py:131
  57.8 15.0 %all_gather.28.left_ref = bf16[1408,352]{1,0:T(8,128)(2,1)} all-gather(bf16[176,352]{1,0:T(8,128)(2,1)S(1)} %multiply_bitcast_fusion.at_ref), channel_id=1, replica_groups=mesh['zh'=4,'zl'=4,'y'=4,'x'=4,'c'=2] {'y','c'}, dimensions={0}, use_global_device_ids=true | all-gather | bytes 1115136 | tf_op jit(solution)/shard_map/all_gather | solution.py:176
  72.9 13.9 %all-to-all-done = bf16[4,176,256]{2,1,0:T(8,128)(2,1)S(1)} async-done(((bf16[4,176,256]{2,1,0:T(8,128)(2,1)}), bf16[4,176,256]{2,1,0:T(8,128)(2,1)S(1)}, u32[]{:S(2)}, u32[]{:S(2)}) %all-to-all-start) | async-done | bytes 360480 | tf_op jit(solution)/shard_map/all_to_all | solution.py:131
  87.6 15.3 %all_gather.31.left_ref = bf16[1408,256]{1,0:T(8,128)(2,1)S(1)} all-gather(bf16[176,256]{1,0:T(8,128)(2,1)S(1)} %reduce_sum.77), channel_id=1, replica_groups=mesh['zh'=4,'zl'=4,'y'=4,'x'=4,'c'=2] {'y','c'}, dimensions={0}, use_global_device_ids=true | all-gather | bytes 811008 | tf_op jit(solution)/shard_map/all_gather | solution.py:180
  103.5 11.0 %all-gather.6.cloned.1.call-done = bf16[9728,128]{1,0:T(8,128)(2,1)} async-done(((bf16[608,128]{1,0:T(8,128)(2,1)}), bf16[9728,128]{1,0:T(8,128)(2,1)}) %all-gather.6.cloned.1.call-update) | async-done | bytes 2490384 | tf_op jit(solution)/shard_map/all_gather | solution.py:170
  114.5 1.7 copy-done
  116.2 1.4 shard_map.103
  117.7 4.8 %all-to-all-start.1 = ((bf16[4,256,128]{2,1,0:T(8,128)(2,1)}), bf16[4,256,128]{2,1,0:T(8,128)(2,1)S(1)}, u32[]{:S(2)}, u32[]{:S(2)}) async-start(bf16[4,256,128]{2,1,0:T(8,128)(2,1)} %shard_map.103), calls=%async_computation.1 | async-start | bytes 524288 | tf_op jit(solution)/shard_map/all_to_all | solution.py:131
  122.6 1.2 copy-done.2
  123.8 1.0 shard_map.104
  124.8 4.4 %all-to-all-done.1 = bf16[4,256,128]{2,1,0:T(8,128)(2,1)S(1)} async-done(((bf16[4,256,128]{2,1,0:T(8,128)(2,1)}), bf16[4,256,128]{2,1,0:T(8,128)(2,1)S(1)}, u32[]{:S(2)}, u32[]{:S(2)}) %all-to-all-start.1) | async-done | bytes 262176 | tf_op jit(solution)/shard_map/all_to_all | solution.py:131
  129.8 15.9 %all-gather.1 = bf16[2048,128]{1,0:T(8,128)(2,1)S(1)} all-gather(bf16[256,128]{1,0:T(8,128)(2,1)S(1)} %get-tuple-element.42), channel_id=3, replica_groups=mesh['zh'=4,'zl'=4,'y'=4,'x'=4,'c'=2] {'y','c'}, dimensions={0}, use_global_device_ids=true | all-gather | bytes 589824 | tf_op jit(solution)/shard_map/all_gather | solution.py:200
  145.7 1.2 shard_map.105
  146.8 3.4 %all-to-all-start.2 = ((bf16[4,256,128]{2,1,0:T(8,128)(2,1)}), bf16[4,256,128]{2,1,0:T(8,128)(2,1)S(1)}, u32[]{:S(2)}, u32[]{:S(2)}) async-start(bf16[4,256,128]{2,1,0:T(8,128)(2,1)} %shard_map.105), calls=%async_computation.2 | async-start | bytes 524288 | tf_op jit(solution)/shard_map/all_to_all | solution.py:131
  150.4 3.9 %collective-permute-start.5 = (bf16[352,128]{1,0:T(8,128)(2,1)S(1)}, bf16[352,128]{1,0:T(8,128)(2,1)S(1)}, u32[]{:S(2)}, u32[]{:S(2)}) collective-permute-start(bf16[352,128]{1,0:T(8,128)(2,1)S(1)} %get-tuple-element.34), channel_id=1, source_target_pairs={{0,2},{2,4},{4,6},{6,0},{1,3},{3,5},{5,7},{7,1},{8,10},{10,12},{12... | collective-permute-start | bytes 270344 | tf_op jit(solution)/shard_map/ppermute | solution.py:113
  154.2 4.6 %collective-permute-start.6 = (bf16[352,128]{1,0:T(8,128)(2,1)S(1)}, bf16[352,128]{1,0:T(8,128)(2,1)S(1)}, u32[]{:S(2)}, u32[]{:S(2)}) collective-permute-start(bf16[352,128]{1,0:T(8,128)(2,1)S(1)} %get-tuple-element.36), channel_id=1, source_target_pairs={{0,4},{2,6},{4,0},{6,2},{1,5},{3,7},{5,1},{7,3},{8,12},{10,14},{12... | collective-permute-start | bytes 270344 | tf_op jit(solution)/shard_map/ppermute | solution.py:113
  158.8 3.4 %collective-permute-start.7 = (bf16[352,128]{1,0:T(8,128)(2,1)S(1)}, bf16[352,128]{1,0:T(8,128)(2,1)S(1)}, u32[]{:S(2)}, u32[]{:S(2)}) collective-permute-start(bf16[352,128]{1,0:T(8,128)(2,1)S(1)} %get-tuple-element.38), channel_id=1, source_target_pairs={{0,6},{2,0},{4,2},{6,4},{1,7},{3,1},{5,3},{7,5},{8,14},{10,8},{12,... | collective-permute-start | bytes 270344 | tf_op jit(solution)/shard_map/ppermute | solution.py:113
  162.4 18.9 %all_gather.36.image_ref = bf16[4,256,128]{2,1,0:T(8,128)(2,1)S(1)} all-gather(bf16[1,256,128]{2,1,0:T(8,128)(2,1)S(1)} %fusion), channel_id=1, replica_groups=mesh['zh'=4,'zl'=4,'y'=4,'x'=4,'c'=2] {'zh'}, dimensions={0}, use_global_device_ids=true | all-gather | bytes 327680 | tf_op jit(solution)/shard_map/all_gather | solution.py:211
  181.3 1.6 copy-done.4
  182.9 1.4 shard_map.106
  184.4 6.5 %all-to-all-start.3 = ((bf16[4,256,128]{2,1,0:T(8,128)(2,1)}), bf16[4,256,128]{2,1,0:T(8,128)(2,1)S(1)}, u32[]{:S(2)}, u32[]{:S(2)}) async-start(bf16[4,256,128]{2,1,0:T(8,128)(2,1)} %shard_map.106), calls=%async_computation.3 | async-start | bytes 524288 | tf_op jit(solution)/shard_map/all_to_all | solution.py:131
  192.3 4.7 %all-to-all-done.3 = bf16[4,256,128]{2,1,0:T(8,128)(2,1)S(1)} async-done(((bf16[4,256,128]{2,1,0:T(8,128)(2,1)}), bf16[4,256,128]{2,1,0:T(8,128)(2,1)S(1)}, u32[]{:S(2)}, u32[]{:S(2)}) %all-to-all-start.3) | async-done | bytes 262176 | tf_op jit(solution)/shard_map/all_to_all | solution.py:131
  (58 shorter events, 9.7 us)
Async XLA Ops:
  7.2 107.4 %all-gather.6.cloned.1.call-start = ((), (), s32[]{:S(2)}) async-start(), calls=%async_computation.4 | async-start | bytes 2646016 | tf_op jit(solution)/shard_map/all_gather | solution.py:170
  9.0 8.9 %collective-permute-start.4 = (bf16[608,128]{1,0:T(8,128)(2,1)S(1)}, bf16[608,128]{1,0:T(8,128)(2,1)S(1)}, u32[]{:S(2)}, u32[]{:S(2)}) collective-permute-start(bf16[608,128]{1,0:T(8,128)(2,1)S(1)} %pad_maximum_fusion), channel_id=1, source_target_pairs={{0,0},{2,32},{4,64},{6,480},{32,2},{34,34},{36,66},{38,98},{64,132... | collective-permute-start | bytes 466952 | tf_op jit(solution)/shard_map/ppermute | solution.py:127
  14.6 1.8 copy-start.3
  17.9 0.7 copy-start.5
  18.6 32.4 %collective-permute-start = (bf16[4,176,256]{2,1,0:T(8,128)(2,1)S(1)}, bf16[4,176,256]{2,1,0:T(8,128)(2,1)S(1)}, u32[]{:S(2)}, u32[]{:S(2)}) collective-permute-start(bf16[4,176,256]{2,1,0:T(8,128)(2,1)S(1)} %get-tuple-element.24), channel_id=1, source_target_pairs={{0,32},{32,64},{64,96},{96,128},{128,160},{160,192},{192,224},{224... | collective-permute-start | bytes 1081352 | tf_op jit(solution)/shard_map/ppermute | solution.py:109
  28.4 22.7 %collective-permute-start.1 = (bf16[4,176,256]{2,1,0:T(8,128)(2,1)S(1)}, bf16[4,176,256]{2,1,0:T(8,128)(2,1)S(1)}, u32[]{:S(2)}, u32[]{:S(2)}) collective-permute-start(bf16[4,176,256]{2,1,0:T(8,128)(2,1)S(1)} %get-tuple-element.25), channel_id=1, source_target_pairs={{0,480},{32,0},{64,32},{96,64},{128,96},{160,128},{192,160},{224,1... | collective-permute-start | bytes 1081352 | tf_op jit(solution)/shard_map/ppermute | solution.py:109
  30.3 56.6 %copy-start.6 = (bf16[256,128]{1,0:T(8,128)(2,1)S(1)}, bf16[256,128]{1,0:T(8,128)(2,1)}, u32[]{:S(2)}) copy-start(bf16[256,128]{1,0:T(8,128)(2,1)} %param.12) | copy-start | bytes 196612
  30.3 15.2 %collective-permute-start.2 = (bf16[2,176,256]{2,1,0:T(8,128)(2,1)S(1)}, bf16[2,176,256]{2,1,0:T(8,128)(2,1)S(1)}, u32[]{:S(2)}, u32[]{:S(2)}) collective-permute-start(bf16[2,176,256]{2,1,0:T(8,128)(2,1)S(1)} %get-tuple-element.44), channel_id=1, source_target_pairs={{0,64},{32,96},{64,128},{96,160},{128,192},{160,224},{192,256},{22... | collective-permute-start | bytes 540680 | tf_op jit(solution)/shard_map/ppermute | solution.py:109
  34.6 16.4 %collective-permute-start.3 = (bf16[2,176,256]{2,1,0:T(8,128)(2,1)S(1)}, bf16[2,176,256]{2,1,0:T(8,128)(2,1)S(1)}, u32[]{:S(2)}, u32[]{:S(2)}) collective-permute-start(bf16[2,176,256]{2,1,0:T(8,128)(2,1)S(1)} %get-tuple-element.45), channel_id=1, source_target_pairs={{0,448},{32,480},{64,0},{96,32},{128,64},{160,96},{192,128},{224,1... | collective-permute-start | bytes 540680 | tf_op jit(solution)/shard_map/ppermute | solution.py:109
  52.0 34.8 %all-to-all-start = ((bf16[4,176,256]{2,1,0:T(8,128)(2,1)}), bf16[4,176,256]{2,1,0:T(8,128)(2,1)S(1)}, u32[]{:S(2)}, u32[]{:S(2)}) async-start(bf16[4,176,256]{2,1,0:T(8,128)(2,1)} %add_convert_fusion), calls=%async_computation | async-start | bytes 720896 | tf_op jit(solution)/shard_map/all_to_all | solution.py:131
  57.8 123.5 %all-gather.8.cloned.1.call-start = ((), (), s32[]{:S(2)}) async-start(), calls=%async_computation.5 | async-start | bytes 2162688 | tf_op jit(solution)/shard_map/all_gather | solution.py:181
  86.9 35.6 %copy-start.10 = (s32[16]{0:T(128)S(1)}, s32[16]{0:T(128)}, u32[]{:S(2)}) copy-start(s32[16]{0:T(128)} %param.11) | copy-start | bytes 196
  86.9 15.9 %collective-permute-start.8 = (bf16[256,128]{1,0:T(8,128)(2,1)S(1)}, bf16[256,128]{1,0:T(8,128)(2,1)S(1)}, u32[]{:S(2)}, u32[]{:S(2)}) collective-permute-start(bf16[256,128]{1,0:T(8,128)(2,1)S(1)} %copy-done.6), channel_id=1, source_target_pairs={{0,0},{8,128},{16,256},{24,384},{128,8},{136,136},{144,264},{152,3... | collective-permute-start | bytes 196616 | tf_op jit(solution)/shard_map/ppermute | solution.py:118
  102.8 0.6 copy-start.8
  114.5 1.7 copy-start
  116.2 6.3 %copy-start.1 = (bf16[9728,128]{1,0:T(8,128)(2,1)S(1)}, bf16[9728,128]{1,0:T(8,128)(2,1)}, u32[]{:S(2)}) copy-start(bf16[9728,128]{1,0:T(8,128)(2,1)} %all-gather.6.cloned.1.call-done) | copy-start | bytes 7471108
  117.7 11.5 %copy-start.7 = (bf16[256,128]{1,0:T(8,128)(2,1)S(1)}, bf16[256,128]{1,0:T(8,128)(2,1)}, u32[]{:S(2)}) copy-start(bf16[256,128]{1,0:T(8,128)(2,1)} %param.10) | copy-start | bytes 196612
  117.7 11.5 %all-to-all-start.1 = ((bf16[4,256,128]{2,1,0:T(8,128)(2,1)}), bf16[4,256,128]{2,1,0:T(8,128)(2,1)S(1)}, u32[]{:S(2)}, u32[]{:S(2)}) async-start(bf16[4,256,128]{2,1,0:T(8,128)(2,1)} %shard_map.103), calls=%async_computation.1 | async-start | bytes 524288 | tf_op jit(solution)/shard_map/all_to_all | solution.py:131
  122.6 1.2 copy-start.2
  146.8 15.4 %all-to-all-start.2 = ((bf16[4,256,128]{2,1,0:T(8,128)(2,1)}), bf16[4,256,128]{2,1,0:T(8,128)(2,1)S(1)}, u32[]{:S(2)}, u32[]{:S(2)}) async-start(bf16[4,256,128]{2,1,0:T(8,128)(2,1)} %shard_map.105), calls=%async_computation.2 | async-start | bytes 524288 | tf_op jit(solution)/shard_map/all_to_all | solution.py:131
  150.4 30.9 %collective-permute-start.5 = (bf16[352,128]{1,0:T(8,128)(2,1)S(1)}, bf16[352,128]{1,0:T(8,128)(2,1)S(1)}, u32[]{:S(2)}, u32[]{:S(2)}) collective-permute-start(bf16[352,128]{1,0:T(8,128)(2,1)S(1)} %get-tuple-element.34), channel_id=1, source_target_pairs={{0,2},{2,4},{4,6},{6,0},{1,3},{3,5},{5,7},{7,1},{8,10},{10,12},{12... | collective-permute-start | bytes 270344 | tf_op jit(solution)/shard_map/ppermute | solution.py:113
  154.2 27.0 %collective-permute-start.6 = (bf16[352,128]{1,0:T(8,128)(2,1)S(1)}, bf16[352,128]{1,0:T(8,128)(2,1)S(1)}, u32[]{:S(2)}, u32[]{:S(2)}) collective-permute-start(bf16[352,128]{1,0:T(8,128)(2,1)S(1)} %get-tuple-element.36), channel_id=1, source_target_pairs={{0,4},{2,6},{4,0},{6,2},{1,5},{3,7},{5,1},{7,3},{8,12},{10,14},{12... | collective-permute-start | bytes 270344 | tf_op jit(solution)/shard_map/ppermute | solution.py:113
  158.8 22.5 %collective-permute-start.7 = (bf16[352,128]{1,0:T(8,128)(2,1)S(1)}, bf16[352,128]{1,0:T(8,128)(2,1)S(1)}, u32[]{:S(2)}, u32[]{:S(2)}) collective-permute-start(bf16[352,128]{1,0:T(8,128)(2,1)S(1)} %get-tuple-element.38), channel_id=1, source_target_pairs={{0,6},{2,0},{4,2},{6,4},{1,7},{3,1},{5,3},{7,5},{8,14},{10,8},{12,... | collective-permute-start | bytes 270344 | tf_op jit(solution)/shard_map/ppermute | solution.py:113
  162.3 34.8 %copy-start.9 = (bf16[256,128]{1,0:T(8,128)(2,1)S(1)}, bf16[256,128]{1,0:T(8,128)(2,1)}, u32[]{:S(2)}) copy-start(bf16[256,128]{1,0:T(8,128)(2,1)} %param.13) | copy-start | bytes 196612
  181.3 1.6 copy-start.4
  184.4 12.7 %all-to-all-start.3 = ((bf16[4,256,128]{2,1,0:T(8,128)(2,1)}), bf16[4,256,128]{2,1,0:T(8,128)(2,1)S(1)}, u32[]{:S(2)}, u32[]{:S(2)}) async-start(bf16[4,256,128]{2,1,0:T(8,128)(2,1)} %shard_map.106), calls=%async_computation.3 | async-start | bytes 524288 | tf_op jit(solution)/shard_map/all_to_all | solution.py:131
Sparse Core Ops, SparseCore 0:
  18.7 95.7 all-gather.5
  118.2 59.8 all-gather.7

commit v7 on v6

--- a/solution.py
+++ b/solution.py
@@ -196,15 +196,16 @@
     inner = jnp.sum(after(exchange(inner, "x"), besides[0]).astype(F32), axis=0)
     parent_diag = (parent_inverse.astype(F32) + inner).astype(BF)
 
+    across = along_x(besides[2], 2)
     diag_wide = parent_diag * child_column_keep[None, :].astype(BF)
     diag_wide = lax.all_gather(diag_wide, ("y", "c"), axis=0)
     (product,) = call(
         child_kernel,
         [jax.ShapeDtypeStruct((4, 256, 128), BF)],
-        [place, diag_wide, blocks],
+        [place, after(diag_wide, across), blocks],
         2 * 1024 * 256 * 512,
     )
-    moved = [along_x(after(besides[d], product), d) for d in range(1, 4)]
+    moved = [along_x(after(besides[d], product), d) for d in (1, 3)] + [across]
     product = jnp.sum(exchange(product, "x").astype(F32), axis=0)
     parent_child = (-product * child_keep[:, None].astype(F32)).astype(BF)
 

time: 206 us -> 204 us (level)
  the two profiles are of different devices: /device:TPU:32 before, /device:TPU:2 now
where the time goes in v7:
time: 204 us; the launch traced here: 203 us
  blocking collectives  67.2 us (33%)
  starting transfers between devices  57.1 us (28%)
  waiting for transfers between devices  41.4 us (20%)
  between operations  14.4 us (7%)
  local copies, waits for them, and re-layouts  8.58 us (4%)
  other arithmetic  7.67 us (4%)
  Pallas kernels  6.46 us (3%)
    ppermute x4, starting transfers between devices, shift(): return lax.ppermute(value, Z, [(i, (i + by) % 16) for i in range(16)])  22.5 us
    all_to_all x4, starting transfers between devices, exchange(): return lax.all_to_all(value, axis, split_axis=0, concat_axis=0, tiled=True)  20.4 us
    all_gather x1, blocking collectives, per_device(): child_wide = lax.all_gather(parent_child, 'zh', axis=0)  18.2 us
    all_to_all x4, waiting for transfers between devices, exchange(): return lax.all_to_all(value, axis, split_axis=0, concat_axis=0, tiled=True)  18 us
    all_gather x1, blocking collectives, per_device(): diag_wide = lax.all_gather(diag_wide, ('y', 'c'), axis=0)  17.7 us
    all_gather x1, blocking collectives, per_device(): cov_wide = lax.all_gather(after(cov, image), ('y', 'c'), axis=0, tiled=True)  15.7 us
    all_gather x1, blocking collectives, per_device(): image_wide = lax.all_gather(image, ('y', 'c'), axis=0, tiled=True)  15.6 us
    all_gather x1, waiting for transfers between devices, per_device(): blocks = lax.all_gather(after(swapped, own), Z, axis=0)  14.9 us
  transfers between devices with their start and end apart: 15, of which 5 were waited for; matrix products, arithmetic and copies ran while one was open for 3% of the time, Pallas kernels for 2%

profile of v7, /device:TPU:2, one launch (start us, length us, event | category | flops | bytes accessed | tf_op | source)
XLA Modules:
  0.0 202.8 jit_solution(6446591978640935208)
XLA Ops:
  9.0 3.8 %collective-permute-start.4 = (bf16[608,128]{1,0:T(8,128)(2,1)S(1)}, bf16[608,128]{1,0:T(8,128)(2,1)S(1)}, u32[]{:S(2)}, u32[]{:S(2)}) collective-permute-start(bf16[608,128]{1,0:T(8,128)(2,1)S(1)} %pad_maximum_fusion), channel_id=1, source_target_pairs={{0,0},{2,32},{4,64},{6,480},{32,2},{34,34},{36,66},{38,98},{64,132... | collective-permute-start | bytes 466952 | tf_op jit(solution)/shard_map/ppermute | solution.py:127
  14.4 1.0 multiply_bitcast_fusion.at_ref
  15.5 1.8 copy-done.3
  17.3 1.5 shard_map.102
  19.5 1.9 collective-permute-start
  21.4 12.7 %collective-permute-start.1 = (bf16[4,176,256]{2,1,0:T(8,128)(2,1)S(1)}, bf16[4,176,256]{2,1,0:T(8,128)(2,1)S(1)}, u32[]{:S(2)}, u32[]{:S(2)}) collective-permute-start(bf16[4,176,256]{2,1,0:T(8,128)(2,1)S(1)} %get-tuple-element.25), channel_id=1, source_target_pairs={{0,480},{32,0},{64,32},{96,64},{128,96},{160,128},{192,160},{224,1... | collective-permute-start | bytes 1081352 | tf_op jit(solution)/shard_map/ppermute | solution.py:109
  34.1 1.9 collective-permute-start.2
  36.0 6.0 %collective-permute-start.3 = (bf16[2,176,256]{2,1,0:T(8,128)(2,1)S(1)}, bf16[2,176,256]{2,1,0:T(8,128)(2,1)S(1)}, u32[]{:S(2)}, u32[]{:S(2)}) collective-permute-start(bf16[2,176,256]{2,1,0:T(8,128)(2,1)S(1)} %get-tuple-element.45), channel_id=1, source_target_pairs={{0,448},{32,480},{64,0},{96,32},{128,64},{160,96},{192,128},{224,1... | collective-permute-start | bytes 540680 | tf_op jit(solution)/shard_map/ppermute | solution.py:109
  42.1 4.1 %collective-permute-done.2 = bf16[2,176,256]{2,1,0:T(8,128)(2,1)S(1)} collective-permute-done((bf16[2,176,256]{2,1,0:T(8,128)(2,1)S(1)}, bf16[2,176,256]{2,1,0:T(8,128)(2,1)S(1)}, u32[]{:S(2)}, u32[]{:S(2)}) %collective-permute-start.2) | collective-permute-done | bytes 180256 | tf_op jit(solution)/shard_map/ppermute | solution.py:109
  46.2 4.3 %collective-permute-done.3 = bf16[2,176,256]{2,1,0:T(8,128)(2,1)S(1)} collective-permute-done((bf16[2,176,256]{2,1,0:T(8,128)(2,1)S(1)}, bf16[2,176,256]{2,1,0:T(8,128)(2,1)S(1)}, u32[]{:S(2)}, u32[]{:S(2)}) %collective-permute-start.3) | collective-permute-done | bytes 180256 | tf_op jit(solution)/shard_map/ppermute | solution.py:109
  50.4 0.9 add_convert_fusion
  51.4 7.7 %all-to-all-start = ((bf16[4,176,256]{2,1,0:T(8,128)(2,1)}), bf16[4,176,256]{2,1,0:T(8,128)(2,1)S(1)}, u32[]{:S(2)}, u32[]{:S(2)}) async-start(bf16[4,176,256]{2,1,0:T(8,128)(2,1)} %add_convert_fusion), calls=%async_computation | async-start | bytes 720896 | tf_op jit(solution)/shard_map/all_to_all | solution.py:131
  59.1 15.7 %all_gather.28.left_ref = bf16[1408,352]{1,0:T(8,128)(2,1)} all-gather(bf16[176,352]{1,0:T(8,128)(2,1)S(1)} %multiply_bitcast_fusion.at_ref), channel_id=1, replica_groups=mesh['zh'=4,'zl'=4,'y'=4,'x'=4,'c'=2] {'y','c'}, dimensions={0}, use_global_device_ids=true | all-gather | bytes 1115136 | tf_op jit(solution)/shard_map/all_gather | solution.py:176
  74.8 10.4 %all-to-all-done = bf16[4,176,256]{2,1,0:T(8,128)(2,1)S(1)} async-done(((bf16[4,176,256]{2,1,0:T(8,128)(2,1)}), bf16[4,176,256]{2,1,0:T(8,128)(2,1)S(1)}, u32[]{:S(2)}, u32[]{:S(2)}) %all-to-all-start) | async-done | bytes 360480 | tf_op jit(solution)/shard_map/all_to_all | solution.py:131
  85.9 15.6 %all_gather.31.left_ref = bf16[1408,256]{1,0:T(8,128)(2,1)S(1)} all-gather(bf16[176,256]{1,0:T(8,128)(2,1)S(1)} %reduce_sum.77), channel_id=1, replica_groups=mesh['zh'=4,'zl'=4,'y'=4,'x'=4,'c'=2] {'y','c'}, dimensions={0}, use_global_device_ids=true | all-gather | bytes 811008 | tf_op jit(solution)/shard_map/all_gather | solution.py:180
  102.2 14.9 %all-gather.6.cloned.1.call-done = bf16[9728,128]{1,0:T(8,128)(2,1)} async-done(((bf16[608,128]{1,0:T(8,128)(2,1)}), bf16[9728,128]{1,0:T(8,128)(2,1)}) %all-gather.6.cloned.1.call-update) | async-done | bytes 2490384 | tf_op jit(solution)/shard_map/all_gather | solution.py:170
  117.2 1.7 copy-done
  118.9 1.4 shard_map.103
  120.3 3.5 %all-to-all-start.1 = ((bf16[4,256,128]{2,1,0:T(8,128)(2,1)}), bf16[4,256,128]{2,1,0:T(8,128)(2,1)S(1)}, u32[]{:S(2)}, u32[]{:S(2)}) async-start(bf16[4,256,128]{2,1,0:T(8,128)(2,1)} %shard_map.103), calls=%async_computation.1 | async-start | bytes 524288 | tf_op jit(solution)/shard_map/all_to_all | solution.py:131
  124.0 1.2 copy-done.2
  125.2 0.9 shard_map.104
  126.2 3.9 %collective-permute-start.5 = (bf16[352,128]{1,0:T(8,128)(2,1)S(1)}, bf16[352,128]{1,0:T(8,128)(2,1)S(1)}, u32[]{:S(2)}, u32[]{:S(2)}) collective-permute-start(bf16[352,128]{1,0:T(8,128)(2,1)S(1)} %get-tuple-element.34), channel_id=1, source_target_pairs={{0,4},{2,6},{4,0},{6,2},{1,5},{3,7},{5,1},{7,3},{8,12},{10,14},{12... | collective-permute-start | bytes 270344 | tf_op jit(solution)/shard_map/ppermute | solution.py:113
  130.8 17.7 %all-gather.1 = bf16[2048,128]{1,0:T(8,128)(2,1)S(1)} all-gather(bf16[256,128]{1,0:T(8,128)(2,1)S(1)} %get-tuple-element.42), channel_id=3, replica_groups=mesh['zh'=4,'zl'=4,'y'=4,'x'=4,'c'=2] {'y','c'}, dimensions={0}, use_global_device_ids=true | all-gather | bytes 589824 | tf_op jit(solution)/shard_map/all_gather | solution.py:201
  148.4 1.2 shard_map.105
  149.6 4.9 %all-to-all-start.2 = ((bf16[4,256,128]{2,1,0:T(8,128)(2,1)}), bf16[4,256,128]{2,1,0:T(8,128)(2,1)S(1)}, u32[]{:S(2)}, u32[]{:S(2)}) async-start(bf16[4,256,128]{2,1,0:T(8,128)(2,1)} %shard_map.105), calls=%async_computation.2 | async-start | bytes 524288 | tf_op jit(solution)/shard_map/all_to_all | solution.py:131
  154.6 3.4 %collective-permute-start.6 = (bf16[352,128]{1,0:T(8,128)(2,1)S(1)}, bf16[352,128]{1,0:T(8,128)(2,1)S(1)}, u32[]{:S(2)}, u32[]{:S(2)}) collective-permute-start(bf16[352,128]{1,0:T(8,128)(2,1)S(1)} %get-tuple-element.36), channel_id=1, source_target_pairs={{0,2},{2,4},{4,6},{6,0},{1,3},{3,5},{5,7},{7,1},{8,10},{10,12},{12... | collective-permute-start | bytes 270344 | tf_op jit(solution)/shard_map/ppermute | solution.py:113
  158.0 2.5 %collective-permute-start.7 = (bf16[352,128]{1,0:T(8,128)(2,1)S(1)}, bf16[352,128]{1,0:T(8,128)(2,1)S(1)}, u32[]{:S(2)}, u32[]{:S(2)}) collective-permute-start(bf16[352,128]{1,0:T(8,128)(2,1)S(1)} %get-tuple-element.38), channel_id=1, source_target_pairs={{0,6},{2,0},{4,2},{6,4},{1,7},{3,1},{5,3},{7,5},{8,14},{10,8},{12,... | collective-permute-start | bytes 270344 | tf_op jit(solution)/shard_map/ppermute | solution.py:113
  160.6 18.2 %all_gather.36.image_ref = bf16[4,256,128]{2,1,0:T(8,128)(2,1)S(1)} all-gather(bf16[1,256,128]{2,1,0:T(8,128)(2,1)S(1)} %fusion), channel_id=1, replica_groups=mesh['zh'=4,'zl'=4,'y'=4,'x'=4,'c'=2] {'zh'}, dimensions={0}, use_global_device_ids=true | all-gather | bytes 327680 | tf_op jit(solution)/shard_map/all_gather | solution.py:212
  178.8 1.6 copy-done.4
  180.4 1.4 shard_map.106
  181.9 4.3 %all-to-all-start.3 = ((bf16[4,256,128]{2,1,0:T(8,128)(2,1)}), bf16[4,256,128]{2,1,0:T(8,128)(2,1)S(1)}, u32[]{:S(2)}, u32[]{:S(2)}) async-start(bf16[4,256,128]{2,1,0:T(8,128)(2,1)} %shard_map.106), calls=%async_computation.3 | async-start | bytes 524288 | tf_op jit(solution)/shard_map/all_to_all | solution.py:131
  187.6 7.6 %all-to-all-done.3 = bf16[4,256,128]{2,1,0:T(8,128)(2,1)S(1)} async-done(((bf16[4,256,128]{2,1,0:T(8,128)(2,1)}), bf16[4,256,128]{2,1,0:T(8,128)(2,1)S(1)}, u32[]{:S(2)}, u32[]{:S(2)}) %all-to-all-start.3) | async-done | bytes 262176 | tf_op jit(solution)/shard_map/all_to_all | solution.py:131
  (58 shorter events, 8.8 us)
Async XLA Ops:
  7.2 110.0 %all-gather.6.cloned.1.call-start = ((), (), s32[]{:S(2)}) async-start(), calls=%async_computation.4 | async-start | bytes 2646016 | tf_op jit(solution)/shard_map/all_gather | solution.py:170
  9.0 9.8 %collective-permute-start.4 = (bf16[608,128]{1,0:T(8,128)(2,1)S(1)}, bf16[608,128]{1,0:T(8,128)(2,1)S(1)}, u32[]{:S(2)}, u32[]{:S(2)}) collective-permute-start(bf16[608,128]{1,0:T(8,128)(2,1)S(1)} %pad_maximum_fusion), channel_id=1, source_target_pairs={{0,0},{2,32},{4,64},{6,480},{32,2},{34,34},{36,66},{38,98},{64,132... | collective-permute-start | bytes 466952 | tf_op jit(solution)/shard_map/ppermute | solution.py:127
  15.5 1.8 copy-start.3
  18.8 0.7 copy-start.5
  19.5 31.0 %collective-permute-start = (bf16[4,176,256]{2,1,0:T(8,128)(2,1)S(1)}, bf16[4,176,256]{2,1,0:T(8,128)(2,1)S(1)}, u32[]{:S(2)}, u32[]{:S(2)}) collective-permute-start(bf16[4,176,256]{2,1,0:T(8,128)(2,1)S(1)} %get-tuple-element.24), channel_id=1, source_target_pairs={{0,32},{32,64},{64,96},{96,128},{128,160},{160,192},{192,224},{224... | collective-permute-start | bytes 1081352 | tf_op jit(solution)/shard_map/ppermute | solution.py:109
  21.4 29.1 %collective-permute-start.1 = (bf16[4,176,256]{2,1,0:T(8,128)(2,1)S(1)}, bf16[4,176,256]{2,1,0:T(8,128)(2,1)S(1)}, u32[]{:S(2)}, u32[]{:S(2)}) collective-permute-start(bf16[4,176,256]{2,1,0:T(8,128)(2,1)S(1)} %get-tuple-element.25), channel_id=1, source_target_pairs={{0,480},{32,0},{64,32},{96,64},{128,96},{160,128},{192,160},{224,1... | collective-permute-start | bytes 1081352 | tf_op jit(solution)/shard_map/ppermute | solution.py:109
  34.1 51.2 %copy-start.6 = (bf16[256,128]{1,0:T(8,128)(2,1)S(1)}, bf16[256,128]{1,0:T(8,128)(2,1)}, u32[]{:S(2)}) copy-start(bf16[256,128]{1,0:T(8,128)(2,1)} %param.12) | copy-start | bytes 196612
  34.1 12.1 %collective-permute-start.2 = (bf16[2,176,256]{2,1,0:T(8,128)(2,1)S(1)}, bf16[2,176,256]{2,1,0:T(8,128)(2,1)S(1)}, u32[]{:S(2)}, u32[]{:S(2)}) collective-permute-start(bf16[2,176,256]{2,1,0:T(8,128)(2,1)S(1)} %get-tuple-element.44), channel_id=1, source_target_pairs={{0,64},{32,96},{64,128},{96,160},{128,192},{160,224},{192,256},{22... | collective-permute-start | bytes 540680 | tf_op jit(solution)/shard_map/ppermute | solution.py:109
  36.0 14.4 %collective-permute-start.3 = (bf16[2,176,256]{2,1,0:T(8,128)(2,1)S(1)}, bf16[2,176,256]{2,1,0:T(8,128)(2,1)S(1)}, u32[]{:S(2)}, u32[]{:S(2)}) collective-permute-start(bf16[2,176,256]{2,1,0:T(8,128)(2,1)S(1)} %get-tuple-element.45), channel_id=1, source_target_pairs={{0,448},{32,480},{64,0},{96,32},{128,64},{160,96},{192,128},{224,1... | collective-permute-start | bytes 540680 | tf_op jit(solution)/shard_map/ppermute | solution.py:109
  51.4 33.8 %all-to-all-start = ((bf16[4,176,256]{2,1,0:T(8,128)(2,1)}), bf16[4,176,256]{2,1,0:T(8,128)(2,1)S(1)}, u32[]{:S(2)}, u32[]{:S(2)}) async-start(bf16[4,176,256]{2,1,0:T(8,128)(2,1)} %add_convert_fusion), calls=%async_computation | async-start | bytes 720896 | tf_op jit(solution)/shard_map/all_to_all | solution.py:131
  59.1 119.7 %all-gather.8.cloned.1.call-start = ((), (), s32[]{:S(2)}) async-start(), calls=%async_computation.5 | async-start | bytes 2162688 | tf_op jit(solution)/shard_map/all_gather | solution.py:181
  85.3 38.6 %copy-start.10 = (s32[16]{0:T(128)S(1)}, s32[16]{0:T(128)}, u32[]{:S(2)}) copy-start(s32[16]{0:T(128)} %param.11) | copy-start | bytes 196
  85.3 16.3 %collective-permute-start.8 = (bf16[256,128]{1,0:T(8,128)(2,1)S(1)}, bf16[256,128]{1,0:T(8,128)(2,1)S(1)}, u32[]{:S(2)}, u32[]{:S(2)}) collective-permute-start(bf16[256,128]{1,0:T(8,128)(2,1)S(1)} %copy-done.6), channel_id=1, source_target_pairs={{0,0},{8,128},{16,256},{24,384},{128,8},{136,136},{144,264},{152,3... | collective-permute-start | bytes 196616 | tf_op jit(solution)/shard_map/ppermute | solution.py:118
  101.6 0.6 copy-start.8
  117.2 1.7 copy-start
  118.9 5.1 %copy-start.1 = (bf16[9728,128]{1,0:T(8,128)(2,1)S(1)}, bf16[9728,128]{1,0:T(8,128)(2,1)}, u32[]{:S(2)}) copy-start(bf16[9728,128]{1,0:T(8,128)(2,1)} %all-gather.6.cloned.1.call-done) | copy-start | bytes 7471108
  120.3 9.8 %copy-start.7 = (bf16[256,128]{1,0:T(8,128)(2,1)S(1)}, bf16[256,128]{1,0:T(8,128)(2,1)}, u32[]{:S(2)}) copy-start(bf16[256,128]{1,0:T(8,128)(2,1)} %param.10) | copy-start | bytes 196612
  120.3 9.7 %all-to-all-start.1 = ((bf16[4,256,128]{2,1,0:T(8,128)(2,1)}), bf16[4,256,128]{2,1,0:T(8,128)(2,1)S(1)}, u32[]{:S(2)}, u32[]{:S(2)}) async-start(bf16[4,256,128]{2,1,0:T(8,128)(2,1)} %shard_map.103), calls=%async_computation.1 | async-start | bytes 524288 | tf_op jit(solution)/shard_map/all_to_all | solution.py:131
  124.0 1.2 copy-start.2
  126.2 22.3 %collective-permute-start.5 = (bf16[352,128]{1,0:T(8,128)(2,1)S(1)}, bf16[352,128]{1,0:T(8,128)(2,1)S(1)}, u32[]{:S(2)}, u32[]{:S(2)}) collective-permute-start(bf16[352,128]{1,0:T(8,128)(2,1)S(1)} %get-tuple-element.34), channel_id=1, source_target_pairs={{0,4},{2,6},{4,0},{6,2},{1,5},{3,7},{5,1},{7,3},{8,12},{10,14},{12... | collective-permute-start | bytes 270344 | tf_op jit(solution)/shard_map/ppermute | solution.py:113
  149.6 10.9 %all-to-all-start.2 = ((bf16[4,256,128]{2,1,0:T(8,128)(2,1)}), bf16[4,256,128]{2,1,0:T(8,128)(2,1)S(1)}, u32[]{:S(2)}, u32[]{:S(2)}) async-start(bf16[4,256,128]{2,1,0:T(8,128)(2,1)} %shard_map.105), calls=%async_computation.2 | async-start | bytes 524288 | tf_op jit(solution)/shard_map/all_to_all | solution.py:131
  154.6 24.2 %collective-permute-start.6 = (bf16[352,128]{1,0:T(8,128)(2,1)S(1)}, bf16[352,128]{1,0:T(8,128)(2,1)S(1)}, u32[]{:S(2)}, u32[]{:S(2)}) collective-permute-start(bf16[352,128]{1,0:T(8,128)(2,1)S(1)} %get-tuple-element.36), channel_id=1, source_target_pairs={{0,2},{2,4},{4,6},{6,0},{1,3},{3,5},{5,7},{7,1},{8,10},{10,12},{12... | collective-permute-start | bytes 270344 | tf_op jit(solution)/shard_map/ppermute | solution.py:113
  158.0 20.8 %collective-permute-start.7 = (bf16[352,128]{1,0:T(8,128)(2,1)S(1)}, bf16[352,128]{1,0:T(8,128)(2,1)S(1)}, u32[]{:S(2)}, u32[]{:S(2)}) collective-permute-start(bf16[352,128]{1,0:T(8,128)(2,1)S(1)} %get-tuple-element.38), channel_id=1, source_target_pairs={{0,6},{2,0},{4,2},{6,4},{1,7},{3,1},{5,3},{7,5},{8,14},{10,8},{12,... | collective-permute-start | bytes 270344 | tf_op jit(solution)/shard_map/ppermute | solution.py:113
  160.5 34.8 %copy-start.9 = (bf16[256,128]{1,0:T(8,128)(2,1)S(1)}, bf16[256,128]{1,0:T(8,128)(2,1)}, u32[]{:S(2)}) copy-start(bf16[256,128]{1,0:T(8,128)(2,1)} %param.13) | copy-start | bytes 196612
  178.8 1.6 copy-start.4
  181.9 13.4 %all-to-all-start.3 = ((bf16[4,256,128]{2,1,0:T(8,128)(2,1)}), bf16[4,256,128]{2,1,0:T(8,128)(2,1)S(1)}, u32[]{:S(2)}, u32[]{:S(2)}) async-start(bf16[4,256,128]{2,1,0:T(8,128)(2,1)} %shard_map.106), calls=%async_computation.3 | async-start | bytes 524288 | tf_op jit(solution)/shard_map/all_to_all | solution.py:131
Sparse Core Ops, SparseCore 0:
  19.6 97.5 all-gather.5
  120.9 57.1 all-gather.7

commit v8 on v7

--- a/solution.py
+++ b/solution.py
@@ -96,8 +96,7 @@
     for x in range(4):
         total = None
         for y in range(4):
-            n = (y * 4 + x) * 2
-            left = jnp.concatenate([factor_ref[n], factor_ref[n + 1]], axis=1)
+            left = jnp.concatenate([factor_ref[y, x, 0], factor_ref[y, x, 1]], axis=1)
             part = lax.dot_general(
                 left, image_ref[y], (((0,), (0,)), ((), ())), preferred_element_type=F32
             )
@@ -178,7 +177,10 @@
     image = jnp.sum(image.astype(F32), axis=0).astype(BF)
     factor = swap(after(child_panel, image), "zh", "y")
     image_wide = lax.all_gather(image, ("y", "c"), axis=0, tiled=True)
-    factor = lax.all_gather(after(factor, image_wide), PLANE, axis=0)
+    factor = lax.all_gather(after(factor, image_wide), "c", axis=0)
+    factor = lax.all_gather(factor, "x", axis=0)
+    image_wide = after(image_wide, factor)
+    factor = lax.all_gather(factor, "y", axis=0)
 
     (inner,) = call(
         panel_kernel,
@@ -209,7 +211,7 @@
     product = jnp.sum(exchange(product, "x").astype(F32), axis=0)
     parent_child = (-product * child_keep[:, None].astype(F32)).astype(BF)
 
-    child_wide = lax.all_gather(parent_child, "zh", axis=0)
+    child_wide = lax.all_gather(after(parent_child, factor), "zh", axis=0)
     (inner,) = call(
         last_kernel,
         [jax.ShapeDtypeStruct((4, 256, 128), BF)],

time: 204 us -> 213 us (1.044)
  the two profiles are of different devices: /device:TPU:2 before, /device:TPU:32 now
where the time goes in v8:
time: 213 us; the launch traced here: 212 us
  blocking collectives  86.5 us (41%)
  starting transfers between devices  60.6 us (28%)
  waiting for transfers between devices  29.4 us (14%)
  between operations  14.4 us (7%)
  local copies, waits for them, and re-layouts  7.94 us (4%)
  other arithmetic  6.93 us (3%)
  Pallas kernels  6.48 us (3%)
    ppermute x4, starting transfers between devices, shift(): return lax.ppermute(value, Z, [(i, (i + by) % 16) for i in range(16)])  22.6 us
    all_gather x1, blocking collectives, per_device(): child_wide = lax.all_gather(after(parent_child, factor), 'zh', axis=0)  22.5 us
    all_to_all x4, starting transfers between devices, exchange(): return lax.all_to_all(value, axis, split_axis=0, concat_axis=0, tiled=True)  21.7 us
    all_to_all x4, waiting for transfers between devices, exchange(): return lax.all_to_all(value, axis, split_axis=0, concat_axis=0, tiled=True)  19.6 us
    all_gather x1, blocking collectives, per_device(): diag_wide = lax.all_gather(diag_wide, ('y', 'c'), axis=0)  17.4 us
    all_gather x1, blocking collectives, per_device(): image_wide = lax.all_gather(image, ('y', 'c'), axis=0, tiled=True)  15.3 us
    all_gather x1, blocking collectives, per_device(): cov_wide = lax.all_gather(after(cov, image), ('y', 'c'), axis=0, tiled=True)  15 us
    all_gather x1, blocking collectives, per_device(): factor = lax.all_gather(factor, 'x', axis=0)  14.3 us
  transfers between devices with their start and end apart: 15, of which 5 were waited for; matrix products, arithmetic and copies ran while one was open for 3% of the time, Pallas kernels for 2%

profile of v8, /device:TPU:32, one launch (start us, length us, event | category | flops | bytes accessed | tf_op | source)
XLA Modules:
  0.0 212.3 jit_solution(3784847308020282872)
XLA Ops:
  9.0 2.9 %collective-permute-start.4 = (bf16[608,128]{1,0:T(8,128)(2,1)S(1)}, bf16[608,128]{1,0:T(8,128)(2,1)S(1)}, u32[]{:S(2)}, u32[]{:S(2)}) collective-permute-start(bf16[608,128]{1,0:T(8,128)(2,1)S(1)} %pad_maximum_fusion), channel_id=1, source_target_pairs={{0,0},{2,32},{4,64},{6,480},{32,2},{34,34},{36,66},{38,98},{64,132... | collective-permute-start | bytes 466952 | tf_op jit(solution)/shard_map/ppermute | solution.py:126
  13.5 1.0 multiply_bitcast_fusion.at_ref
  14.6 1.8 copy-done.3
  16.4 1.5 shard_map.102
  18.6 9.7 %collective-permute-start = (bf16[4,176,256]{2,1,0:T(8,128)(2,1)S(1)}, bf16[4,176,256]{2,1,0:T(8,128)(2,1)S(1)}, u32[]{:S(2)}, u32[]{:S(2)}) collective-permute-start(bf16[4,176,256]{2,1,0:T(8,128)(2,1)S(1)} %get-tuple-element.26), channel_id=1, source_target_pairs={{0,32},{32,64},{64,96},{96,128},{128,160},{160,192},{192,224},{224... | collective-permute-start | bytes 1081352 | tf_op jit(solution)/shard_map/ppermute | solution.py:108
  28.3 1.9 collective-permute-start.1
  30.3 4.3 %collective-permute-start.2 = (bf16[2,176,256]{2,1,0:T(8,128)(2,1)S(1)}, bf16[2,176,256]{2,1,0:T(8,128)(2,1)S(1)}, u32[]{:S(2)}, u32[]{:S(2)}) collective-permute-start(bf16[2,176,256]{2,1,0:T(8,128)(2,1)S(1)} %get-tuple-element.48), channel_id=1, source_target_pairs={{0,64},{32,96},{64,128},{96,160},{128,192},{160,224},{192,256},{22... | collective-permute-start | bytes 540680 | tf_op jit(solution)/shard_map/ppermute | solution.py:108
  34.6 6.7 %collective-permute-start.3 = (bf16[2,176,256]{2,1,0:T(8,128)(2,1)S(1)}, bf16[2,176,256]{2,1,0:T(8,128)(2,1)S(1)}, u32[]{:S(2)}, u32[]{:S(2)}) collective-permute-start(bf16[2,176,256]{2,1,0:T(8,128)(2,1)S(1)} %get-tuple-element.49), channel_id=1, source_target_pairs={{0,448},{32,480},{64,0},{96,32},{128,64},{160,96},{192,128},{224,1... | collective-permute-start | bytes 540680 | tf_op jit(solution)/shard_map/ppermute | solution.py:108
  41.3 4.2 %collective-permute-done.2 = bf16[2,176,256]{2,1,0:T(8,128)(2,1)S(1)} collective-permute-done((bf16[2,176,256]{2,1,0:T(8,128)(2,1)S(1)}, bf16[2,176,256]{2,1,0:T(8,128)(2,1)S(1)}, u32[]{:S(2)}, u32[]{:S(2)}) %collective-permute-start.2) | collective-permute-done | bytes 180256 | tf_op jit(solution)/shard_map/ppermute | solution.py:108
  45.5 5.5 %collective-permute-done.3 = bf16[2,176,256]{2,1,0:T(8,128)(2,1)S(1)} collective-permute-done((bf16[2,176,256]{2,1,0:T(8,128)(2,1)S(1)}, bf16[2,176,256]{2,1,0:T(8,128)(2,1)S(1)}, u32[]{:S(2)}, u32[]{:S(2)}) %collective-permute-start.3) | collective-permute-done | bytes 180256 | tf_op jit(solution)/shard_map/ppermute | solution.py:108
  52.0 5.9 %all-to-all-start = ((bf16[4,176,256]{2,1,0:T(8,128)(2,1)}), bf16[4,176,256]{2,1,0:T(8,128)(2,1)S(1)}, u32[]{:S(2)}, u32[]{:S(2)}) async-start(bf16[4,176,256]{2,1,0:T(8,128)(2,1)} %add_convert_fusion), calls=%async_computation | async-start | bytes 720896 | tf_op jit(solution)/shard_map/all_to_all | solution.py:130
  57.8 15.0 %all_gather.42.left_ref = bf16[1408,352]{1,0:T(8,128)(2,1)} all-gather(bf16[176,352]{1,0:T(8,128)(2,1)S(1)} %multiply_bitcast_fusion.at_ref), channel_id=1, replica_groups=mesh['zh'=4,'zl'=4,'y'=4,'x'=4,'c'=2] {'y','c'}, dimensions={0}, use_global_device_ids=true | all-gather | bytes 1115136 | tf_op jit(solution)/shard_map/all_gather | solution.py:175
  72.9 13.9 %all-to-all-done = bf16[4,176,256]{2,1,0:T(8,128)(2,1)S(1)} async-done(((bf16[4,176,256]{2,1,0:T(8,128)(2,1)}), bf16[4,176,256]{2,1,0:T(8,128)(2,1)S(1)}, u32[]{:S(2)}, u32[]{:S(2)}) %all-to-all-start) | async-done | bytes 360480 | tf_op jit(solution)/shard_map/all_to_all | solution.py:130
  87.6 15.3 %all_gather.45.left_ref = bf16[1408,256]{1,0:T(8,128)(2,1)S(1)} all-gather(bf16[176,256]{1,0:T(8,128)(2,1)S(1)} %reduce_sum.77), channel_id=1, replica_groups=mesh['zh'=4,'zl'=4,'y'=4,'x'=4,'c'=2] {'y','c'}, dimensions={0}, use_global_device_ids=true | all-gather | bytes 811008 | tf_op jit(solution)/shard_map/all_gather | solution.py:179
  102.8 1.9 all-gather.1
  104.7 14.3 %all-gather.2 = bf16[8,256,128]{2,1,0:T(8,128)(2,1)} all-gather(bf16[2,256,128]{2,1,0:T(8,128)(2,1)S(1)} %bitcast.20), channel_id=4, replica_groups=mesh['zh'=4,'zl'=4,'y'=4,'x'=4,'c'=2] {'x'}, dimensions={0}, use_global_device_ids=true | all-gather | bytes 655360 | tf_op jit(solution)/shard_map/all_gather | solution.py:181
  119.1 1.7 copy-done
  120.8 1.4 shard_map.103
  122.2 4.9 %all-to-all-start.1 = ((bf16[4,256,128]{2,1,0:T(8,128)(2,1)}), bf16[4,256,128]{2,1,0:T(8,128)(2,1)S(1)}, u32[]{:S(2)}, u32[]{:S(2)}) async-start(bf16[4,256,128]{2,1,0:T(8,128)(2,1)} %shard_map.103), calls=%async_computation.1 | async-start | bytes 524288 | tf_op jit(solution)/shard_map/all_to_all | solution.py:130
  127.3 1.2 copy-done.2
  128.5 1.0 shard_map.104
  129.5 5.4 %collective-permute-start.6 = (bf16[352,128]{1,0:T(8,128)(2,1)S(1)}, bf16[352,128]{1,0:T(8,128)(2,1)S(1)}, u32[]{:S(2)}, u32[]{:S(2)}) collective-permute-start(bf16[352,128]{1,0:T(8,128)(2,1)S(1)} %get-tuple-element.39), channel_id=1, source_target_pairs={{0,4},{2,6},{4,0},{6,2},{1,5},{3,7},{5,1},{7,3},{8,12},{10,14},{12... | collective-permute-start | bytes 270344 | tf_op jit(solution)/shard_map/ppermute | solution.py:112
  135.7 17.4 %all-gather.3 = bf16[2048,128]{1,0:T(8,128)(2,1)S(1)} all-gather(bf16[256,128]{1,0:T(8,128)(2,1)S(1)} %get-tuple-element.46), channel_id=5, replica_groups=mesh['zh'=4,'zl'=4,'y'=4,'x'=4,'c'=2] {'y','c'}, dimensions={0}, use_global_device_ids=true | all-gather | bytes 589824 | tf_op jit(solution)/shard_map/all_gather | solution.py:203
  153.1 1.2 shard_map.105
  154.3 3.4 %all-to-all-start.2 = ((bf16[4,256,128]{2,1,0:T(8,128)(2,1)}), bf16[4,256,128]{2,1,0:T(8,128)(2,1)S(1)}, u32[]{:S(2)}, u32[]{:S(2)}) async-start(bf16[4,256,128]{2,1,0:T(8,128)(2,1)} %shard_map.105), calls=%async_computation.2 | async-start | bytes 524288 | tf_op jit(solution)/shard_map/all_to_all | solution.py:130
  157.8 3.9 %collective-permute-start.7 = (bf16[352,128]{1,0:T(8,128)(2,1)S(1)}, bf16[352,128]{1,0:T(8,128)(2,1)S(1)}, u32[]{:S(2)}, u32[]{:S(2)}) collective-permute-start(bf16[352,128]{1,0:T(8,128)(2,1)S(1)} %get-tuple-element.41), channel_id=1, source_target_pairs={{0,2},{2,4},{4,6},{6,0},{1,3},{3,5},{5,7},{7,1},{8,10},{10,12},{12... | collective-permute-start | bytes 270344 | tf_op jit(solution)/shard_map/ppermute | solution.py:112
  161.7 3.3 %collective-permute-start.8 = (bf16[352,128]{1,0:T(8,128)(2,1)S(1)}, bf16[352,128]{1,0:T(8,128)(2,1)S(1)}, u32[]{:S(2)}, u32[]{:S(2)}) collective-permute-start(bf16[352,128]{1,0:T(8,128)(2,1)S(1)} %get-tuple-element.43), channel_id=1, source_target_pairs={{0,6},{2,0},{4,2},{6,4},{1,7},{3,1},{5,3},{7,5},{8,14},{10,8},{12,... | collective-permute-start | bytes 270344 | tf_op jit(solution)/shard_map/ppermute | solution.py:112
  165.4 22.5 %all-gather.5 = bf16[1024,128]{1,0:T(8,128)(2,1)S(1)} all-gather(bf16[256,128]{1,0:T(8,128)(2,1)S(1)} %multiply_convert_fusion.1), channel_id=7, replica_groups=mesh['zh'=4,'zl'=4,'y'=4,'x'=4,'c'=2] {'zh'}, dimensions={0}, use_global_device_ids=true | all-gather | bytes 327680 | tf_op jit(solution)/shard_map/all_gather | solution.py:214
  188.0 1.6 copy-done.4
  189.5 1.4 shard_map.106
  191.0 7.5 %all-to-all-start.3 = ((bf16[4,256,128]{2,1,0:T(8,128)(2,1)}), bf16[4,256,128]{2,1,0:T(8,128)(2,1)S(1)}, u32[]{:S(2)}, u32[]{:S(2)}) async-start(bf16[4,256,128]{2,1,0:T(8,128)(2,1)} %shard_map.106), calls=%async_computation.3 | async-start | bytes 524288 | tf_op jit(solution)/shard_map/all_to_all | solution.py:130
  199.3 5.5 %all-to-all-done.3 = bf16[4,256,128]{2,1,0:T(8,128)(2,1)S(1)} async-done(((bf16[4,256,128]{2,1,0:T(8,128)(2,1)}), bf16[4,256,128]{2,1,0:T(8,128)(2,1)S(1)}, u32[]{:S(2)}, u32[]{:S(2)}) %all-to-all-start.3) | async-done | bytes 262176 | tf_op jit(solution)/shard_map/all_to_all | solution.py:130
  (59 shorter events, 8.6 us)
Async XLA Ops:
  7.2 111.9 %all-gather.9.cloned.1.call-start = ((), (), s32[]{:S(2)}) async-start(), calls=%async_computation.4 | async-start | bytes 2646016 | tf_op jit(solution)/shard_map/all_gather | solution.py:169
  9.0 8.9 %collective-permute-start.4 = (bf16[608,128]{1,0:T(8,128)(2,1)S(1)}, bf16[608,128]{1,0:T(8,128)(2,1)S(1)}, u32[]{:S(2)}, u32[]{:S(2)}) collective-permute-start(bf16[608,128]{1,0:T(8,128)(2,1)S(1)} %pad_maximum_fusion), channel_id=1, source_target_pairs={{0,0},{2,32},{4,64},{6,480},{32,2},{34,34},{36,66},{38,98},{64,132... | collective-permute-start | bytes 466952 | tf_op jit(solution)/shard_map/ppermute | solution.py:126
  14.6 1.8 copy-start.3
  17.9 0.7 copy-start.6
  18.6 32.4 %collective-permute-start = (bf16[4,176,256]{2,1,0:T(8,128)(2,1)S(1)}, bf16[4,176,256]{2,1,0:T(8,128)(2,1)S(1)}, u32[]{:S(2)}, u32[]{:S(2)}) collective-permute-start(bf16[4,176,256]{2,1,0:T(8,128)(2,1)S(1)} %get-tuple-element.26), channel_id=1, source_target_pairs={{0,32},{32,64},{64,96},{96,128},{128,160},{160,192},{192,224},{224... | collective-permute-start | bytes 1081352 | tf_op jit(solution)/shard_map/ppermute | solution.py:108
  28.3 22.7 %collective-permute-start.1 = (bf16[4,176,256]{2,1,0:T(8,128)(2,1)S(1)}, bf16[4,176,256]{2,1,0:T(8,128)(2,1)S(1)}, u32[]{:S(2)}, u32[]{:S(2)}) collective-permute-start(bf16[4,176,256]{2,1,0:T(8,128)(2,1)S(1)} %get-tuple-element.27), channel_id=1, source_target_pairs={{0,480},{32,0},{64,32},{96,64},{128,96},{160,128},{192,160},{224,1... | collective-permute-start | bytes 1081352 | tf_op jit(solution)/shard_map/ppermute | solution.py:108
  30.3 56.6 %copy-start.7 = (bf16[256,128]{1,0:T(8,128)(2,1)S(1)}, bf16[256,128]{1,0:T(8,128)(2,1)}, u32[]{:S(2)}) copy-start(bf16[256,128]{1,0:T(8,128)(2,1)} %param.12) | copy-start | bytes 196612
  30.3 15.2 %collective-permute-start.2 = (bf16[2,176,256]{2,1,0:T(8,128)(2,1)S(1)}, bf16[2,176,256]{2,1,0:T(8,128)(2,1)S(1)}, u32[]{:S(2)}, u32[]{:S(2)}) collective-permute-start(bf16[2,176,256]{2,1,0:T(8,128)(2,1)S(1)} %get-tuple-element.48), channel_id=1, source_target_pairs={{0,64},{32,96},{64,128},{96,160},{128,192},{160,224},{192,256},{22... | collective-permute-start | bytes 540680 | tf_op jit(solution)/shard_map/ppermute | solution.py:108
  34.6 16.4 %collective-permute-start.3 = (bf16[2,176,256]{2,1,0:T(8,128)(2,1)S(1)}, bf16[2,176,256]{2,1,0:T(8,128)(2,1)S(1)}, u32[]{:S(2)}, u32[]{:S(2)}) collective-permute-start(bf16[2,176,256]{2,1,0:T(8,128)(2,1)S(1)} %get-tuple-element.49), channel_id=1, source_target_pairs={{0,448},{32,480},{64,0},{96,32},{128,64},{160,96},{192,128},{224,1... | collective-permute-start | bytes 540680 | tf_op jit(solution)/shard_map/ppermute | solution.py:108
  52.0 34.8 %all-to-all-start = ((bf16[4,176,256]{2,1,0:T(8,128)(2,1)}), bf16[4,176,256]{2,1,0:T(8,128)(2,1)S(1)}, u32[]{:S(2)}, u32[]{:S(2)}) async-start(bf16[4,176,256]{2,1,0:T(8,128)(2,1)} %add_convert_fusion), calls=%async_computation | async-start | bytes 720896 | tf_op jit(solution)/shard_map/all_to_all | solution.py:130
  57.8 107.6 %all-gather.11.cloned.1.call-start = ((), (), s32[]{:S(2)}) async-start(), calls=%async_computation.5 | async-start | bytes 2621440 | tf_op jit(solution)/shard_map/all_gather | solution.py:183
  86.9 15.9 %collective-permute-start.5 = (bf16[256,128]{1,0:T(8,128)(2,1)S(1)}, bf16[256,128]{1,0:T(8,128)(2,1)S(1)}, u32[]{:S(2)}, u32[]{:S(2)}) collective-permute-start(bf16[256,128]{1,0:T(8,128)(2,1)S(1)} %copy-done.7), channel_id=1, source_target_pairs={{0,0},{8,128},{16,256},{24,384},{128,8},{136,136},{144,264},{152,3... | collective-permute-start | bytes 196616 | tf_op jit(solution)/shard_map/ppermute | solution.py:117
  104.7 22.5 %copy-start.10 = (s32[16]{0:T(128)S(1)}, s32[16]{0:T(128)}, u32[]{:S(2)}) copy-start(s32[16]{0:T(128)} %param.11) | copy-start | bytes 196
  119.1 1.7 copy-start
  120.8 6.5 %copy-start.1 = (bf16[9728,128]{1,0:T(8,128)(2,1)S(1)}, bf16[9728,128]{1,0:T(8,128)(2,1)}, u32[]{:S(2)}) copy-start(bf16[9728,128]{1,0:T(8,128)(2,1)} %all-gather.9.cloned.1.call-done) | copy-start | bytes 7471108
  122.2 12.8 %copy-start.8 = (bf16[256,128]{1,0:T(8,128)(2,1)S(1)}, bf16[256,128]{1,0:T(8,128)(2,1)}, u32[]{:S(2)}) copy-start(bf16[256,128]{1,0:T(8,128)(2,1)} %param.10) | copy-start | bytes 196612
  122.2 12.7 %all-to-all-start.1 = ((bf16[4,256,128]{2,1,0:T(8,128)(2,1)}), bf16[4,256,128]{2,1,0:T(8,128)(2,1)S(1)}, u32[]{:S(2)}, u32[]{:S(2)}) async-start(bf16[4,256,128]{2,1,0:T(8,128)(2,1)} %shard_map.103), calls=%async_computation.1 | async-start | bytes 524288 | tf_op jit(solution)/shard_map/all_to_all | solution.py:130
  127.3 1.2 copy-start.2
  129.5 23.6 %collective-permute-start.6 = (bf16[352,128]{1,0:T(8,128)(2,1)S(1)}, bf16[352,128]{1,0:T(8,128)(2,1)S(1)}, u32[]{:S(2)}, u32[]{:S(2)}) collective-permute-start(bf16[352,128]{1,0:T(8,128)(2,1)S(1)} %get-tuple-element.39), channel_id=1, source_target_pairs={{0,4},{2,6},{4,0},{6,2},{1,5},{3,7},{5,1},{7,3},{8,12},{10,14},{12... | collective-permute-start | bytes 270344 | tf_op jit(solution)/shard_map/ppermute | solution.py:112
  154.3 10.9 %all-to-all-start.2 = ((bf16[4,256,128]{2,1,0:T(8,128)(2,1)}), bf16[4,256,128]{2,1,0:T(8,128)(2,1)S(1)}, u32[]{:S(2)}, u32[]{:S(2)}) async-start(bf16[4,256,128]{2,1,0:T(8,128)(2,1)} %shard_map.105), calls=%async_computation.2 | async-start | bytes 524288 | tf_op jit(solution)/shard_map/all_to_all | solution.py:130
  157.8 30.1 %collective-permute-start.7 = (bf16[352,128]{1,0:T(8,128)(2,1)S(1)}, bf16[352,128]{1,0:T(8,128)(2,1)S(1)}, u32[]{:S(2)}, u32[]{:S(2)}) collective-permute-start(bf16[352,128]{1,0:T(8,128)(2,1)S(1)} %get-tuple-element.41), channel_id=1, source_target_pairs={{0,2},{2,4},{4,6},{6,0},{1,3},{3,5},{5,7},{7,1},{8,10},{10,12},{12... | collective-permute-start | bytes 270344 | tf_op jit(solution)/shard_map/ppermute | solution.py:112
  161.7 43.1 %copy-start.9 = (bf16[256,128]{1,0:T(8,128)(2,1)S(1)}, bf16[256,128]{1,0:T(8,128)(2,1)}, u32[]{:S(2)}) copy-start(bf16[256,128]{1,0:T(8,128)(2,1)} %param.13) | copy-start | bytes 196612
  161.7 26.2 %collective-permute-start.8 = (bf16[352,128]{1,0:T(8,128)(2,1)S(1)}, bf16[352,128]{1,0:T(8,128)(2,1)S(1)}, u32[]{:S(2)}, u32[]{:S(2)}) collective-permute-start(bf16[352,128]{1,0:T(8,128)(2,1)S(1)} %get-tuple-element.43), channel_id=1, source_target_pairs={{0,6},{2,0},{4,2},{6,4},{1,7},{3,1},{5,3},{7,5},{8,14},{10,8},{12,... | collective-permute-start | bytes 270344 | tf_op jit(solution)/shard_map/ppermute | solution.py:112
  165.4 40.1 %copy-start.5 = (bf16[256,128]{1,0:T(8,128)(2,1)}, bf16[256,128]{1,0:T(8,128)(2,1)S(1)}, u32[]{:S(2)}) copy-start(bf16[256,128]{1,0:T(8,128)(2,1)S(1)} %multiply_convert_fusion.1) | copy-start | bytes 196612
  187.9 1.6 copy-start.4
  191.0 13.7 %all-to-all-start.3 = ((bf16[4,256,128]{2,1,0:T(8,128)(2,1)}), bf16[4,256,128]{2,1,0:T(8,128)(2,1)S(1)}, u32[]{:S(2)}, u32[]{:S(2)}) async-start(bf16[4,256,128]{2,1,0:T(8,128)(2,1)} %shard_map.106), calls=%async_computation.3 | async-start | bytes 524288 | tf_op jit(solution)/shard_map/all_to_all | solution.py:130
Sparse Core Ops, SparseCore 0:
  18.7 95.6 all-gather.8
  119.2 44.8 all-gather.10

commit v9 on v7

--- a/solution.py
+++ b/solution.py
@@ -109,8 +109,8 @@
     return lax.ppermute(value, Z, [(i, (i + by) % 16) for i in range(16)])
 
 
-def along_x(value, by):
-    return lax.ppermute(value, "x", [(i, (i + by) % 4) for i in range(4)])
+def along(value, axis, by):
+    return lax.ppermute(value, axis, [(i, (i + by) % 4) for i in range(4)])
 
 
 def swap(value, first, second):
@@ -171,11 +171,19 @@
     right, left = shift(right, 1), shift(left, -1)
     far = jnp.concatenate([shift(far[:2], 2), shift(far[2:], -2)], axis=0)
     image = own + right.astype(F32) + left.astype(F32) + far.astype(F32)
-    image = image.astype(BF)
-
-    cov_wide = lax.all_gather(after(cov, image), ("y", "c"), axis=0, tiled=True)
-    image = after(exchange(image, "zh"), cov_wide)
-    image = jnp.sum(image.astype(F32), axis=0).astype(BF)
+
+    zh = lax.axis_index("zh")
+    near = [lax.dynamic_index_in_dim(image, (zh + d) % 4, 0, False) for d in range(4)]
+    half = near[2].astype(BF)
+    ahead, behind = along(half[:, :128], "zh", 1), along(half[:, 128:], "zh", 3)
+    cov_wide = lax.all_gather(after(cov, half), ("y", "c"), axis=0, tiled=True)
+    ahead = after(ahead, cov_wide)
+    nothing = jnp.zeros((176, 128), F32)
+    ahead = near[1] + jnp.concatenate([ahead.astype(F32), nothing], axis=1)
+    behind = near[3] + jnp.concatenate([nothing, behind.astype(F32)], axis=1)
+    ahead = along(ahead.astype(BF), "zh", 1)
+    behind = along(behind.astype(BF), "zh", 3)
+    image = (near[0] + ahead.astype(F32) + behind.astype(F32)).astype(BF)
     factor = swap(after(child_panel, image), "zh", "y")
     image_wide = lax.all_gather(image, ("y", "c"), axis=0, tiled=True)
     factor = lax.all_gather(after(factor, image_wide), PLANE, axis=0)
@@ -196,7 +204,7 @@
     inner = jnp.sum(after(exchange(inner, "x"), besides[0]).astype(F32), axis=0)
     parent_diag = (parent_inverse.astype(F32) + inner).astype(BF)
 
-    across = along_x(besides[2], 2)
+    across = along(besides[2], "x", 2)
     diag_wide = parent_diag * child_column_keep[None, :].astype(BF)
     diag_wide = lax.all_gather(diag_wide, ("y", "c"), axis=0)
     (product,) = call(
@@ -205,7 +213,7 @@
         [place, after(diag_wide, across), blocks],
         2 * 1024 * 256 * 512,
     )
-    moved = [along_x(after(besides[d], product), d) for d in (1, 3)] + [across]
+    moved = [along(after(besides[d], product), "x", d) for d in (1, 3)] + [across]
     product = jnp.sum(exchange(product, "x").astype(F32), axis=0)
     parent_child = (-product * child_keep[:, None].astype(F32)).astype(BF)
 

time: 204 us -> 208 us (1.020)
  the two profiles are of different devices: /device:TPU:2 before, /device:TPU:32 now
where the time goes in v9:
time: 208 us; the launch traced here: 207 us
  starting transfers between devices  75.9 us (36%)
  blocking collectives  71.5 us (34%)
  waiting for transfers between devices  22.9 us (11%)
  between operations  14.5 us (7%)
  local copies, waits for them, and re-layouts  8.63 us (4%)
  other arithmetic  6.87 us (3%)
  Pallas kernels  6.48 us (3%)
    ppermute x7, starting transfers between devices, along(): return lax.ppermute(value, axis, [(i, (i + by) % 4) for i in range(4)])  32 us
    all_gather x1, blocking collectives, per_device(): image_wide = lax.all_gather(image, ('y', 'c'), axis=0, tiled=True)  23.8 us
    ppermute x4, starting transfers between devices, shift(): return lax.ppermute(value, Z, [(i, (i + by) % 16) for i in range(16)])  22.6 us
    all_gather x1, blocking collectives, per_device(): child_wide = lax.all_gather(parent_child, 'zh', axis=0)  19.2 us
    all_to_all x3, starting transfers between devices, exchange(): return lax.all_to_all(value, axis, split_axis=0, concat_axis=0, tiled=True)  17.6 us
    all_gather x1, blocking collectives, per_device(): cov_wide = lax.all_gather(after(cov, half), ('y', 'c'), axis=0, tiled=True)  15.3 us
    all_gather x1, blocking collectives, per_device(): diag_wide = lax.all_gather(diag_wide, ('y', 'c'), axis=0)  13.2 us
    ppermute x4, waiting for transfers between devices, shift(): return lax.ppermute(value, Z, [(i, (i + by) % 16) for i in range(16)])  9.69 us
  transfers between devices with their start and end apart: 18, of which 7 were waited for; matrix products, arithmetic and copies ran while one was open for 3% of the time, Pallas kernels for 2%

profile of v9, /device:TPU:32, one launch (start us, length us, event | category | flops | bytes accessed | tf_op | source)
XLA Modules:
  0.0 206.7 jit_solution(220024825504634410)
XLA Ops:
  9.0 2.9 %collective-permute-start.4 = (bf16[608,128]{1,0:T(8,128)(2,1)S(1)}, bf16[608,128]{1,0:T(8,128)(2,1)S(1)}, u32[]{:S(2)}, u32[]{:S(2)}) collective-permute-start(bf16[608,128]{1,0:T(8,128)(2,1)S(1)} %pad_maximum_fusion), channel_id=1, source_target_pairs={{0,0},{2,32},{4,64},{6,480},{32,2},{34,34},{36,66},{38,98},{64,132... | collective-permute-start | bytes 466952 | tf_op jit(solution)/shard_map/ppermute | solution.py:127
  14.6 1.8 copy-done.3
  16.4 1.5 shard_map.102
  18.7 9.7 %collective-permute-start = (bf16[4,176,256]{2,1,0:T(8,128)(2,1)S(1)}, bf16[4,176,256]{2,1,0:T(8,128)(2,1)S(1)}, u32[]{:S(2)}, u32[]{:S(2)}) collective-permute-start(bf16[4,176,256]{2,1,0:T(8,128)(2,1)S(1)} %get-tuple-element.24), channel_id=1, source_target_pairs={{0,32},{32,64},{64,96},{96,128},{128,160},{160,192},{192,224},{224... | collective-permute-start | bytes 1081352 | tf_op jit(solution)/shard_map/ppermute | solution.py:109
  28.4 1.9 collective-permute-start.1
  30.4 4.3 %collective-permute-start.2 = (bf16[2,176,256]{2,1,0:T(8,128)(2,1)S(1)}, bf16[2,176,256]{2,1,0:T(8,128)(2,1)S(1)}, u32[]{:S(2)}, u32[]{:S(2)}) collective-permute-start(bf16[2,176,256]{2,1,0:T(8,128)(2,1)S(1)} %get-tuple-element.46), channel_id=1, source_target_pairs={{0,64},{32,96},{64,128},{96,160},{128,192},{160,224},{192,256},{22... | collective-permute-start | bytes 540680 | tf_op jit(solution)/shard_map/ppermute | solution.py:109
  34.6 6.7 %collective-permute-start.3 = (bf16[2,176,256]{2,1,0:T(8,128)(2,1)S(1)}, bf16[2,176,256]{2,1,0:T(8,128)(2,1)S(1)}, u32[]{:S(2)}, u32[]{:S(2)}) collective-permute-start(bf16[2,176,256]{2,1,0:T(8,128)(2,1)S(1)} %get-tuple-element.47), channel_id=1, source_target_pairs={{0,448},{32,480},{64,0},{96,32},{128,64},{160,96},{192,128},{224,1... | collective-permute-start | bytes 540680 | tf_op jit(solution)/shard_map/ppermute | solution.py:109
  41.4 4.2 %collective-permute-done.2 = bf16[2,176,256]{2,1,0:T(8,128)(2,1)S(1)} collective-permute-done((bf16[2,176,256]{2,1,0:T(8,128)(2,1)S(1)}, bf16[2,176,256]{2,1,0:T(8,128)(2,1)S(1)}, u32[]{:S(2)}, u32[]{:S(2)}) %collective-permute-start.2) | collective-permute-done | bytes 180256 | tf_op jit(solution)/shard_map/ppermute | solution.py:109
  45.6 5.5 %collective-permute-done.3 = bf16[2,176,256]{2,1,0:T(8,128)(2,1)S(1)} collective-permute-done((bf16[2,176,256]{2,1,0:T(8,128)(2,1)S(1)}, bf16[2,176,256]{2,1,0:T(8,128)(2,1)S(1)}, u32[]{:S(2)}, u32[]{:S(2)}) %collective-permute-start.3) | collective-permute-done | bytes 180256 | tf_op jit(solution)/shard_map/ppermute | solution.py:109
  51.3 3.5 %collective-permute-start.5 = (bf16[176,128]{1,0:T(8,128)(2,1)S(1)}, bf16[176,128]{1,0:T(8,128)(2,1)S(1)}, u32[]{:S(2)}, u32[]{:S(2)}) collective-permute-start(bf16[176,128]{1,0:T(8,128)(2,1)S(1)} %get-tuple-element.48), channel_id=1, source_target_pairs={{0,128},{128,256},{256,384},{384,0},{1,129},{129,257},{257,385},{3... | collective-permute-start | bytes 135176 | tf_op jit(solution)/shard_map/ppermute | solution.py:113
  54.8 6.3 %collective-permute-start.7 = (bf16[176,128]{1,0:T(8,128)(2,1)S(1)}, bf16[176,128]{1,0:T(8,128)(2,1)S(1)}, u32[]{:S(2)}, u32[]{:S(2)}) collective-permute-start(bf16[176,128]{1,0:T(8,128)(2,1)S(1)} %get-tuple-element.49), channel_id=1, source_target_pairs={{0,384},{128,0},{256,128},{384,256},{1,385},{129,1},{257,129},{385... | collective-permute-start | bytes 135176 | tf_op jit(solution)/shard_map/ppermute | solution.py:113
  61.1 15.3 %all_gather.28.left_ref = bf16[1408,352]{1,0:T(8,128)(2,1)} all-gather(bf16[176,352]{1,0:T(8,128)(2,1)S(1)} %multiply_bitcast_fusion.at_ref), channel_id=1, replica_groups=mesh['zh'=4,'zl'=4,'y'=4,'x'=4,'c'=2] {'y','c'}, dimensions={0}, use_global_device_ids=true | all-gather | bytes 1115136 | tf_op jit(solution)/shard_map/all_gather | solution.py:179
  76.4 3.5 %collective-permute-start.6 = (bf16[176,256]{1,0:T(8,128)(2,1)S(1)}, bf16[176,256]{1,0:T(8,128)(2,1)S(1)}, u32[]{:S(2)}, u32[]{:S(2)}) collective-permute-start(bf16[176,256]{1,0:T(8,128)(2,1)S(1)} %get-tuple-element.44), channel_id=1, source_target_pairs={{0,128},{128,256},{256,384},{384,0},{1,129},{129,257},{257,385},{3... | collective-permute-start | bytes 270344 | tf_op jit(solution)/shard_map/ppermute | solution.py:113
  79.9 6.2 %collective-permute-start.8 = (bf16[176,256]{1,0:T(8,128)(2,1)S(1)}, bf16[176,256]{1,0:T(8,128)(2,1)S(1)}, u32[]{:S(2)}, u32[]{:S(2)}) collective-permute-start(bf16[176,256]{1,0:T(8,128)(2,1)S(1)} %get-tuple-element.45), channel_id=1, source_target_pairs={{0,384},{128,0},{256,128},{384,256},{1,385},{129,1},{257,129},{385... | collective-permute-start | bytes 270344 | tf_op jit(solution)/shard_map/ppermute | solution.py:113
  86.2 5.9 %collective-permute-done.6 = bf16[176,256]{1,0:T(8,128)(2,1)S(1)} collective-permute-done((bf16[176,256]{1,0:T(8,128)(2,1)S(1)}, bf16[176,256]{1,0:T(8,128)(2,1)S(1)}, u32[]{:S(2)}, u32[]{:S(2)}) %collective-permute-start.6) | collective-permute-done | bytes 90144 | tf_op jit(solution)/shard_map/ppermute | solution.py:113
  93.5 23.8 %all_gather.31.left_ref = bf16[1408,256]{1,0:T(8,128)(2,1)S(1)} all-gather(bf16[176,256]{1,0:T(8,128)(2,1)S(1)} %fusion.3), channel_id=1, replica_groups=mesh['zh'=4,'zl'=4,'y'=4,'x'=4,'c'=2] {'y','c'}, dimensions={0}, use_global_device_ids=true | all-gather | bytes 811008 | tf_op jit(solution)/shard_map/all_gather | solution.py:188
  118.0 1.7 copy-done
  119.7 1.5 shard_map.103
  121.2 4.2 %all-to-all-start = ((bf16[4,256,128]{2,1,0:T(8,128)(2,1)}), bf16[4,256,128]{2,1,0:T(8,128)(2,1)S(1)}, u32[]{:S(2)}, u32[]{:S(2)}) async-start(bf16[4,256,128]{2,1,0:T(8,128)(2,1)} %shard_map.103), calls=%async_computation | async-start | bytes 524288 | tf_op jit(solution)/shard_map/all_to_all | solution.py:131
  125.5 1.2 copy-done.2
  127.7 5.4 %collective-permute-start.9 = (bf16[352,128]{1,0:T(8,128)(2,1)S(1)}, bf16[352,128]{1,0:T(8,128)(2,1)S(1)}, u32[]{:S(2)}, u32[]{:S(2)}) collective-permute-start(bf16[352,128]{1,0:T(8,128)(2,1)S(1)} %get-tuple-element.34), channel_id=1, source_target_pairs={{0,4},{2,6},{4,0},{6,2},{1,5},{3,7},{5,1},{7,3},{8,12},{10,14},{12... | collective-permute-start | bytes 270344 | tf_op jit(solution)/shard_map/ppermute | solution.py:113
  133.9 13.2 %all-gather.1 = bf16[2048,128]{1,0:T(8,128)(2,1)S(1)} all-gather(bf16[256,128]{1,0:T(8,128)(2,1)S(1)} %get-tuple-element.42), channel_id=3, replica_groups=mesh['zh'=4,'zl'=4,'y'=4,'x'=4,'c'=2] {'y','c'}, dimensions={0}, use_global_device_ids=true | all-gather | bytes 589824 | tf_op jit(solution)/shard_map/all_gather | solution.py:209
  147.1 1.2 shard_map.105
  148.3 3.4 %all-to-all-start.1 = ((bf16[4,256,128]{2,1,0:T(8,128)(2,1)}), bf16[4,256,128]{2,1,0:T(8,128)(2,1)S(1)}, u32[]{:S(2)}, u32[]{:S(2)}) async-start(bf16[4,256,128]{2,1,0:T(8,128)(2,1)} %shard_map.105), calls=%async_computation.1 | async-start | bytes 524288 | tf_op jit(solution)/shard_map/all_to_all | solution.py:131
  151.8 3.9 %collective-permute-start.10 = (bf16[352,128]{1,0:T(8,128)(2,1)S(1)}, bf16[352,128]{1,0:T(8,128)(2,1)S(1)}, u32[]{:S(2)}, u32[]{:S(2)}) collective-permute-start(bf16[352,128]{1,0:T(8,128)(2,1)S(1)} %get-tuple-element.36), channel_id=1, source_target_pairs={{0,2},{2,4},{4,6},{6,0},{1,3},{3,5},{5,7},{7,1},{8,10},{10,12},{12... | collective-permute-start | bytes 270344 | tf_op jit(solution)/shard_map/ppermute | solution.py:113
  155.7 3.2 %collective-permute-start.11 = (bf16[352,128]{1,0:T(8,128)(2,1)S(1)}, bf16[352,128]{1,0:T(8,128)(2,1)S(1)}, u32[]{:S(2)}, u32[]{:S(2)}) collective-permute-start(bf16[352,128]{1,0:T(8,128)(2,1)S(1)} %get-tuple-element.38), channel_id=1, source_target_pairs={{0,6},{2,0},{4,2},{6,4},{1,7},{3,1},{5,3},{7,5},{8,14},{10,8},{12,... | collective-permute-start | bytes 270344 | tf_op jit(solution)/shard_map/ppermute | solution.py:113
  159.4 19.2 %all_gather.36.image_ref = bf16[4,256,128]{2,1,0:T(8,128)(2,1)S(1)} all-gather(bf16[1,256,128]{2,1,0:T(8,128)(2,1)S(1)} %fusion.4), channel_id=1, replica_groups=mesh['zh'=4,'zl'=4,'y'=4,'x'=4,'c'=2] {'zh'}, dimensions={0}, use_global_device_ids=true | all-gather | bytes 327680 | tf_op jit(solution)/shard_map/all_gather | solution.py:220
  178.6 1.4 all-gather.8.cloned.1.call-done
  180.0 1.6 copy-done.4
  181.6 1.4 shard_map.106
  183.0 10.0 %all-to-all-start.2 = ((bf16[4,256,128]{2,1,0:T(8,128)(2,1)}), bf16[4,256,128]{2,1,0:T(8,128)(2,1)S(1)}, u32[]{:S(2)}, u32[]{:S(2)}) async-start(bf16[4,256,128]{2,1,0:T(8,128)(2,1)} %shard_map.106), calls=%async_computation.2 | async-start | bytes 524288 | tf_op jit(solution)/shard_map/all_to_all | solution.py:131
  194.5 4.7 %all-to-all-done.2 = bf16[4,256,128]{2,1,0:T(8,128)(2,1)S(1)} async-done(((bf16[4,256,128]{2,1,0:T(8,128)(2,1)}), bf16[4,256,128]{2,1,0:T(8,128)(2,1)S(1)}, u32[]{:S(2)}, u32[]{:S(2)}) %all-to-all-start.2) | async-done | bytes 262176 | tf_op jit(solution)/shard_map/all_to_all | solution.py:131
  (67 shorter events, 12.0 us)
Async XLA Ops:
  7.2 110.9 %all-gather.6.cloned.1.call-start = ((), (), s32[]{:S(2)}) async-start(), calls=%async_computation.3 | async-start | bytes 2646016 | tf_op jit(solution)/shard_map/all_gather | solution.py:170
  9.0 8.9 %collective-permute-start.4 = (bf16[608,128]{1,0:T(8,128)(2,1)S(1)}, bf16[608,128]{1,0:T(8,128)(2,1)S(1)}, u32[]{:S(2)}, u32[]{:S(2)}) collective-permute-start(bf16[608,128]{1,0:T(8,128)(2,1)S(1)} %pad_maximum_fusion), channel_id=1, source_target_pairs={{0,0},{2,32},{4,64},{6,480},{32,2},{34,34},{36,66},{38,98},{64,132... | collective-permute-start | bytes 466952 | tf_op jit(solution)/shard_map/ppermute | solution.py:127
  14.6 1.8 copy-start.3
  17.9 0.7 copy-start.5
  18.6 161.4 %all-gather.8.cloned.1.call-start = ((), (), s32[]{:S(2)}) async-start(), calls=%async_computation.4 | async-start | bytes 2162688 | tf_op jit(solution)/shard_map/all_gather | solution.py:189
  18.7 32.4 %collective-permute-start = (bf16[4,176,256]{2,1,0:T(8,128)(2,1)S(1)}, bf16[4,176,256]{2,1,0:T(8,128)(2,1)S(1)}, u32[]{:S(2)}, u32[]{:S(2)}) collective-permute-start(bf16[4,176,256]{2,1,0:T(8,128)(2,1)S(1)} %get-tuple-element.24), channel_id=1, source_target_pairs={{0,32},{32,64},{64,96},{96,128},{128,160},{160,192},{192,224},{224... | collective-permute-start | bytes 1081352 | tf_op jit(solution)/shard_map/ppermute | solution.py:109
  28.4 22.7 %collective-permute-start.1 = (bf16[4,176,256]{2,1,0:T(8,128)(2,1)S(1)}, bf16[4,176,256]{2,1,0:T(8,128)(2,1)S(1)}, u32[]{:S(2)}, u32[]{:S(2)}) collective-permute-start(bf16[4,176,256]{2,1,0:T(8,128)(2,1)S(1)} %get-tuple-element.25), channel_id=1, source_target_pairs={{0,480},{32,0},{64,32},{96,64},{128,96},{160,128},{192,160},{224,1... | collective-permute-start | bytes 1081352 | tf_op jit(solution)/shard_map/ppermute | solution.py:109
  30.4 15.2 %collective-permute-start.2 = (bf16[2,176,256]{2,1,0:T(8,128)(2,1)S(1)}, bf16[2,176,256]{2,1,0:T(8,128)(2,1)S(1)}, u32[]{:S(2)}, u32[]{:S(2)}) collective-permute-start(bf16[2,176,256]{2,1,0:T(8,128)(2,1)S(1)} %get-tuple-element.46), channel_id=1, source_target_pairs={{0,64},{32,96},{64,128},{96,160},{128,192},{160,224},{192,256},{22... | collective-permute-start | bytes 540680 | tf_op jit(solution)/shard_map/ppermute | solution.py:109
  34.6 16.5 %collective-permute-start.3 = (bf16[2,176,256]{2,1,0:T(8,128)(2,1)S(1)}, bf16[2,176,256]{2,1,0:T(8,128)(2,1)S(1)}, u32[]{:S(2)}, u32[]{:S(2)}) collective-permute-start(bf16[2,176,256]{2,1,0:T(8,128)(2,1)S(1)} %get-tuple-element.47), channel_id=1, source_target_pairs={{0,448},{32,480},{64,0},{96,32},{128,64},{160,96},{192,128},{224,1... | collective-permute-start | bytes 540680 | tf_op jit(solution)/shard_map/ppermute | solution.py:109
  41.4 51.4 %copy-start.6 = (bf16[256,128]{1,0:T(8,128)(2,1)S(1)}, bf16[256,128]{1,0:T(8,128)(2,1)}, u32[]{:S(2)}) copy-start(bf16[256,128]{1,0:T(8,128)(2,1)} %param.12) | copy-start | bytes 196612
  51.3 25.0 %collective-permute-start.5 = (bf16[176,128]{1,0:T(8,128)(2,1)S(1)}, bf16[176,128]{1,0:T(8,128)(2,1)S(1)}, u32[]{:S(2)}, u32[]{:S(2)}) collective-permute-start(bf16[176,128]{1,0:T(8,128)(2,1)S(1)} %get-tuple-element.48), channel_id=1, source_target_pairs={{0,128},{128,256},{256,384},{384,0},{1,129},{129,257},{257,385},{3... | collective-permute-start | bytes 135176 | tf_op jit(solution)/shard_map/ppermute | solution.py:113
  54.8 21.5 %collective-permute-start.7 = (bf16[176,128]{1,0:T(8,128)(2,1)S(1)}, bf16[176,128]{1,0:T(8,128)(2,1)S(1)}, u32[]{:S(2)}, u32[]{:S(2)}) collective-permute-start(bf16[176,128]{1,0:T(8,128)(2,1)S(1)} %get-tuple-element.49), channel_id=1, source_target_pairs={{0,384},{128,0},{256,128},{384,256},{1,385},{129,1},{257,129},{385... | collective-permute-start | bytes 135176 | tf_op jit(solution)/shard_map/ppermute | solution.py:113
  76.4 15.7 %collective-permute-start.6 = (bf16[176,256]{1,0:T(8,128)(2,1)S(1)}, bf16[176,256]{1,0:T(8,128)(2,1)S(1)}, u32[]{:S(2)}, u32[]{:S(2)}) collective-permute-start(bf16[176,256]{1,0:T(8,128)(2,1)S(1)} %get-tuple-element.44), channel_id=1, source_target_pairs={{0,128},{128,256},{256,384},{384,0},{1,129},{129,257},{257,385},{3... | collective-permute-start | bytes 270344 | tf_op jit(solution)/shard_map/ppermute | solution.py:113
  79.9 12.9 %collective-permute-start.8 = (bf16[176,256]{1,0:T(8,128)(2,1)S(1)}, bf16[176,256]{1,0:T(8,128)(2,1)S(1)}, u32[]{:S(2)}, u32[]{:S(2)}) collective-permute-start(bf16[176,256]{1,0:T(8,128)(2,1)S(1)} %get-tuple-element.45), channel_id=1, source_target_pairs={{0,384},{128,0},{256,128},{384,256},{1,385},{129,1},{257,129},{385... | collective-permute-start | bytes 270344 | tf_op jit(solution)/shard_map/ppermute | solution.py:113
  92.9 32.6 %copy-start.10 = (s32[16]{0:T(128)S(1)}, s32[16]{0:T(128)}, u32[]{:S(2)}) copy-start(s32[16]{0:T(128)} %param.11) | copy-start | bytes 196
  92.9 24.5 %collective-permute-start.12 = (bf16[256,128]{1,0:T(8,128)(2,1)S(1)}, bf16[256,128]{1,0:T(8,128)(2,1)S(1)}, u32[]{:S(2)}, u32[]{:S(2)}) collective-permute-start(bf16[256,128]{1,0:T(8,128)(2,1)S(1)} %copy-done.6), channel_id=1, source_target_pairs={{0,0},{8,128},{16,256},{24,384},{128,8},{136,136},{144,264},{152,3... | collective-permute-start | bytes 196616 | tf_op jit(solution)/shard_map/ppermute | solution.py:118
  117.4 0.6 copy-start.8
  118.0 1.7 copy-start
  119.7 5.8 %copy-start.1 = (bf16[9728,128]{1,0:T(8,128)(2,1)S(1)}, bf16[9728,128]{1,0:T(8,128)(2,1)}, u32[]{:S(2)}) copy-start(bf16[9728,128]{1,0:T(8,128)(2,1)} %all-gather.6.cloned.1.call-done) | copy-start | bytes 7471108
  121.2 12.0 %copy-start.7 = (bf16[256,128]{1,0:T(8,128)(2,1)S(1)}, bf16[256,128]{1,0:T(8,128)(2,1)}, u32[]{:S(2)}) copy-start(bf16[256,128]{1,0:T(8,128)(2,1)} %param.10) | copy-start | bytes 196612
  121.2 12.0 %all-to-all-start = ((bf16[4,256,128]{2,1,0:T(8,128)(2,1)}), bf16[4,256,128]{2,1,0:T(8,128)(2,1)S(1)}, u32[]{:S(2)}, u32[]{:S(2)}) async-start(bf16[4,256,128]{2,1,0:T(8,128)(2,1)} %shard_map.103), calls=%async_computation | async-start | bytes 524288 | tf_op jit(solution)/shard_map/all_to_all | solution.py:131
  125.5 1.2 copy-start.2
  127.7 19.4 %collective-permute-start.9 = (bf16[352,128]{1,0:T(8,128)(2,1)S(1)}, bf16[352,128]{1,0:T(8,128)(2,1)S(1)}, u32[]{:S(2)}, u32[]{:S(2)}) collective-permute-start(bf16[352,128]{1,0:T(8,128)(2,1)S(1)} %get-tuple-element.34), channel_id=1, source_target_pairs={{0,4},{2,6},{4,0},{6,2},{1,5},{3,7},{5,1},{7,3},{8,12},{10,14},{12... | collective-permute-start | bytes 270344 | tf_op jit(solution)/shard_map/ppermute | solution.py:113
  148.3 10.9 %all-to-all-start.1 = ((bf16[4,256,128]{2,1,0:T(8,128)(2,1)}), bf16[4,256,128]{2,1,0:T(8,128)(2,1)S(1)}, u32[]{:S(2)}, u32[]{:S(2)}) async-start(bf16[4,256,128]{2,1,0:T(8,128)(2,1)} %shard_map.105), calls=%async_computation.1 | async-start | bytes 524288 | tf_op jit(solution)/shard_map/all_to_all | solution.py:131
  151.8 26.8 %collective-permute-start.10 = (bf16[352,128]{1,0:T(8,128)(2,1)S(1)}, bf16[352,128]{1,0:T(8,128)(2,1)S(1)}, u32[]{:S(2)}, u32[]{:S(2)}) collective-permute-start(bf16[352,128]{1,0:T(8,128)(2,1)S(1)} %get-tuple-element.36), channel_id=1, source_target_pairs={{0,2},{2,4},{4,6},{6,0},{1,3},{3,5},{5,7},{7,1},{8,10},{10,12},{12... | collective-permute-start | bytes 270344 | tf_op jit(solution)/shard_map/ppermute | solution.py:113
  155.7 22.9 %collective-permute-start.11 = (bf16[352,128]{1,0:T(8,128)(2,1)S(1)}, bf16[352,128]{1,0:T(8,128)(2,1)S(1)}, u32[]{:S(2)}, u32[]{:S(2)}) collective-permute-start(bf16[352,128]{1,0:T(8,128)(2,1)S(1)} %get-tuple-element.38), channel_id=1, source_target_pairs={{0,6},{2,0},{4,2},{6,4},{1,7},{3,1},{5,3},{7,5},{8,14},{10,8},{12,... | collective-permute-start | bytes 270344 | tf_op jit(solution)/shard_map/ppermute | solution.py:113
  159.2 40.0 %copy-start.9 = (bf16[256,128]{1,0:T(8,128)(2,1)S(1)}, bf16[256,128]{1,0:T(8,128)(2,1)}, u32[]{:S(2)}) copy-start(bf16[256,128]{1,0:T(8,128)(2,1)} %param.13) | copy-start | bytes 196612
  180.0 1.6 copy-start.4
  183.0 16.2 %all-to-all-start.2 = ((bf16[4,256,128]{2,1,0:T(8,128)(2,1)}), bf16[4,256,128]{2,1,0:T(8,128)(2,1)S(1)}, u32[]{:S(2)}, u32[]{:S(2)}) async-start(bf16[4,256,128]{2,1,0:T(8,128)(2,1)} %shard_map.106), calls=%async_computation.2 | async-start | bytes 524288 | tf_op jit(solution)/shard_map/all_to_all | solution.py:131
Sparse Core Ops, SparseCore 0:
  18.7 91.2 all-gather.5
  118.1 61.8 all-gather.7

commit v10 on v9

--- a/solution.py
+++ b/solution.py
@@ -170,14 +170,14 @@
     blocks = lax.all_gather(after(swapped, own), Z, axis=0)
     right, left = shift(right, 1), shift(left, -1)
     far = jnp.concatenate([shift(far[:2], 2), shift(far[2:], -2)], axis=0)
+    cov_wide = lax.all_gather(after(cov, own), ("y", "c"), axis=0, tiled=True)
+    right = after(right, cov_wide)
     image = own + right.astype(F32) + left.astype(F32) + far.astype(F32)
 
     zh = lax.axis_index("zh")
     near = [lax.dynamic_index_in_dim(image, (zh + d) % 4, 0, False) for d in range(4)]
     half = near[2].astype(BF)
     ahead, behind = along(half[:, :128], "zh", 1), along(half[:, 128:], "zh", 3)
-    cov_wide = lax.all_gather(after(cov, half), ("y", "c"), axis=0, tiled=True)
-    ahead = after(ahead, cov_wide)
     nothing = jnp.zeros((176, 128), F32)
     ahead = near[1] + jnp.concatenate([ahead.astype(F32), nothing], axis=1)
     behind = near[3] + jnp.concatenate([nothing, behind.astype(F32)], axis=1)

time: 208 us -> 206 us (level)
  blocking collectives: 71.5 us -> 67.7 us
    ppermute x7, waiting for transfers between devices: 6.67 us -> 18.2 us  [along(): return lax.ppermute(value, axis, [(i, (i + by) % 4) for i in range(4)])]
    ppermute x4, waiting for transfers between devices: 9.69 us -> 0.01 us  [shift(): return lax.ppermute(value, Z, [(i, (i + by) % 16) for i in range(16)])]
    all_gather x1, blocking collectives: 23.8 us -> 17.8 us  [per_device(): image_wide = lax.all_gather(image, ('y', 'c'), axis=0, tiled=True)]
    all_gather x1, blocking collectives: 19.2 us -> 21.3 us  [per_device(): child_wide = lax.all_gather(parent_child, 'zh', axis=0)]
  transfers between devices with their start and end apart: 18 -> 18, of which waited for: 7 -> 6; matrix products, arithmetic and copies ran while one was open for 3% -> 3% of each run, Pallas kernels for 2% -> 2%
where the time goes in v10:
time: 206 us; the launch traced here: 205 us
  starting transfers between devices  77.1 us (37%)
  blocking collectives  67.7 us (33%)
  waiting for transfers between devices  23.4 us (11%)
  between operations  14.5 us (7%)
  local copies, waits for them, and re-layouts  8.62 us (4%)
  other arithmetic  6.88 us (3%)
  Pallas kernels  6.49 us (3%)
    ppermute x7, starting transfers between devices, along(): return lax.ppermute(value, axis, [(i, (i + by) % 4) for i in range(4)])  33.2 us
    ppermute x4, starting transfers between devices, shift(): return lax.ppermute(value, Z, [(i, (i + by) % 16) for i in range(16)])  22.8 us
    all_gather x1, blocking collectives, per_device(): child_wide = lax.all_gather(parent_child, 'zh', axis=0)  21.3 us
    ppermute x7, waiting for transfers between devices, along(): return lax.ppermute(value, axis, [(i, (i + by) % 4) for i in range(4)])  18.2 us
    all_gather x1, blocking collectives, per_device(): image_wide = lax.all_gather(image, ('y', 'c'), axis=0, tiled=True)  17.8 us
    all_to_all x3, starting transfers between devices, exchange(): return lax.all_to_all(value, axis, split_axis=0, concat_axis=0, tiled=True)  17.4 us
    all_gather x1, blocking collectives, per_device(): cov_wide = lax.all_gather(after(cov, own), ('y', 'c'), axis=0, tiled=True)  15.3 us
    all_gather x1, blocking collectives, per_device(): diag_wide = lax.all_gather(diag_wide, ('y', 'c'), axis=0)  13.2 us
  transfers between devices with their start and end apart: 18, of which 6 were waited for; matrix products, arithmetic and copies ran while one was open for 3% of the time, Pallas kernels for 2%

profile of v10, /device:TPU:32, one launch (start us, length us, event | category | flops | bytes accessed | tf_op | source)
XLA Modules:
  0.0 204.6 jit_solution(5281892202585627930)
XLA Ops:
  9.0 2.9 %collective-permute-start = (bf16[608,128]{1,0:T(8,128)(2,1)S(1)}, bf16[608,128]{1,0:T(8,128)(2,1)S(1)}, u32[]{:S(2)}, u32[]{:S(2)}) collective-permute-start(bf16[608,128]{1,0:T(8,128)(2,1)S(1)} %pad_maximum_fusion), channel_id=1, source_target_pairs={{0,0},{2,32},{4,64},{6,480},{32,2},{34,34},{36,66},{38,98},{64,132... | collective-permute-start | bytes 466952 | tf_op jit(solution)/shard_map/ppermute | solution.py:127
  14.6 1.8 copy-done.3
  16.4 1.5 shard_map.102
  18.7 9.7 %collective-permute-start.1 = (bf16[4,176,256]{2,1,0:T(8,128)(2,1)S(1)}, bf16[4,176,256]{2,1,0:T(8,128)(2,1)S(1)}, u32[]{:S(2)}, u32[]{:S(2)}) collective-permute-start(bf16[4,176,256]{2,1,0:T(8,128)(2,1)S(1)} %get-tuple-element.26), channel_id=1, source_target_pairs={{0,32},{32,64},{64,96},{96,128},{128,160},{160,192},{192,224},{224... | collective-permute-start | bytes 1081352 | tf_op jit(solution)/shard_map/ppermute | solution.py:109
  28.5 2.3 %collective-permute-start.3 = (bf16[2,176,256]{2,1,0:T(8,128)(2,1)S(1)}, bf16[2,176,256]{2,1,0:T(8,128)(2,1)S(1)}, u32[]{:S(2)}, u32[]{:S(2)}) collective-permute-start(bf16[2,176,256]{2,1,0:T(8,128)(2,1)S(1)} %get-tuple-element.46), channel_id=1, source_target_pairs={{0,64},{32,96},{64,128},{96,160},{128,192},{160,224},{192,256},{22... | collective-permute-start | bytes 540680 | tf_op jit(solution)/shard_map/ppermute | solution.py:109
  30.7 5.7 %collective-permute-start.4 = (bf16[2,176,256]{2,1,0:T(8,128)(2,1)S(1)}, bf16[2,176,256]{2,1,0:T(8,128)(2,1)S(1)}, u32[]{:S(2)}, u32[]{:S(2)}) collective-permute-start(bf16[2,176,256]{2,1,0:T(8,128)(2,1)S(1)} %get-tuple-element.47), channel_id=1, source_target_pairs={{0,448},{32,480},{64,0},{96,32},{128,64},{160,96},{192,128},{224,1... | collective-permute-start | bytes 540680 | tf_op jit(solution)/shard_map/ppermute | solution.py:109
  36.4 5.1 %collective-permute-start.2 = (bf16[4,176,256]{2,1,0:T(8,128)(2,1)S(1)}, bf16[4,176,256]{2,1,0:T(8,128)(2,1)S(1)}, u32[]{:S(2)}, u32[]{:S(2)}) collective-permute-start(bf16[4,176,256]{2,1,0:T(8,128)(2,1)S(1)} %get-tuple-element.28), channel_id=1, source_target_pairs={{0,480},{32,0},{64,32},{96,64},{128,96},{160,128},{192,160},{224,1... | collective-permute-start | bytes 1081352 | tf_op jit(solution)/shard_map/ppermute | solution.py:109
  41.5 15.3 %all_gather.28.left_ref = bf16[1408,352]{1,0:T(8,128)(2,1)} all-gather(bf16[176,352]{1,0:T(8,128)(2,1)S(1)} %multiply_bitcast_fusion.at_ref), channel_id=1, replica_groups=mesh['zh'=4,'zl'=4,'y'=4,'x'=4,'c'=2] {'y','c'}, dimensions={0}, use_global_device_ids=true | all-gather | bytes 1115136 | tf_op jit(solution)/shard_map/all_gather | solution.py:173
  57.0 7.7 %collective-permute-start.5 = (bf16[176,128]{1,0:T(8,128)(2,1)S(1)}, bf16[176,128]{1,0:T(8,128)(2,1)S(1)}, u32[]{:S(2)}, u32[]{:S(2)}) collective-permute-start(bf16[176,128]{1,0:T(8,128)(2,1)S(1)} %get-tuple-element.48), channel_id=1, source_target_pairs={{0,128},{128,256},{256,384},{384,0},{1,129},{129,257},{257,385},{3... | collective-permute-start | bytes 135176 | tf_op jit(solution)/shard_map/ppermute | solution.py:113
  64.7 3.3 %collective-permute-start.7 = (bf16[176,128]{1,0:T(8,128)(2,1)S(1)}, bf16[176,128]{1,0:T(8,128)(2,1)S(1)}, u32[]{:S(2)}, u32[]{:S(2)}) collective-permute-start(bf16[176,128]{1,0:T(8,128)(2,1)S(1)} %get-tuple-element.49), channel_id=1, source_target_pairs={{0,384},{128,0},{256,128},{384,256},{1,385},{129,1},{257,129},{385... | collective-permute-start | bytes 135176 | tf_op jit(solution)/shard_map/ppermute | solution.py:113
  68.1 1.4 collective-permute-done.5
  69.5 7.6 %collective-permute-done.7 = bf16[176,128]{1,0:T(8,128)(2,1)S(1)} collective-permute-done((bf16[176,128]{1,0:T(8,128)(2,1)S(1)}, bf16[176,128]{1,0:T(8,128)(2,1)S(1)}, u32[]{:S(2)}, u32[]{:S(2)}) %collective-permute-start.7) | collective-permute-done | bytes 45088 | tf_op jit(solution)/shard_map/ppermute | solution.py:113
  77.1 4.4 %collective-permute-start.6 = (bf16[176,256]{1,0:T(8,128)(2,1)S(1)}, bf16[176,256]{1,0:T(8,128)(2,1)S(1)}, u32[]{:S(2)}, u32[]{:S(2)}) collective-permute-start(bf16[176,256]{1,0:T(8,128)(2,1)S(1)} %get-tuple-element.44), channel_id=1, source_target_pairs={{0,128},{128,256},{256,384},{384,0},{1,129},{129,257},{257,385},{3... | collective-permute-start | bytes 270344 | tf_op jit(solution)/shard_map/ppermute | solution.py:113
  81.5 5.3 %collective-permute-start.8 = (bf16[176,256]{1,0:T(8,128)(2,1)S(1)}, bf16[176,256]{1,0:T(8,128)(2,1)S(1)}, u32[]{:S(2)}, u32[]{:S(2)}) collective-permute-start(bf16[176,256]{1,0:T(8,128)(2,1)S(1)} %get-tuple-element.45), channel_id=1, source_target_pairs={{0,384},{128,0},{256,128},{384,256},{1,385},{129,1},{257,129},{385... | collective-permute-start | bytes 270344 | tf_op jit(solution)/shard_map/ppermute | solution.py:113
  86.9 4.0 %collective-permute-done.6 = bf16[176,256]{1,0:T(8,128)(2,1)S(1)} collective-permute-done((bf16[176,256]{1,0:T(8,128)(2,1)S(1)}, bf16[176,256]{1,0:T(8,128)(2,1)S(1)}, u32[]{:S(2)}, u32[]{:S(2)}) %collective-permute-start.6) | collective-permute-done | bytes 90144 | tf_op jit(solution)/shard_map/ppermute | solution.py:113
  90.9 5.2 %collective-permute-done.8 = bf16[176,256]{1,0:T(8,128)(2,1)S(1)} collective-permute-done((bf16[176,256]{1,0:T(8,128)(2,1)S(1)}, bf16[176,256]{1,0:T(8,128)(2,1)S(1)}, u32[]{:S(2)}, u32[]{:S(2)}) %collective-permute-start.8) | collective-permute-done | bytes 90144 | tf_op jit(solution)/shard_map/ppermute | solution.py:113
  96.8 17.8 %all_gather.31.left_ref = bf16[1408,256]{1,0:T(8,128)(2,1)S(1)} all-gather(bf16[176,256]{1,0:T(8,128)(2,1)S(1)} %fusion.3), channel_id=1, replica_groups=mesh['zh'=4,'zl'=4,'y'=4,'x'=4,'c'=2] {'y','c'}, dimensions={0}, use_global_device_ids=true | all-gather | bytes 811008 | tf_op jit(solution)/shard_map/all_gather | solution.py:188
  115.3 1.7 copy-done
  117.0 1.5 shard_map.103
  118.5 5.5 %all-to-all-start = ((bf16[4,256,128]{2,1,0:T(8,128)(2,1)}), bf16[4,256,128]{2,1,0:T(8,128)(2,1)S(1)}, u32[]{:S(2)}, u32[]{:S(2)}) async-start(bf16[4,256,128]{2,1,0:T(8,128)(2,1)} %shard_map.103), calls=%async_computation | async-start | bytes 524288 | tf_op jit(solution)/shard_map/all_to_all | solution.py:131
  124.1 1.2 copy-done.2
  126.3 5.4 %collective-permute-start.9 = (bf16[352,128]{1,0:T(8,128)(2,1)S(1)}, bf16[352,128]{1,0:T(8,128)(2,1)S(1)}, u32[]{:S(2)}, u32[]{:S(2)}) collective-permute-start(bf16[352,128]{1,0:T(8,128)(2,1)S(1)} %get-tuple-element.34), channel_id=1, source_target_pairs={{0,4},{2,6},{4,0},{6,2},{1,5},{3,7},{5,1},{7,3},{8,12},{10,14},{12... | collective-permute-start | bytes 270344 | tf_op jit(solution)/shard_map/ppermute | solution.py:113
  132.4 13.2 %all-gather.1 = bf16[2048,128]{1,0:T(8,128)(2,1)S(1)} all-gather(bf16[256,128]{1,0:T(8,128)(2,1)S(1)} %get-tuple-element.42), channel_id=3, replica_groups=mesh['zh'=4,'zl'=4,'y'=4,'x'=4,'c'=2] {'y','c'}, dimensions={0}, use_global_device_ids=true | all-gather | bytes 589824 | tf_op jit(solution)/shard_map/all_gather | solution.py:209
  145.7 1.2 shard_map.105
  146.8 3.4 %all-to-all-start.1 = ((bf16[4,256,128]{2,1,0:T(8,128)(2,1)}), bf16[4,256,128]{2,1,0:T(8,128)(2,1)S(1)}, u32[]{:S(2)}, u32[]{:S(2)}) async-start(bf16[4,256,128]{2,1,0:T(8,128)(2,1)} %shard_map.105), calls=%async_computation.1 | async-start | bytes 524288 | tf_op jit(solution)/shard_map/all_to_all | solution.py:131
  150.4 3.9 %collective-permute-start.10 = (bf16[352,128]{1,0:T(8,128)(2,1)S(1)}, bf16[352,128]{1,0:T(8,128)(2,1)S(1)}, u32[]{:S(2)}, u32[]{:S(2)}) collective-permute-start(bf16[352,128]{1,0:T(8,128)(2,1)S(1)} %get-tuple-element.36), channel_id=1, source_target_pairs={{0,2},{2,4},{4,6},{6,0},{1,3},{3,5},{5,7},{7,1},{8,10},{10,12},{12... | collective-permute-start | bytes 270344 | tf_op jit(solution)/shard_map/ppermute | solution.py:113
  154.3 3.2 %collective-permute-start.11 = (bf16[352,128]{1,0:T(8,128)(2,1)S(1)}, bf16[352,128]{1,0:T(8,128)(2,1)S(1)}, u32[]{:S(2)}, u32[]{:S(2)}) collective-permute-start(bf16[352,128]{1,0:T(8,128)(2,1)S(1)} %get-tuple-element.38), channel_id=1, source_target_pairs={{0,6},{2,0},{4,2},{6,4},{1,7},{3,1},{5,3},{7,5},{8,14},{10,8},{12,... | collective-permute-start | bytes 270344 | tf_op jit(solution)/shard_map/ppermute | solution.py:113
  157.9 21.3 %all_gather.36.image_ref = bf16[4,256,128]{2,1,0:T(8,128)(2,1)S(1)} all-gather(bf16[1,256,128]{2,1,0:T(8,128)(2,1)S(1)} %fusion.4), channel_id=1, replica_groups=mesh['zh'=4,'zl'=4,'y'=4,'x'=4,'c'=2] {'zh'}, dimensions={0}, use_global_device_ids=true | all-gather | bytes 327680 | tf_op jit(solution)/shard_map/all_gather | solution.py:220
  179.3 1.6 copy-done.4
  180.9 1.4 shard_map.106
  182.3 8.5 %all-to-all-start.2 = ((bf16[4,256,128]{2,1,0:T(8,128)(2,1)}), bf16[4,256,128]{2,1,0:T(8,128)(2,1)S(1)}, u32[]{:S(2)}, u32[]{:S(2)}) async-start(bf16[4,256,128]{2,1,0:T(8,128)(2,1)} %shard_map.106), calls=%async_computation.2 | async-start | bytes 524288 | tf_op jit(solution)/shard_map/all_to_all | solution.py:131
  192.4 4.7 %all-to-all-done.2 = bf16[4,256,128]{2,1,0:T(8,128)(2,1)S(1)} async-done(((bf16[4,256,128]{2,1,0:T(8,128)(2,1)}), bf16[4,256,128]{2,1,0:T(8,128)(2,1)S(1)}, u32[]{:S(2)}, u32[]{:S(2)}) %all-to-all-start.2) | async-done | bytes 262176 | tf_op jit(solution)/shard_map/all_to_all | solution.py:131
  (67 shorter events, 11.3 us)
Async XLA Ops:
  7.2 108.2 %all-gather.6.cloned.1.call-start = ((), (), s32[]{:S(2)}) async-start(), calls=%async_computation.3 | async-start | bytes 2646016 | tf_op jit(solution)/shard_map/all_gather | solution.py:170
  9.0 8.9 %collective-permute-start = (bf16[608,128]{1,0:T(8,128)(2,1)S(1)}, bf16[608,128]{1,0:T(8,128)(2,1)S(1)}, u32[]{:S(2)}, u32[]{:S(2)}) collective-permute-start(bf16[608,128]{1,0:T(8,128)(2,1)S(1)} %pad_maximum_fusion), channel_id=1, source_target_pairs={{0,0},{2,32},{4,64},{6,480},{32,2},{34,34},{36,66},{38,98},{64,132... | collective-permute-start | bytes 466952 | tf_op jit(solution)/shard_map/ppermute | solution.py:127
  14.6 1.8 copy-start.3
  17.9 0.7 copy-start.5
  18.6 160.7 %all-gather.8.cloned.1.call-start = ((), (), s32[]{:S(2)}) async-start(), calls=%async_computation.4 | async-start | bytes 2162688 | tf_op jit(solution)/shard_map/all_gather | solution.py:189
  18.7 38.1 %collective-permute-start.1 = (bf16[4,176,256]{2,1,0:T(8,128)(2,1)S(1)}, bf16[4,176,256]{2,1,0:T(8,128)(2,1)S(1)}, u32[]{:S(2)}, u32[]{:S(2)}) collective-permute-start(bf16[4,176,256]{2,1,0:T(8,128)(2,1)S(1)} %get-tuple-element.26), channel_id=1, source_target_pairs={{0,32},{32,64},{64,96},{96,128},{128,160},{160,192},{192,224},{224... | collective-permute-start | bytes 1081352 | tf_op jit(solution)/shard_map/ppermute | solution.py:109
  28.5 28.4 %collective-permute-start.3 = (bf16[2,176,256]{2,1,0:T(8,128)(2,1)S(1)}, bf16[2,176,256]{2,1,0:T(8,128)(2,1)S(1)}, u32[]{:S(2)}, u32[]{:S(2)}) collective-permute-start(bf16[2,176,256]{2,1,0:T(8,128)(2,1)S(1)} %get-tuple-element.46), channel_id=1, source_target_pairs={{0,64},{32,96},{64,128},{96,160},{128,192},{160,224},{192,256},{22... | collective-permute-start | bytes 540680 | tf_op jit(solution)/shard_map/ppermute | solution.py:109
  30.7 26.1 %collective-permute-start.4 = (bf16[2,176,256]{2,1,0:T(8,128)(2,1)S(1)}, bf16[2,176,256]{2,1,0:T(8,128)(2,1)S(1)}, u32[]{:S(2)}, u32[]{:S(2)}) collective-permute-start(bf16[2,176,256]{2,1,0:T(8,128)(2,1)S(1)} %get-tuple-element.47), channel_id=1, source_target_pairs={{0,448},{32,480},{64,0},{96,32},{128,64},{160,96},{192,128},{224,1... | collective-permute-start | bytes 540680 | tf_op jit(solution)/shard_map/ppermute | solution.py:109
  36.4 59.7 %copy-start.6 = (bf16[256,128]{1,0:T(8,128)(2,1)S(1)}, bf16[256,128]{1,0:T(8,128)(2,1)}, u32[]{:S(2)}) copy-start(bf16[256,128]{1,0:T(8,128)(2,1)} %param.12) | copy-start | bytes 196612
  36.4 20.4 %collective-permute-start.2 = (bf16[4,176,256]{2,1,0:T(8,128)(2,1)S(1)}, bf16[4,176,256]{2,1,0:T(8,128)(2,1)S(1)}, u32[]{:S(2)}, u32[]{:S(2)}) collective-permute-start(bf16[4,176,256]{2,1,0:T(8,128)(2,1)S(1)} %get-tuple-element.28), channel_id=1, source_target_pairs={{0,480},{32,0},{64,32},{96,64},{128,96},{160,128},{192,160},{224,1... | collective-permute-start | bytes 1081352 | tf_op jit(solution)/shard_map/ppermute | solution.py:109
  57.0 12.5 %collective-permute-start.5 = (bf16[176,128]{1,0:T(8,128)(2,1)S(1)}, bf16[176,128]{1,0:T(8,128)(2,1)S(1)}, u32[]{:S(2)}, u32[]{:S(2)}) collective-permute-start(bf16[176,128]{1,0:T(8,128)(2,1)S(1)} %get-tuple-element.48), channel_id=1, source_target_pairs={{0,128},{128,256},{256,384},{384,0},{1,129},{129,257},{257,385},{3... | collective-permute-start | bytes 135176 | tf_op jit(solution)/shard_map/ppermute | solution.py:113
  64.7 12.4 %collective-permute-start.7 = (bf16[176,128]{1,0:T(8,128)(2,1)S(1)}, bf16[176,128]{1,0:T(8,128)(2,1)S(1)}, u32[]{:S(2)}, u32[]{:S(2)}) collective-permute-start(bf16[176,128]{1,0:T(8,128)(2,1)S(1)} %get-tuple-element.49), channel_id=1, source_target_pairs={{0,384},{128,0},{256,128},{384,256},{1,385},{129,1},{257,129},{385... | collective-permute-start | bytes 135176 | tf_op jit(solution)/shard_map/ppermute | solution.py:113
  77.1 13.8 %collective-permute-start.6 = (bf16[176,256]{1,0:T(8,128)(2,1)S(1)}, bf16[176,256]{1,0:T(8,128)(2,1)S(1)}, u32[]{:S(2)}, u32[]{:S(2)}) collective-permute-start(bf16[176,256]{1,0:T(8,128)(2,1)S(1)} %get-tuple-element.44), channel_id=1, source_target_pairs={{0,128},{128,256},{256,384},{384,0},{1,129},{129,257},{257,385},{3... | collective-permute-start | bytes 270344 | tf_op jit(solution)/shard_map/ppermute | solution.py:113
  81.5 14.6 %collective-permute-start.8 = (bf16[176,256]{1,0:T(8,128)(2,1)S(1)}, bf16[176,256]{1,0:T(8,128)(2,1)S(1)}, u32[]{:S(2)}, u32[]{:S(2)}) collective-permute-start(bf16[176,256]{1,0:T(8,128)(2,1)S(1)} %get-tuple-element.45), channel_id=1, source_target_pairs={{0,384},{128,0},{256,128},{384,256},{1,385},{129,1},{257,129},{385... | collective-permute-start | bytes 270344 | tf_op jit(solution)/shard_map/ppermute | solution.py:113
  96.2 27.8 %copy-start.10 = (s32[16]{0:T(128)S(1)}, s32[16]{0:T(128)}, u32[]{:S(2)}) copy-start(s32[16]{0:T(128)} %param.11) | copy-start | bytes 196
  96.2 18.5 %collective-permute-start.12 = (bf16[256,128]{1,0:T(8,128)(2,1)S(1)}, bf16[256,128]{1,0:T(8,128)(2,1)S(1)}, u32[]{:S(2)}, u32[]{:S(2)}) collective-permute-start(bf16[256,128]{1,0:T(8,128)(2,1)S(1)} %copy-done.6), channel_id=1, source_target_pairs={{0,0},{8,128},{16,256},{24,384},{128,8},{136,136},{144,264},{152,3... | collective-permute-start | bytes 196616 | tf_op jit(solution)/shard_map/ppermute | solution.py:118
  114.6 0.6 copy-start.8
  115.3 1.7 copy-start
  117.0 7.0 %copy-start.1 = (bf16[9728,128]{1,0:T(8,128)(2,1)S(1)}, bf16[9728,128]{1,0:T(8,128)(2,1)}, u32[]{:S(2)}) copy-start(bf16[9728,128]{1,0:T(8,128)(2,1)} %all-gather.6.cloned.1.call-done) | copy-start | bytes 7471108
  118.5 13.3 %copy-start.7 = (bf16[256,128]{1,0:T(8,128)(2,1)S(1)}, bf16[256,128]{1,0:T(8,128)(2,1)}, u32[]{:S(2)}) copy-start(bf16[256,128]{1,0:T(8,128)(2,1)} %param.10) | copy-start | bytes 196612
  118.5 13.2 %all-to-all-start = ((bf16[4,256,128]{2,1,0:T(8,128)(2,1)}), bf16[4,256,128]{2,1,0:T(8,128)(2,1)S(1)}, u32[]{:S(2)}, u32[]{:S(2)}) async-start(bf16[4,256,128]{2,1,0:T(8,128)(2,1)} %shard_map.103), calls=%async_computation | async-start | bytes 524288 | tf_op jit(solution)/shard_map/all_to_all | solution.py:131
  124.1 1.2 copy-start.2
  126.3 19.4 %collective-permute-start.9 = (bf16[352,128]{1,0:T(8,128)(2,1)S(1)}, bf16[352,128]{1,0:T(8,128)(2,1)S(1)}, u32[]{:S(2)}, u32[]{:S(2)}) collective-permute-start(bf16[352,128]{1,0:T(8,128)(2,1)S(1)} %get-tuple-element.34), channel_id=1, source_target_pairs={{0,4},{2,6},{4,0},{6,2},{1,5},{3,7},{5,1},{7,3},{8,12},{10,14},{12... | collective-permute-start | bytes 270344 | tf_op jit(solution)/shard_map/ppermute | solution.py:113
  146.8 10.9 %all-to-all-start.1 = ((bf16[4,256,128]{2,1,0:T(8,128)(2,1)}), bf16[4,256,128]{2,1,0:T(8,128)(2,1)S(1)}, u32[]{:S(2)}, u32[]{:S(2)}) async-start(bf16[4,256,128]{2,1,0:T(8,128)(2,1)} %shard_map.105), calls=%async_computation.1 | async-start | bytes 524288 | tf_op jit(solution)/shard_map/all_to_all | solution.py:131
  150.4 28.9 %collective-permute-start.10 = (bf16[352,128]{1,0:T(8,128)(2,1)S(1)}, bf16[352,128]{1,0:T(8,128)(2,1)S(1)}, u32[]{:S(2)}, u32[]{:S(2)}) collective-permute-start(bf16[352,128]{1,0:T(8,128)(2,1)S(1)} %get-tuple-element.36), channel_id=1, source_target_pairs={{0,2},{2,4},{4,6},{6,0},{1,3},{3,5},{5,7},{7,1},{8,10},{10,12},{12... | collective-permute-start | bytes 270344 | tf_op jit(solution)/shard_map/ppermute | solution.py:113
  154.3 25.0 %collective-permute-start.11 = (bf16[352,128]{1,0:T(8,128)(2,1)S(1)}, bf16[352,128]{1,0:T(8,128)(2,1)S(1)}, u32[]{:S(2)}, u32[]{:S(2)}) collective-permute-start(bf16[352,128]{1,0:T(8,128)(2,1)S(1)} %get-tuple-element.38), channel_id=1, source_target_pairs={{0,6},{2,0},{4,2},{6,4},{1,7},{3,1},{5,3},{7,5},{8,14},{10,8},{12,... | collective-permute-start | bytes 270344 | tf_op jit(solution)/shard_map/ppermute | solution.py:113
  157.8 39.3 %copy-start.9 = (bf16[256,128]{1,0:T(8,128)(2,1)S(1)}, bf16[256,128]{1,0:T(8,128)(2,1)}, u32[]{:S(2)}) copy-start(bf16[256,128]{1,0:T(8,128)(2,1)} %param.13) | copy-start | bytes 196612
  179.3 1.6 copy-start.4
  182.3 14.8 %all-to-all-start.2 = ((bf16[4,256,128]{2,1,0:T(8,128)(2,1)}), bf16[4,256,128]{2,1,0:T(8,128)(2,1)S(1)}, u32[]{:S(2)}, u32[]{:S(2)}) async-start(bf16[4,256,128]{2,1,0:T(8,128)(2,1)} %shard_map.106), calls=%async_computation.2 | async-start | bytes 524288 | tf_op jit(solution)/shard_map/all_to_all | solution.py:131
Sparse Core Ops, SparseCore 0:
  18.7 91.3 all-gather.5
  115.4 61.7 all-gather.7

commit v11 on v7

--- a/solution.py
+++ b/solution.py
@@ -93,16 +93,31 @@
 
 
 def last_kernel(factor_ref, image_ref, out_ref):
-    for x in range(4):
-        total = None
-        for y in range(4):
-            n = (y * 4 + x) * 2
-            left = jnp.concatenate([factor_ref[n], factor_ref[n + 1]], axis=1)
-            part = lax.dot_general(
-                left, image_ref[y], (((0,), (0,)), ((), ())), preferred_element_type=F32
-            )
-            total = part if total is None else total + part
-        out_ref[x] = total.astype(out_ref.dtype)
+    total = None
+    for y in range(4):
+        left = jnp.concatenate([factor_ref[y, 0], factor_ref[y, 1]], axis=1)
+        part = lax.dot_general(
+            left, image_ref[y], (((0,), (0,)), ((), ())), preferred_element_type=F32
+        )
+        total = part if total is None else total + part
+    out_ref[0] = total.astype(out_ref.dtype)
+
+
+def last_product(factor, image):
+    return pl.pallas_call(
+        last_kernel,
+        grid=(4,),
+        out_shape=jax.ShapeDtypeStruct((4, 256, 128), BF),
+        in_specs=[
+            pl.BlockSpec((4, 2, 256, 128), lambda x: (0, x, 0, 0)),
+            pl.BlockSpec((4, 256, 128), lambda x: (0, 0, 0)),
+        ],
+        out_specs=pl.BlockSpec((1, 256, 128), lambda x: (x, 0, 0)),
+        compiler_params=pltpu.CompilerParams(vmem_limit_bytes=60 * 1024 * 1024),
+        cost_estimate=pl.CostEstimate(
+            flops=2 * 1024 * 1024 * 128, bytes_accessed=2621440, transcendentals=0
+        ),
+    )(factor.reshape(4, 8, 256, 128), image)
 
 
 def shift(value, by):
@@ -210,12 +225,7 @@
     parent_child = (-product * child_keep[:, None].astype(F32)).astype(BF)
 
     child_wide = lax.all_gather(parent_child, "zh", axis=0)
-    (inner,) = call(
-        last_kernel,
-        [jax.ShapeDtypeStruct((4, 256, 128), BF)],
-        [factor, after(child_wide, *moved)],
-        2 * 1024 * 1024 * 128,
-    )
+    inner = last_product(factor, after(child_wide, *moved))
     inner = jnp.sum(exchange(inner, "zl").astype(F32), axis=0)
     product = besides[0] + sum(block.astype(F32) for block in moved)
     ancestor_block = (-product * ancestor_keep[:, None].astype(F32)).astype(BF)

time: 204 us -> 205 us (level)
  Pallas kernels: 6.46 us -> 9.15 us
    pallas_call x0 -> x1, Pallas kernels: none -> 4.14 us  [last_product(): pl.pallas_call(last_kernel, grid=(4,), out_shape=jax.ShapeDtypeStruct((4,...]
    unnamed x22 -> x20, local copies, waits for them, and re-layouts: 7.65 us -> 6.07 us
    pallas_call x5 -> x4, Pallas kernels: 6.46 us -> 5.02 us  [call(): pl.pallas_call(kernel, out_shape=outs, in_specs=specs, out_specs=[VMEM] *...]
  transfers between devices with their start and end apart: 15 -> 15, of which waited for: 5 -> 6; matrix products, arithmetic and copies ran while one was open for 3% -> 3% of each run, Pallas kernels for 2% -> 2%
where the time goes in v11:
time: 205 us; the launch traced here: 204 us
  blocking collectives  67.7 us (33%)
  starting transfers between devices  57.9 us (28%)
  waiting for transfers between devices  40.3 us (20%)
  between operations  14.4 us (7%)
  Pallas kernels  9.15 us (4%)
  other arithmetic  7.67 us (4%)
  local copies, waits for them, and re-layouts  7 us (3%)
    ppermute x4, starting transfers between devices, shift(): return lax.ppermute(value, Z, [(i, (i + by) % 16) for i in range(16)])  22.5 us
    all_to_all x4, starting transfers between devices, exchange(): return lax.all_to_all(value, axis, split_axis=0, concat_axis=0, tiled=True)  21.1 us
    all_gather x1, blocking collectives, per_device(): child_wide = lax.all_gather(parent_child, 'zh', axis=0)  18.7 us
    all_gather x1, blocking collectives, per_device(): diag_wide = lax.all_gather(diag_wide, ('y', 'c'), axis=0)  17.6 us
    all_to_all x4, waiting for transfers between devices, exchange(): return lax.all_to_all(value, axis, split_axis=0, concat_axis=0, tiled=True)  16.9 us
    all_gather x1, blocking collectives, per_device(): cov_wide = lax.all_gather(after(cov, image), ('y', 'c'), axis=0, tiled=True)  15.7 us
    all_gather x1, blocking collectives, per_device(): image_wide = lax.all_gather(image, ('y', 'c'), axis=0, tiled=True)  15.7 us
    all_gather x1, waiting for transfers between devices, per_device(): blocks = lax.all_gather(after(swapped, own), Z, axis=0)  15 us
  transfers between devices with their start and end apart: 15, of which 6 were waited for; matrix products, arithmetic and copies ran while one was open for 3% of the time, Pallas kernels for 2%

profile of v11, /device:TPU:2, one launch (start us, length us, event | category | flops | bytes accessed | tf_op | source)
XLA Modules:
  0.0 204.0 jit_solution(8386987255754391763)
XLA Ops:
  7.2 0.9 constant_dynamic-slice_fusion
  9.0 3.8 %collective-permute-start.4 = (bf16[608,128]{1,0:T(8,128)(2,1)S(1)}, bf16[608,128]{1,0:T(8,128)(2,1)S(1)}, u32[]{:S(2)}, u32[]{:S(2)}) collective-permute-start(bf16[608,128]{1,0:T(8,128)(2,1)S(1)} %pad_maximum_fusion), channel_id=1, source_target_pairs={{0,0},{2,32},{4,64},{6,480},{32,2},{34,34},{36,66},{38,98},{64,132... | collective-permute-start | bytes 466952 | tf_op jit(solution)/shard_map/ppermute | solution.py:142
  14.4 1.0 multiply_bitcast_fusion.at_ref
  15.5 1.8 copy-done.3
  17.3 1.5 shard_map.102
  19.5 1.9 collective-permute-start
  21.4 12.7 %collective-permute-start.1 = (bf16[4,176,256]{2,1,0:T(8,128)(2,1)S(1)}, bf16[4,176,256]{2,1,0:T(8,128)(2,1)S(1)}, u32[]{:S(2)}, u32[]{:S(2)}) collective-permute-start(bf16[4,176,256]{2,1,0:T(8,128)(2,1)S(1)} %get-tuple-element.25), channel_id=1, source_target_pairs={{0,480},{32,0},{64,32},{96,64},{128,96},{160,128},{192,160},{224,1... | collective-permute-start | bytes 1081352 | tf_op jit(solution)/shard_map/ppermute | solution.py:124
  34.1 1.9 collective-permute-start.2
  36.0 6.0 %collective-permute-start.3 = (bf16[2,176,256]{2,1,0:T(8,128)(2,1)S(1)}, bf16[2,176,256]{2,1,0:T(8,128)(2,1)S(1)}, u32[]{:S(2)}, u32[]{:S(2)}) collective-permute-start(bf16[2,176,256]{2,1,0:T(8,128)(2,1)S(1)} %get-tuple-element.45), channel_id=1, source_target_pairs={{0,448},{32,480},{64,0},{96,32},{128,64},{160,96},{192,128},{224,1... | collective-permute-start | bytes 540680 | tf_op jit(solution)/shard_map/ppermute | solution.py:124
  42.1 4.1 %collective-permute-done.2 = bf16[2,176,256]{2,1,0:T(8,128)(2,1)S(1)} collective-permute-done((bf16[2,176,256]{2,1,0:T(8,128)(2,1)S(1)}, bf16[2,176,256]{2,1,0:T(8,128)(2,1)S(1)}, u32[]{:S(2)}, u32[]{:S(2)}) %collective-permute-start.2) | collective-permute-done | bytes 180256 | tf_op jit(solution)/shard_map/ppermute | solution.py:124
  46.2 4.3 %collective-permute-done.3 = bf16[2,176,256]{2,1,0:T(8,128)(2,1)S(1)} collective-permute-done((bf16[2,176,256]{2,1,0:T(8,128)(2,1)S(1)}, bf16[2,176,256]{2,1,0:T(8,128)(2,1)S(1)}, u32[]{:S(2)}, u32[]{:S(2)}) %collective-permute-start.3) | collective-permute-done | bytes 180256 | tf_op jit(solution)/shard_map/ppermute | solution.py:124
  50.4 0.9 add_convert_fusion
  51.4 7.7 %all-to-all-start = ((bf16[4,176,256]{2,1,0:T(8,128)(2,1)}), bf16[4,176,256]{2,1,0:T(8,128)(2,1)S(1)}, u32[]{:S(2)}, u32[]{:S(2)}) async-start(bf16[4,176,256]{2,1,0:T(8,128)(2,1)} %add_convert_fusion), calls=%async_computation | async-start | bytes 720896 | tf_op jit(solution)/shard_map/all_to_all | solution.py:146
  59.1 15.7 %all_gather.28.left_ref = bf16[1408,352]{1,0:T(8,128)(2,1)} all-gather(bf16[176,352]{1,0:T(8,128)(2,1)S(1)} %multiply_bitcast_fusion.at_ref), channel_id=1, replica_groups=mesh['zh'=4,'zl'=4,'y'=4,'x'=4,'c'=2] {'y','c'}, dimensions={0}, use_global_device_ids=true | all-gather | bytes 1115136 | tf_op jit(solution)/shard_map/all_gather | solution.py:191
  74.8 10.4 %all-to-all-done = bf16[4,176,256]{2,1,0:T(8,128)(2,1)S(1)} async-done(((bf16[4,176,256]{2,1,0:T(8,128)(2,1)}), bf16[4,176,256]{2,1,0:T(8,128)(2,1)S(1)}, u32[]{:S(2)}, u32[]{:S(2)}) %all-to-all-start) | async-done | bytes 360480 | tf_op jit(solution)/shard_map/all_to_all | solution.py:146
  85.9 15.7 %all_gather.31.left_ref = bf16[1408,256]{1,0:T(8,128)(2,1)S(1)} all-gather(bf16[176,256]{1,0:T(8,128)(2,1)S(1)} %reduce_sum.77), channel_id=1, replica_groups=mesh['zh'=4,'zl'=4,'y'=4,'x'=4,'c'=2] {'y','c'}, dimensions={0}, use_global_device_ids=true | all-gather | bytes 811008 | tf_op jit(solution)/shard_map/all_gather | solution.py:195
  102.2 15.0 %all-gather.6.cloned.1.call-done = bf16[9728,128]{1,0:T(8,128)(2,1)} async-done(((bf16[608,128]{1,0:T(8,128)(2,1)}), bf16[9728,128]{1,0:T(8,128)(2,1)}) %all-gather.6.cloned.1.call-update) | async-done | bytes 2490384 | tf_op jit(solution)/shard_map/all_gather | solution.py:185
  117.2 1.7 copy-done
  118.9 1.4 shard_map.103
  120.3 3.5 %all-to-all-start.1 = ((bf16[4,256,128]{2,1,0:T(8,128)(2,1)}), bf16[4,256,128]{2,1,0:T(8,128)(2,1)S(1)}, u32[]{:S(2)}, u32[]{:S(2)}) async-start(bf16[4,256,128]{2,1,0:T(8,128)(2,1)} %shard_map.103), calls=%async_computation.1 | async-start | bytes 524288 | tf_op jit(solution)/shard_map/all_to_all | solution.py:146
  124.0 1.2 copy-done.2
  125.2 1.0 shard_map.104
  126.2 3.9 %collective-permute-start.5 = (bf16[352,128]{1,0:T(8,128)(2,1)S(1)}, bf16[352,128]{1,0:T(8,128)(2,1)S(1)}, u32[]{:S(2)}, u32[]{:S(2)}) collective-permute-start(bf16[352,128]{1,0:T(8,128)(2,1)S(1)} %get-tuple-element.34), channel_id=1, source_target_pairs={{0,4},{2,6},{4,0},{6,2},{1,5},{3,7},{5,1},{7,3},{8,12},{10,14},{12... | collective-permute-start | bytes 270344 | tf_op jit(solution)/shard_map/ppermute | solution.py:128
  130.8 17.6 %all-gather.1 = bf16[2048,128]{1,0:T(8,128)(2,1)S(1)} all-gather(bf16[256,128]{1,0:T(8,128)(2,1)S(1)} %get-tuple-element.42), channel_id=3, replica_groups=mesh['zh'=4,'zl'=4,'y'=4,'x'=4,'c'=2] {'y','c'}, dimensions={0}, use_global_device_ids=true | all-gather | bytes 589824 | tf_op jit(solution)/shard_map/all_gather | solution.py:216
  148.4 1.2 shard_map.105
  149.6 4.9 %all-to-all-start.2 = ((bf16[4,256,128]{2,1,0:T(8,128)(2,1)}), bf16[4,256,128]{2,1,0:T(8,128)(2,1)S(1)}, u32[]{:S(2)}, u32[]{:S(2)}) async-start(bf16[4,256,128]{2,1,0:T(8,128)(2,1)} %shard_map.105), calls=%async_computation.2 | async-start | bytes 524288 | tf_op jit(solution)/shard_map/all_to_all | solution.py:146
  154.6 3.4 %collective-permute-start.6 = (bf16[352,128]{1,0:T(8,128)(2,1)S(1)}, bf16[352,128]{1,0:T(8,128)(2,1)S(1)}, u32[]{:S(2)}, u32[]{:S(2)}) collective-permute-start(bf16[352,128]{1,0:T(8,128)(2,1)S(1)} %get-tuple-element.36), channel_id=1, source_target_pairs={{0,2},{2,4},{4,6},{6,0},{1,3},{3,5},{5,7},{7,1},{8,10},{10,12},{12... | collective-permute-start | bytes 270344 | tf_op jit(solution)/shard_map/ppermute | solution.py:128
  157.9 2.5 %collective-permute-start.7 = (bf16[352,128]{1,0:T(8,128)(2,1)S(1)}, bf16[352,128]{1,0:T(8,128)(2,1)S(1)}, u32[]{:S(2)}, u32[]{:S(2)}) collective-permute-start(bf16[352,128]{1,0:T(8,128)(2,1)S(1)} %get-tuple-element.38), channel_id=1, source_target_pairs={{0,6},{2,0},{4,2},{6,4},{1,7},{3,1},{5,3},{7,5},{8,14},{10,8},{12,... | collective-permute-start | bytes 270344 | tf_op jit(solution)/shard_map/ppermute | solution.py:128
  160.6 18.7 %all_gather.36.image_ref = bf16[4,256,128]{2,1,0:T(8,128)(2,1)} all-gather(bf16[1,256,128]{2,1,0:T(8,128)(2,1)S(1)} %fusion), channel_id=1, replica_groups=mesh['zh'=4,'zl'=4,'y'=4,'x'=4,'c'=2] {'zh'}, dimensions={0}, use_global_device_ids=true | all-gather | bytes 327680 | tf_op jit(solution)/shard_map/all_gather | solution.py:227
  179.3 4.1 %shard_map.106 = bf16[4,256,128]{2,1,0:T(8,128)(2,1)} custom-call(bf16[4,8,256,128]{3,2,1,0:T(8,128)(2,1)} %bitcast.18, bf16[4,256,128]{2,1,0:T(8,128)(2,1)} %all_gather.36.image_ref), custom_call_target="tpu_custom_call" | custom-call | flops 268435456 | bytes 2621440 | tf_op jit(solution)/shard_map/pallas_call | solution.py:107
  183.5 5.0 %all-to-all-start.3 = ((bf16[4,256,128]{2,1,0:T(8,128)(2,1)}), bf16[4,256,128]{2,1,0:T(8,128)(2,1)S(1)}, u32[]{:S(2)}, u32[]{:S(2)}) async-start(bf16[4,256,128]{2,1,0:T(8,128)(2,1)} %shard_map.106), calls=%async_computation.3 | async-start | bytes 524288 | tf_op jit(solution)/shard_map/all_to_all | solution.py:146
  190.0 6.5 %all-to-all-done.3 = bf16[4,256,128]{2,1,0:T(8,128)(2,1)S(1)} async-done(((bf16[4,256,128]{2,1,0:T(8,128)(2,1)}), bf16[4,256,128]{2,1,0:T(8,128)(2,1)S(1)}, u32[]{:S(2)}, u32[]{:S(2)}) %all-to-all-start.3) | async-done | bytes 262176 | tf_op jit(solution)/shard_map/all_to_all | solution.py:146
  (56 shorter events, 7.9 us)
Async XLA Ops:
  7.2 110.0 %all-gather.6.cloned.1.call-start = ((), (), s32[]{:S(2)}) async-start(), calls=%async_computation.4 | async-start | bytes 2646016 | tf_op jit(solution)/shard_map/all_gather | solution.py:185
  9.0 9.8 %collective-permute-start.4 = (bf16[608,128]{1,0:T(8,128)(2,1)S(1)}, bf16[608,128]{1,0:T(8,128)(2,1)S(1)}, u32[]{:S(2)}, u32[]{:S(2)}) collective-permute-start(bf16[608,128]{1,0:T(8,128)(2,1)S(1)} %pad_maximum_fusion), channel_id=1, source_target_pairs={{0,0},{2,32},{4,64},{6,480},{32,2},{34,34},{36,66},{38,98},{64,132... | collective-permute-start | bytes 466952 | tf_op jit(solution)/shard_map/ppermute | solution.py:142
  15.5 1.8 copy-start.3
  18.8 0.7 copy-start.4
  19.5 31.0 %collective-permute-start = (bf16[4,176,256]{2,1,0:T(8,128)(2,1)S(1)}, bf16[4,176,256]{2,1,0:T(8,128)(2,1)S(1)}, u32[]{:S(2)}, u32[]{:S(2)}) collective-permute-start(bf16[4,176,256]{2,1,0:T(8,128)(2,1)S(1)} %get-tuple-element.24), channel_id=1, source_target_pairs={{0,32},{32,64},{64,96},{96,128},{128,160},{160,192},{192,224},{224... | collective-permute-start | bytes 1081352 | tf_op jit(solution)/shard_map/ppermute | solution.py:124
  21.4 29.1 %collective-permute-start.1 = (bf16[4,176,256]{2,1,0:T(8,128)(2,1)S(1)}, bf16[4,176,256]{2,1,0:T(8,128)(2,1)S(1)}, u32[]{:S(2)}, u32[]{:S(2)}) collective-permute-start(bf16[4,176,256]{2,1,0:T(8,128)(2,1)S(1)} %get-tuple-element.25), channel_id=1, source_target_pairs={{0,480},{32,0},{64,32},{96,64},{128,96},{160,128},{192,160},{224,1... | collective-permute-start | bytes 1081352 | tf_op jit(solution)/shard_map/ppermute | solution.py:124
  34.1 51.2 %copy-start.5 = (bf16[256,128]{1,0:T(8,128)(2,1)S(1)}, bf16[256,128]{1,0:T(8,128)(2,1)}, u32[]{:S(2)}) copy-start(bf16[256,128]{1,0:T(8,128)(2,1)} %param.12) | copy-start | bytes 196612
  34.1 12.1 %collective-permute-start.2 = (bf16[2,176,256]{2,1,0:T(8,128)(2,1)S(1)}, bf16[2,176,256]{2,1,0:T(8,128)(2,1)S(1)}, u32[]{:S(2)}, u32[]{:S(2)}) collective-permute-start(bf16[2,176,256]{2,1,0:T(8,128)(2,1)S(1)} %get-tuple-element.44), channel_id=1, source_target_pairs={{0,64},{32,96},{64,128},{96,160},{128,192},{160,224},{192,256},{22... | collective-permute-start | bytes 540680 | tf_op jit(solution)/shard_map/ppermute | solution.py:124
  36.0 14.4 %collective-permute-start.3 = (bf16[2,176,256]{2,1,0:T(8,128)(2,1)S(1)}, bf16[2,176,256]{2,1,0:T(8,128)(2,1)S(1)}, u32[]{:S(2)}, u32[]{:S(2)}) collective-permute-start(bf16[2,176,256]{2,1,0:T(8,128)(2,1)S(1)} %get-tuple-element.45), channel_id=1, source_target_pairs={{0,448},{32,480},{64,0},{96,32},{128,64},{160,96},{192,128},{224,1... | collective-permute-start | bytes 540680 | tf_op jit(solution)/shard_map/ppermute | solution.py:124
  51.4 33.8 %all-to-all-start = ((bf16[4,176,256]{2,1,0:T(8,128)(2,1)}), bf16[4,176,256]{2,1,0:T(8,128)(2,1)S(1)}, u32[]{:S(2)}, u32[]{:S(2)}) async-start(bf16[4,176,256]{2,1,0:T(8,128)(2,1)} %add_convert_fusion), calls=%async_computation | async-start | bytes 720896 | tf_op jit(solution)/shard_map/all_to_all | solution.py:146
  59.1 120.2 %all-gather.8.cloned.1.call-start = ((), (), s32[]{:S(2)}) async-start(), calls=%async_computation.5 | async-start | bytes 2162688 | tf_op jit(solution)/shard_map/all_gather | solution.py:196
  85.3 38.6 %copy-start.9 = (s32[16]{0:T(128)S(1)}, s32[16]{0:T(128)}, u32[]{:S(2)}) copy-start(s32[16]{0:T(128)} %param.11) | copy-start | bytes 196
  85.3 16.3 %collective-permute-start.8 = (bf16[256,128]{1,0:T(8,128)(2,1)S(1)}, bf16[256,128]{1,0:T(8,128)(2,1)S(1)}, u32[]{:S(2)}, u32[]{:S(2)}) collective-permute-start(bf16[256,128]{1,0:T(8,128)(2,1)S(1)} %copy-done.5), channel_id=1, source_target_pairs={{0,0},{8,128},{16,256},{24,384},{128,8},{136,136},{144,264},{152,3... | collective-permute-start | bytes 196616 | tf_op jit(solution)/shard_map/ppermute | solution.py:133
  101.6 0.6 copy-start.7
  117.2 1.7 copy-start
  118.9 5.1 %copy-start.1 = (bf16[9728,128]{1,0:T(8,128)(2,1)S(1)}, bf16[9728,128]{1,0:T(8,128)(2,1)}, u32[]{:S(2)}) copy-start(bf16[9728,128]{1,0:T(8,128)(2,1)} %all-gather.6.cloned.1.call-done) | copy-start | bytes 7471108
  120.3 9.8 %copy-start.6 = (bf16[256,128]{1,0:T(8,128)(2,1)S(1)}, bf16[256,128]{1,0:T(8,128)(2,1)}, u32[]{:S(2)}) copy-start(bf16[256,128]{1,0:T(8,128)(2,1)} %param.10) | copy-start | bytes 196612
  120.3 9.7 %all-to-all-start.1 = ((bf16[4,256,128]{2,1,0:T(8,128)(2,1)}), bf16[4,256,128]{2,1,0:T(8,128)(2,1)S(1)}, u32[]{:S(2)}, u32[]{:S(2)}) async-start(bf16[4,256,128]{2,1,0:T(8,128)(2,1)} %shard_map.103), calls=%async_computation.1 | async-start | bytes 524288 | tf_op jit(solution)/shard_map/all_to_all | solution.py:146
  124.0 1.2 copy-start.2
  126.2 22.2 %collective-permute-start.5 = (bf16[352,128]{1,0:T(8,128)(2,1)S(1)}, bf16[352,128]{1,0:T(8,128)(2,1)S(1)}, u32[]{:S(2)}, u32[]{:S(2)}) collective-permute-start(bf16[352,128]{1,0:T(8,128)(2,1)S(1)} %get-tuple-element.34), channel_id=1, source_target_pairs={{0,4},{2,6},{4,0},{6,2},{1,5},{3,7},{5,1},{7,3},{8,12},{10,14},{12... | collective-permute-start | bytes 270344 | tf_op jit(solution)/shard_map/ppermute | solution.py:128
  149.6 10.9 %all-to-all-start.2 = ((bf16[4,256,128]{2,1,0:T(8,128)(2,1)}), bf16[4,256,128]{2,1,0:T(8,128)(2,1)S(1)}, u32[]{:S(2)}, u32[]{:S(2)}) async-start(bf16[4,256,128]{2,1,0:T(8,128)(2,1)} %shard_map.105), calls=%async_computation.2 | async-start | bytes 524288 | tf_op jit(solution)/shard_map/all_to_all | solution.py:146
  154.6 24.7 %collective-permute-start.6 = (bf16[352,128]{1,0:T(8,128)(2,1)S(1)}, bf16[352,128]{1,0:T(8,128)(2,1)S(1)}, u32[]{:S(2)}, u32[]{:S(2)}) collective-permute-start(bf16[352,128]{1,0:T(8,128)(2,1)S(1)} %get-tuple-element.36), channel_id=1, source_target_pairs={{0,2},{2,4},{4,6},{6,0},{1,3},{3,5},{5,7},{7,1},{8,10},{10,12},{12... | collective-permute-start | bytes 270344 | tf_op jit(solution)/shard_map/ppermute | solution.py:128
  157.9 21.4 %collective-permute-start.7 = (bf16[352,128]{1,0:T(8,128)(2,1)S(1)}, bf16[352,128]{1,0:T(8,128)(2,1)S(1)}, u32[]{:S(2)}, u32[]{:S(2)}) collective-permute-start(bf16[352,128]{1,0:T(8,128)(2,1)S(1)} %get-tuple-element.38), channel_id=1, source_target_pairs={{0,6},{2,0},{4,2},{6,4},{1,7},{3,1},{5,3},{7,5},{8,14},{10,8},{12,... | collective-permute-start | bytes 270344 | tf_op jit(solution)/shard_map/ppermute | solution.py:128
  160.5 36.0 %copy-start.8 = (bf16[256,128]{1,0:T(8,128)(2,1)S(1)}, bf16[256,128]{1,0:T(8,128)(2,1)}, u32[]{:S(2)}) copy-start(bf16[256,128]{1,0:T(8,128)(2,1)} %param.13) | copy-start | bytes 196612
  183.5 13.0 %all-to-all-start.3 = ((bf16[4,256,128]{2,1,0:T(8,128)(2,1)}), bf16[4,256,128]{2,1,0:T(8,128)(2,1)S(1)}, u32[]{:S(2)}, u32[]{:S(2)}) async-start(bf16[4,256,128]{2,1,0:T(8,128)(2,1)} %shard_map.106), calls=%async_computation.3 | async-start | bytes 524288 | tf_op jit(solution)/shard_map/all_to_all | solution.py:146
Sparse Core Ops, SparseCore 0:
  19.6 97.5 all-gather.5
  120.9 57.0 all-gather.7
